TPU v7x, 32 devices: a whole 2x2x4 slice. The times are simulated.
32 devices in a mesh: ens: 2 (over y), lat: 16 (over z, x, core).
Axes of the slice: x: 2, y: 2, z: 4, core: 2. Of those that a mesh axis runs over, the one named last changes fastest.
Arguments:
- field: bfloat16 [128, 1440, 384], P(('ens', 'lat')), parts along dimension 0, may hold values from -6 to 6
- norm_gain: float32 [384], replicated, may hold values from 0.1 to 1.9
- legendre_fwd: bfloat16 [256, 256, 64], P('lat'), as said below
- legendre_inv: bfloat16 [256, 256, 64], P('lat')
- degree_gain: float32 [256, 384], replicated, may hold values from 0.5 to 2
- mix_weight: bfloat16 [2, 384, 384], replicated, may hold values from -0.21875 to 0.21875
- mlp_gain: float32 [384], replicated, may hold values from 0.1 to 1.9
- up_weight: bfloat16 [384, 768], replicated, may hold values from -0.3125 to 0.3125
- up_bias: float32 [768], replicated, may hold values from -4 to 4
- down_weight: bfloat16 [768, 384], replicated, may hold values from -0.21875 to 0.21875
Outputs:
- result: bfloat16 [128, 1440, 384], P(('ens', 'lat')), parts along dimension 0
There are 2 independent parts, one for each index of `ens`. A program takes and returns all parts, laid end to end along the dimension named above; an argument that names none is the same for every part. Nothing has to cross between parts.
Inputs may be any that keep to these rules, and one draw needn't show every extreme that they name: legendre_inv holds orthonormal associated Legendre functions of degree l and order m (zero where l < m) at the grid's colatitudes, legendre_fwd the same times each row's quadrature weight.
All inputs are finite; a program needn't handle non-finite values.
Results may differ from a plain program's by a relative error of at most 0.009.
Values may be sent and summed in bfloat16 or wider, within the bound.
No kernel may reach another device: no remote copies, remote signals or barrier semaphores. Data moves between devices by JAX's collectives and lax.ppermute only.
A program may use at most 64 MiB of HBM per device.

v0:
```python
import functools
import math

import jax
import jax.numpy as jnp
import ml_dtypes
import numpy as np
from jax import lax
from jax.experimental import pallas as pl
from jax.experimental.pallas import tpu as pltpu
from jax.sharding import PartitionSpec as P

BF = jnp.bfloat16
F32 = jnp.float32
EPS = 1e-05
VMEM_LIMIT = 48 * 1024 * 1024


def tables(nlon, modes):
    lon = np.arange(nlon)
    wave = np.arange(modes)
    phase = (wave[:, None] * lon[None, :] % nlon) * (2.0 * math.pi / nlon)
    scale = 2.0 * math.pi / nlon
    weight = np.where(wave == 0, 1.0, 2.0)[:, None]
    forward = np.concatenate([scale * np.cos(phase), -scale * np.sin(phase)], 0)
    inverse = np.concatenate([weight * np.cos(phase), -weight * np.sin(phase)], 0).T
    as_bf = lambda a: a.astype(np.float32).astype(ml_dtypes.bfloat16)
    return as_bf(forward), as_bf(inverse)


def dot(a, b):
    return jnp.dot(a, b, preferred_element_type=F32)


def norm(values, gain):
    center = values - jnp.mean(values, axis=-1, keepdims=True)
    spread = jnp.mean(center * center, axis=-1, keepdims=True)
    return center * lax.rsqrt(spread + EPS) * gain


def analyse_kernel(field_ref, gain_ref, table_ref, spec_ref, normed_ref):
    modes = table_ref.shape[0] // 2
    chan = field_ref.shape[-1]
    normed = norm(field_ref[0].astype(F32), gain_ref[...]).astype(BF)
    normed_ref[0] = normed
    spec = dot(table_ref[...], normed).astype(BF)
    shape = spec_ref.shape[:1] + spec_ref.shape[2:3] + (chan,)
    spec_ref[:, 0, :, :chan] = spec[:modes].reshape(shape)
    spec_ref[:, 0, :, chan:] = spec[modes:].reshape(shape)


def analyse(field, gain, table, devices, modes_here):
    rows, nlon, chan = field.shape
    modes2 = table.shape[0]
    return pl.pallas_call(
        analyse_kernel,
        grid=(rows,),
        in_specs=[
            pl.BlockSpec((1, nlon, chan), lambda j: (j, 0, 0)),
            pl.BlockSpec((1, chan), lambda j: (0, 0)),
            pl.BlockSpec((modes2, nlon), lambda j: (0, 0)),
        ],
        out_specs=[
            pl.BlockSpec((devices, 1, modes_here, 2 * chan), lambda j: (0, j, 0, 0)),
            pl.BlockSpec((1, nlon, chan), lambda j: (j, 0, 0)),
        ],
        out_shape=[
            jax.ShapeDtypeStruct((devices, rows, modes_here, 2 * chan), BF),
            jax.ShapeDtypeStruct(field.shape, BF),
        ],
        compiler_params=pltpu.CompilerParams(vmem_limit_bytes=VMEM_LIMIT),
    )(field, gain.reshape(1, chan), table)


def middle_kernel(
    arrived_ref, fwd_ref, inv_ref, gain_ref, weight_ref, to_modes_ref, to_rows_ref, out_ref, by_mode, back
):
    devices, rows, modes_here, width = arrived_ref.shape
    flat = devices * modes_here
    for row in range(rows):
        block = arrived_ref[:, row].reshape(flat, width)
        by_mode[row] = dot(to_modes_ref[...], block).astype(BF)
    gain = jnp.concatenate([gain_ref[...], gain_ref[...]], axis=1)
    for mode in range(modes_here):
        here = slice(mode * devices, (mode + 1) * devices)
        spectrum = jnp.concatenate([by_mode[row, here] for row in range(rows)], axis=0)
        scaled = (dot(fwd_ref[mode], spectrum) * gain).astype(BF)
        synth = dot(inv_ref[mode], scaled).astype(BF)
        for row in range(rows):
            back[row, here] = synth[row * devices : (row + 1) * devices]
    for row in range(rows):
        block = dot(to_rows_ref[...], back[row]).astype(BF)
        mixed = dot(block, weight_ref[...]).astype(BF)
        out_ref[:, row] = mixed.reshape(devices, modes_here, width)


def middle(arrived, fwd, inv, gain, weight):
    devices, rows, modes_here, width = arrived.shape
    flat = devices * modes_here
    source = np.arange(flat).reshape(devices, modes_here).T.reshape(-1)
    to_modes = np.eye(flat, dtype=np.float32)[source].astype(ml_dtypes.bfloat16)
    return pl.pallas_call(
        middle_kernel,
        out_shape=jax.ShapeDtypeStruct(arrived.shape, BF),
        scratch_shapes=[
            pltpu.VMEM((rows, flat, width), BF),
            pltpu.VMEM((rows, flat, width), BF),
        ],
        compiler_params=pltpu.CompilerParams(vmem_limit_bytes=VMEM_LIMIT),
    )(arrived, fwd, inv, gain, weight, jnp.asarray(to_modes), jnp.asarray(np.ascontiguousarray(to_modes.T)))


def finish_kernel(
    synth_ref, normed_ref, field_ref, table_ref, gain_ref, up_ref, bias_ref, down_ref, out_ref, *, parts
):
    devices, unused, modes_here, width = synth_ref.shape
    chan = width // 2
    flat = synth_ref[:, 0].reshape(devices * modes_here, width)
    stacked = jnp.concatenate([flat[:, :chan], flat[:, chan:]], axis=0)
    size = field_ref.shape[1] // parts
    for part in range(parts):
        here = slice(part * size, (part + 1) * size)
        inner = dot(table_ref[here], stacked) + normed_ref[0, here].astype(F32)
        post = norm(inner, gain_ref[...]).astype(BF)
        hidden = jax.nn.gelu(dot(post, up_ref[...]) + bias_ref[...]).astype(BF)
        out = field_ref[0, here].astype(F32) + dot(hidden, down_ref[...])
        out_ref[0, here] = out.astype(BF)


def finish(synth, normed, field, table, gain, up, bias, down):
    devices, rows, modes_here, width = synth.shape
    nlon, chan = field.shape[1:]
    hidden = up.shape[1]
    whole = lambda a: pl.BlockSpec(a.shape, lambda j: (0,) * a.ndim)
    row_block = pl.BlockSpec((1, nlon, chan), lambda j: (j, 0, 0))
    gain = gain.reshape(1, chan)
    bias = bias.reshape(1, hidden)
    return pl.pallas_call(
        functools.partial(finish_kernel, parts=3),
        grid=(rows,),
        in_specs=[
            pl.BlockSpec((devices, 1, modes_here, width), lambda j: (0, j, 0, 0)),
            row_block,
            row_block,
            whole(table),
            whole(gain),
            whole(up),
            whole(bias),
            whole(down),
        ],
        out_specs=row_block,
        out_shape=jax.ShapeDtypeStruct(field.shape, BF),
        compiler_params=pltpu.CompilerParams(vmem_limit_bytes=VMEM_LIMIT),
    )(synth, normed, field, table, gain, up, bias, down)


def shards(
    field,
    norm_gain,
    legendre_fwd,
    legendre_inv,
    degree_gain,
    mix_weight,
    mlp_gain,
    up_weight,
    up_bias,
    down_weight,
    *,
    devices,
):
    rows, nlon, chan = field.shape
    modes_here, degrees, all_lats = legendre_fwd.shape
    forward, inverse = tables(nlon, modes_here * devices)
    forward, inverse = jnp.asarray(forward), jnp.asarray(inverse)
    spec, normed = analyse(field, norm_gain, forward, devices, modes_here)
    arrived = lax.all_to_all(spec, "lat", split_axis=0, concat_axis=0, tiled=True)
    fwd = legendre_fwd.reshape(modes_here, degrees, devices, rows)
    fwd = fwd.transpose(0, 1, 3, 2).reshape(modes_here, degrees, all_lats)
    inv = legendre_inv.reshape(modes_here, degrees, devices, rows)
    inv = inv.transpose(0, 3, 2, 1).reshape(modes_here, all_lats, degrees)
    real, imag = mix_weight[0], mix_weight[1]
    weight = jnp.concatenate(
        [jnp.concatenate([real, imag], 1), jnp.concatenate([-imag, real], 1)], 0
    )
    back = middle(arrived, fwd, inv, degree_gain, weight)
    synth = lax.all_to_all(back, "lat", split_axis=0, concat_axis=0, tiled=True)
    return finish(synth, normed, field, inverse, mlp_gain, up_weight, up_bias, down_weight)


def solution(mesh):
    return jax.shard_map(
        functools.partial(shards, devices=mesh.shape["lat"]),
        mesh=mesh,
        in_specs=(
            P(("ens", "lat"), None, None),
            P(),
            P("lat", None, None),
            P("lat", None, None),
            P(),
            P(),
            P(),
            P(),
            P(),
            P(),
        ),
        out_specs=P(("ens", "lat"), None, None),
        check_vma=False,
    )
```

profile of v0, /device:TPU:15, one launch (start us, length us, event | category | flops | bytes accessed | tf_op | source)
XLA Modules:
  0.0 126.7 jit_solution(7583724007066067233)
XLA Ops:
  0.0 0.7 reshape.21.gain_ref
  0.7 1.4 %copy-done = bf16[512,1440]{1,0:T(8,128)(2,1)S(1)} copy-done((bf16[512,1440]{1,0:T(8,128)(2,1)S(1)}, bf16[512,1440]{1,0:T(8,128)(2,1)}, u32[]{:S(2)}) %copy-start) | copy-done | bytes 1474584
  2.1 8.2 %shard_map.136 = (bf16[16,4,16,768]{3,2,1,0:T(8,128)(2,1)}, bf16[4,1440,384]{2,1,0:T(8,128)(2,1)}) custom-call(bf16[4,1440,384]{2,1,0:T(8,128)(2,1)} %field_ref.3, f32[1,384]{1,0:T(1,128)S(1)} %reshape.21.gain_ref, bf16[512,1440]{1,0:T(8,128)(2,1)S(1)} %copy-done), custom_call_target="tpu_custom_call" | custom-call | tf_op jit(solution)/shard_map/pallas_call | solution.py:55
  10.3 6.7 %all-to-all-start = ((bf16[16,4,16,768]{3,2,1,0:T(8,128)(2,1)}), bf16[16,4,16,768]{3,2,1,0:T(8,128)(2,1)}, u32[]{:S(2)}, u32[]{:S(2)}) async-start(bf16[16,4,16,768]{3,2,1,0:T(8,128)(2,1)} %get-tuple-element.7), calls=%async_computation | async-start | bytes 3145728 | tf_op jit(solution)/shard_map/all_to_all | solution.py:176
  17.0 0.3 copy.19
  17.3 0.0 copy-start.8
  17.3 0.3 copy.20
  17.6 0.0 copy-start.6
  17.6 0.5 copy.22.fwd_ref
  18.1 0.2 copy-done.8
  18.3 0.1 reshape.24
  18.5 0.1 copy.21
  18.6 0.2 copy-done.6
  18.7 0.0 copy-start.4
  18.8 0.0 copy-start.5
  18.8 0.1 slice_bitcast_fusion
  18.8 0.1 maximum_maximum_fusion.weight_ref
  18.9 34.3 %all-to-all-done.arrived_ref = bf16[16,4,16,768]{3,2,1,0:T(8,128)(2,1)} async-done(((bf16[16,4,16,768]{3,2,1,0:T(8,128)(2,1)}), bf16[16,4,16,768]{3,2,1,0:T(8,128)(2,1)}, u32[]{:S(2)}, u32[]{:S(2)}) %all-to-all-start) | async-done | bytes 1572896 | tf_op jit(solution)/shard_map/all_to_all | solution.py:176
  53.3 9.0 %shard_map.137 = bf16[16,4,16,768]{3,2,1,0:T(8,128)(2,1)} custom-call(bf16[16,4,16,768]{3,2,1,0:T(8,128)(2,1)} %all-to-all-done.arrived_ref, bf16[16,256,64]{2,1,0:T(8,128)(2,1)S(1)} %copy.22.fwd_ref, bf16[16,64,256]{2,1,0:T(8,128)(2,1)S(1)} %bitcast.15, f32[256,384]{1,0:T(8,128)S(1)} %copy-done.5, bf16[768,768]{1,0:T(8,128)(2,1)S(1)} %maximum_maximum_fusion.weight_ref, ...), custom_call_target="tpu_custom_call" | custom-call | tf_op jit(solution)/shard_map/pallas_call | solution.py:102
  62.2 5.0 %all-to-all-start.1 = ((bf16[16,4,16,768]{3,2,1,0:T(8,128)(2,1)}), bf16[16,4,16,768]{3,2,1,0:T(8,128)(2,1)S(1)}, u32[]{:S(2)}, u32[]{:S(2)}) async-start(bf16[16,4,16,768]{3,2,1,0:T(8,128)(2,1)} %shard_map.137), calls=%async_computation.1 | async-start | bytes 3145728 | tf_op jit(solution)/shard_map/all_to_all | solution.py:186
  67.3 36.1 %all-to-all-done.1.synth_ref = bf16[16,4,16,768]{3,2,1,0:T(8,128)(2,1)S(1)} async-done(((bf16[16,4,16,768]{3,2,1,0:T(8,128)(2,1)}), bf16[16,4,16,768]{3,2,1,0:T(8,128)(2,1)S(1)}, u32[]{:S(2)}, u32[]{:S(2)}) %all-to-all-start.1) | async-done | bytes 1572896 | tf_op jit(solution)/shard_map/all_to_all | solution.py:186
  103.5 1.1 copy-done.2
  104.5 1.1 copy-done.3
  105.6 21.1 %shard_map.138 = bf16[4,1440,384]{2,1,0:T(8,128)(2,1)} custom-call(bf16[16,4,16,768]{3,2,1,0:T(8,128)(2,1)S(1)} %all-to-all-done.1.synth_ref, bf16[4,1440,384]{2,1,0:T(8,128)(2,1)} %get-tuple-element.8.normed_ref, bf16[4,1440,384]{2,1,0:T(8,128)(2,1)} %field_ref.3, bf16[1440,512]{1,0:T(8,128)(2,1)S(1)} %copy-done.1, f32[1,384]{1,0:T(1,128)S(1)} %reshape.26.gain_ref, ...), custom_call_target="tpu_custom_call" | custom-call | tf_op jit(solution)/shard_map/pallas_call | solution.py:138
  (16 shorter events, 0.1 us)
Async XLA Ops:
  0.7 1.4 %copy-start = (bf16[512,1440]{1,0:T(8,128)(2,1)S(1)}, bf16[512,1440]{1,0:T(8,128)(2,1)}, u32[]{:S(2)}) copy-start(bf16[512,1440]{1,0:T(8,128)(2,1)} %constant.6.clone.table_ref) | copy-start | bytes 4423684
  10.3 6.7 %copy-start.7 = (bf16[16,256,64]{1,2,0:T(8,128)(2,1)S(1)}, bf16[16,256,64]{1,2,0:T(8,128)(2,1)}, u32[]{:S(2)}) copy-start(bf16[16,256,64]{1,2,0:T(8,128)(2,1)} %param.16) | copy-start | bytes 1572868
  10.3 43.0 %all-to-all-start = ((bf16[16,4,16,768]{3,2,1,0:T(8,128)(2,1)}), bf16[16,4,16,768]{3,2,1,0:T(8,128)(2,1)}, u32[]{:S(2)}, u32[]{:S(2)}) async-start(bf16[16,4,16,768]{3,2,1,0:T(8,128)(2,1)} %get-tuple-element.7), calls=%async_computation | async-start | bytes 3145728 | tf_op jit(solution)/shard_map/all_to_all | solution.py:176
  17.3 1.0 copy-start.8
  17.6 1.1 copy-start.6
  18.7 34.5 %copy-start.4 = (bf16[256,256]{1,0:T(8,128)(2,1)S(1)}, bf16[256,256]{1,0:T(8,128)(2,1)}, u32[]{:S(2)}) copy-start(bf16[256,256]{1,0:T(8,128)(2,1)} %constant.8.clone.to_modes_ref.to_rows_ref) | copy-start | bytes 393220
  18.8 34.5 %copy-start.5 = (f32[256,384]{1,0:T(8,128)S(1)}, f32[256,384]{1,0:T(8,128)}, u32[]{:S(2)}) copy-start(f32[256,384]{1,0:T(8,128)} %gain_ref.1) | copy-start | bytes 1179652
  62.2 5.0 %copy-start.10 = (f32[384]{0:T(512)S(1)}, f32[384]{0:T(512)}, u32[]{:S(2)}) copy-start(f32[384]{0:T(512)} %param.20) | copy-start | bytes 4612
  62.2 5.1 %copy-start.9 = (f32[768]{0:T(1024)S(1)}, f32[768]{0:T(1024)}, u32[]{:S(2)}) copy-start(f32[768]{0:T(1024)} %param.22) | copy-start | bytes 9220
  62.2 41.2 %copy-start.1 = (bf16[1440,512]{1,0:T(8,128)(2,1)S(1)}, bf16[1440,512]{1,0:T(8,128)(2,1)}, u32[]{:S(2)}) copy-start(bf16[1440,512]{1,0:T(8,128)(2,1)} %constant.7.clone.table_ref) | copy-start | bytes 4423684
  62.2 41.2 %all-to-all-start.1 = ((bf16[16,4,16,768]{3,2,1,0:T(8,128)(2,1)}), bf16[16,4,16,768]{3,2,1,0:T(8,128)(2,1)S(1)}, u32[]{:S(2)}, u32[]{:S(2)}) async-start(bf16[16,4,16,768]{3,2,1,0:T(8,128)(2,1)} %shard_map.137), calls=%async_computation.1 | async-start | bytes 3145728 | tf_op jit(solution)/shard_map/all_to_all | solution.py:186
  103.5 1.1 copy-start.2
  104.5 1.1 copy-start.3
where the time goes:
time: 127 us
  waiting for transfers between devices  70.5 us (56%)
  Pallas kernels  38.3 us (30%)
  starting transfers between devices  11.7 us (9%)
  local copies, waits for them, and re-layouts  5.98 us (5%)
    all_to_all x1, waiting for transfers between devices, shards(): synth = lax.all_to_all(back, 'lat', split_axis=0, concat_axis=0, tiled=True)  36.1 us
    all_to_all x1, waiting for transfers between devices, shards(): lax.all_to_all(spec, 'lat', split_axis=0, concat_axis=0, tiled=True)  34.3 us
    pallas_call x1, Pallas kernels, finish(): pl.pallas_call(functools.partial(finish_kernel, parts=3), grid=(rows,), i...  21.1 us
    pallas_call x1, Pallas kernels, middle(): pl.pallas_call(middle_kernel, out_shape=jax.ShapeDtypeStruct(arrived.shap...  8.95 us
    pallas_call x1, Pallas kernels, analyse(): pl.pallas_call(analyse_kernel, grid=(rows,), in_specs=[pl.BlockSpec((1, n...  8.21 us
    all_to_all x1, starting transfers between devices, shards(): lax.all_to_all(spec, 'lat', split_axis=0, concat_axis=0, tiled=True)  6.69 us
    all_to_all x1, starting transfers between devices, shards(): synth = lax.all_to_all(back, 'lat', split_axis=0, concat_axis=0, tiled=True)  5.04 us
    unnamed x23, local copies, waits for them, and re-layouts  4.25 us
  transfers between devices with their start and end apart: 2, of which 2 were waited for; matrix products, arithmetic and copies ran while one was open for 1% of the time, Pallas kernels for 0%

commit v1 on v0

v1 whole, which is shorter than its diff:
```python
import functools
import math

import jax
import jax.numpy as jnp
import ml_dtypes
import numpy as np
from jax import lax
from jax.experimental import pallas as pl
from jax.experimental.pallas import tpu as pltpu
from jax.sharding import PartitionSpec as P

BF = jnp.bfloat16
F32 = jnp.float32
EPS = 1e-05
VMEM_LIMIT = 48 * 1024 * 1024


def tables(nlon, modes):
    lon = np.arange(nlon)
    wave = np.arange(modes)
    phase = (wave[:, None] * lon[None, :] % nlon) * (2.0 * math.pi / nlon)
    scale = 2.0 * math.pi / nlon
    weight = np.where(wave == 0, 1.0, 2.0)[:, None]
    forward = np.concatenate([scale * np.cos(phase), -scale * np.sin(phase)], 0)
    inverse = np.concatenate([weight * np.cos(phase), -weight * np.sin(phase)], 0).T
    as_bf = lambda a: a.astype(np.float32).astype(ml_dtypes.bfloat16)
    return as_bf(forward), as_bf(inverse)


def dot(a, b):
    return jnp.dot(a, b, preferred_element_type=F32)


def norm(values, gain):
    center = values - jnp.mean(values, axis=-1, keepdims=True)
    spread = jnp.mean(center * center, axis=-1, keepdims=True)
    return center * lax.rsqrt(spread + EPS) * gain


def cost(flops):
    return pl.CostEstimate(flops=4 * flops, bytes_accessed=0, transcendentals=0)


def analyse_kernel(me_ref, field_ref, gain_ref, table_ref, spec_ref, normed_ref):
    devices, unused, modes_here, width = spec_ref.shape
    modes = devices * modes_here
    chan = field_ref.shape[-1]
    normed = norm(field_ref[0].astype(F32), gain_ref[...]).astype(BF)
    normed_ref[0] = normed
    spec = dot(table_ref[...], normed).astype(BF)
    for device in range(devices):
        slot = jnp.bitwise_xor(me_ref[0], device)
        here = slice(device * modes_here, (device + 1) * modes_here)
        spec_ref[slot, 0, :, :chan] = spec[:modes][here]
        spec_ref[slot, 0, :, chan:] = spec[modes:][here]


def analyse(me, field, gain, table, devices, modes_here, first, rows):
    unused, nlon, chan = field.shape
    modes2 = table.shape[0]
    return pl.pallas_call(
        analyse_kernel,
        grid=(rows,),
        in_specs=[
            pl.BlockSpec(memory_space=pltpu.SMEM),
            pl.BlockSpec((1, nlon, chan), lambda j: (j + first, 0, 0)),
            pl.BlockSpec((1, chan), lambda j: (0, 0)),
            pl.BlockSpec((modes2, nlon), lambda j: (0, 0)),
        ],
        out_specs=[
            pl.BlockSpec((devices, 1, modes_here, 2 * chan), lambda j: (0, j, 0, 0)),
            pl.BlockSpec((1, nlon, chan), lambda j: (j, 0, 0)),
        ],
        out_shape=[
            jax.ShapeDtypeStruct((devices, rows, modes_here, 2 * chan), BF),
            jax.ShapeDtypeStruct((rows, nlon, chan), BF),
        ],
        compiler_params=pltpu.CompilerParams(vmem_limit_bytes=VMEM_LIMIT),
        cost_estimate=cost(2 * rows * modes2 * nlon * chan),
    )(me, field, gain.reshape(1, chan), table)


def prepare_kernel(fwd_ref, inv_ref, mix_ref, order_ref, fwd_out, inv_out, weight_out):
    chan = mix_ref.shape[-1]
    for mode in range(fwd_ref.shape[0]):
        fwd_out[mode] = dot(order_ref[...], fwd_ref[mode]).T.astype(BF)
        inv_out[mode] = dot(order_ref[...], inv_ref[mode]).astype(BF)
    weight_out[:chan, :chan] = mix_ref[0]
    weight_out[:chan, chan:] = mix_ref[1]
    weight_out[chan:, :chan] = -mix_ref[1]
    weight_out[chan:, chan:] = mix_ref[0]


def prepare(fwd, inv, mix, rows):
    modes_here, degrees, lats = fwd.shape
    chan = mix.shape[-1]
    order = np.arange(lats).reshape(lats // rows, rows).T.reshape(-1)
    order = np.eye(lats, dtype=np.float32)[order].astype(ml_dtypes.bfloat16)
    return pl.pallas_call(
        prepare_kernel,
        out_shape=[
            jax.ShapeDtypeStruct((modes_here, degrees, lats), BF),
            jax.ShapeDtypeStruct((modes_here, lats, degrees), BF),
            jax.ShapeDtypeStruct((2 * chan, 2 * chan), BF),
        ],
        compiler_params=pltpu.CompilerParams(vmem_limit_bytes=VMEM_LIMIT),
        cost_estimate=cost(4 * modes_here * degrees * lats * lats),
    )(fwd.transpose(0, 2, 1), inv.transpose(0, 2, 1), mix, jnp.asarray(order))


def middle_kernel(me_ref, *refs, chunks):
    arrived = refs[:chunks]
    fwd_ref, inv_ref, gain_ref, weight_ref, to_modes_ref, to_rows_ref = refs[chunks : chunks + 6]
    out = refs[chunks + 6 : 2 * chunks + 6]
    by_mode, back = refs[2 * chunks + 6 :]
    devices, unused, modes_here, width = arrived[0].shape
    places = [(ref, row) for ref in range(chunks) for row in range(arrived[ref].shape[1])]
    slots = [jnp.bitwise_xor(me_ref[0], device) for device in range(devices)]
    for at, (ref, row) in enumerate(places):
        block = jnp.concatenate([arrived[ref][slot, row] for slot in slots], axis=0)
        by_mode[at] = dot(to_modes_ref[...], block).astype(BF)
    gain = jnp.concatenate([gain_ref[...], gain_ref[...]], axis=1)
    for mode in range(modes_here):
        here = slice(mode * devices, (mode + 1) * devices)
        spectrum = jnp.concatenate([by_mode[at, here] for at in range(len(places))], axis=0)
        scaled = (dot(fwd_ref[mode], spectrum) * gain).astype(BF)
        synth = dot(inv_ref[mode], scaled).astype(BF)
        for at in range(len(places)):
            back[at, here] = synth[at * devices : (at + 1) * devices]
    for at, (ref, row) in enumerate(places):
        block = dot(to_rows_ref[...], back[at]).astype(BF)
        mixed = dot(block, weight_ref[...]).astype(BF)
        for device, slot in enumerate(slots):
            out[ref][slot, row] = mixed[device * modes_here : (device + 1) * modes_here]


def middle(me, arrived, fwd, inv, gain, weight):
    devices, unused, modes_here, width = arrived[0].shape
    rows = sum(a.shape[1] for a in arrived)
    flat = devices * modes_here
    source = np.arange(flat).reshape(devices, modes_here).T.reshape(-1)
    to_modes = np.eye(flat, dtype=np.float32)[source].astype(ml_dtypes.bfloat16)
    vmem = pl.BlockSpec(memory_space=pltpu.VMEM)
    return pl.pallas_call(
        functools.partial(middle_kernel, chunks=len(arrived)),
        in_specs=[pl.BlockSpec(memory_space=pltpu.SMEM)] + [vmem] * (len(arrived) + 6),
        out_specs=[vmem] * len(arrived),
        out_shape=[jax.ShapeDtypeStruct(a.shape, BF) for a in arrived],
        scratch_shapes=[
            pltpu.VMEM((rows, flat, width), BF),
            pltpu.VMEM((rows, flat, width), BF),
        ],
        compiler_params=pltpu.CompilerParams(vmem_limit_bytes=VMEM_LIMIT),
        cost_estimate=cost(4 * rows * flat * width * width),
    )(
        me,
        *arrived,
        fwd,
        inv,
        gain,
        weight,
        jnp.asarray(to_modes),
        jnp.asarray(np.ascontiguousarray(to_modes.T)),
    )


def finish_kernel(me_ref, synth_ref, normed_ref, field_ref, table_ref, gain_ref, up_ref, bias_ref, down_ref, *rest):
    out_ref, stacked = rest[-2:]
    devices, unused, modes_here, width = synth_ref.shape
    chan = width // 2
    modes = devices * modes_here
    for device in range(devices):
        slot = jnp.bitwise_xor(me_ref[0], device)
        at = device * modes_here
        stacked[at : at + modes_here] = synth_ref[slot, 0, :, :chan]
        stacked[modes + at : modes + at + modes_here] = synth_ref[slot, 0, :, chan:]
    inner = dot(table_ref[...], stacked[...]) + normed_ref[0].astype(F32)
    post = norm(inner, gain_ref[...]).astype(BF)
    hidden = jax.nn.gelu(dot(post, up_ref[...]) + bias_ref[...]).astype(BF)
    out_ref[0] = (field_ref[0].astype(F32) + dot(hidden, down_ref[...])).astype(BF)


def finish(me, synth, normed, field, table, gain, up, bias, down, first, result):
    devices, rows, modes_here, width = synth.shape
    nlon, chan = field.shape[1:]
    hidden = up.shape[1]
    whole = lambda a: pl.BlockSpec(a.shape, lambda j: (0,) * a.ndim)
    gain = gain.reshape(1, chan)
    bias = bias.reshape(1, hidden)
    placed = pl.BlockSpec((1, nlon, chan), lambda j: (j + first, 0, 0))
    operands = [me, synth, normed, field, table, gain, up, bias, down]
    specs = [
        pl.BlockSpec(memory_space=pltpu.SMEM),
        pl.BlockSpec((devices, 1, modes_here, width), lambda j: (0, j, 0, 0)),
        pl.BlockSpec((1, nlon, chan), lambda j: (j, 0, 0)),
        placed,
        whole(table),
        whole(gain),
        whole(up),
        whole(bias),
        whole(down),
    ]
    aliases = {}
    if result is not None:
        aliases = {len(operands): 0}
        operands.append(result)
        specs.append(pl.BlockSpec(memory_space=pl.ANY))
    return pl.pallas_call(
        finish_kernel,
        grid=(rows,),
        in_specs=specs,
        out_specs=placed,
        out_shape=jax.ShapeDtypeStruct(field.shape, BF),
        scratch_shapes=[pltpu.VMEM((2 * devices * modes_here, chan), BF)],
        input_output_aliases=aliases,
        compiler_params=pltpu.CompilerParams(vmem_limit_bytes=VMEM_LIMIT),
        cost_estimate=cost(2 * rows * nlon * chan * (devices * modes_here * 2 + 2 * hidden)),
    )(*operands)


NEAR = 2


def staged(devices):
    return devices % NEAR == 0 and devices & (devices - 1) == 0 and 8 <= devices <= 32


def swap(part, offset, devices):
    return lax.ppermute(part, "lat", [(a, a ^ offset) for a in range(devices)])


def after(values, early):
    return lax.optimization_barrier((values, early))[0]


def swap_near(blocks, devices):
    blocks = blocks.reshape((devices // NEAR, NEAR) + blocks.shape[1:])
    parts = [blocks[:, :1]]
    parts += [swap(blocks[:, k : k + 1], k, devices) for k in range(1, NEAR)]
    return jnp.concatenate(parts, 1)


def swap_far(blocks, devices):
    count = blocks.shape[0]
    parts = [blocks[:1]] + [None] * (count - 1)
    for k in range(count - 1, 0, -1):
        parts[k] = swap(blocks[k : k + 1], k * NEAR, devices)
    return parts


def joined(parts):
    blocks = jnp.concatenate(parts, 0)
    return blocks.reshape((-1,) + blocks.shape[2:])


def shards(
    field,
    norm_gain,
    legendre_fwd,
    legendre_inv,
    degree_gain,
    mix_weight,
    mlp_gain,
    up_weight,
    up_bias,
    down_weight,
    *,
    devices,
):
    rows, nlon, chan = field.shape
    modes_here, degrees, all_lats = legendre_fwd.shape
    forward, inverse = tables(nlon, modes_here * devices)
    forward, inverse = jnp.asarray(forward), jnp.asarray(inverse)
    me = jnp.zeros((1,), jnp.int32)
    if staged(devices):
        me = lax.axis_index("lat").astype(jnp.int32).reshape(1)
    take = lambda me, first, count: analyse(
        me, field, norm_gain, forward, devices, modes_here, first, count
    )
    give = lambda at, synth, result: finish(
        me, synth, normed[at], field, inverse, mlp_gain, up_weight, up_bias, down_weight, chunks[at][0], result
    )
    half = rows // 2
    chunks = [(0, half), (half, rows - half)]
    if not staged(devices):
        move = lambda blocks: lax.all_to_all(blocks, "lat", 0, 0, tiled=True)
        spec, normed = zip(*[take(me, *chunk) for chunk in chunks])
        fwd, inv, weight = prepare(legendre_fwd, legendre_inv, mix_weight, rows)
        back = middle(me, [move(blocks) for blocks in spec], fwd, inv, degree_gain, weight)
        return give(1, move(back[1]), give(0, move(back[0]), None))
    spec_a, normed_a = take(me, *chunks[0])
    spec_a = swap_near(spec_a, devices)
    spec_b, normed_b = take(after(me, spec_a[:, 1:]), *chunks[1])
    parts_a = swap_far(spec_a, devices)
    spec_b = swap_near(spec_b, devices)
    parts_b = swap_far(spec_b, devices)
    normed = [normed_a, normed_b]
    fwd, inv, weight = prepare(legendre_fwd, legendre_inv, mix_weight, rows)
    back = middle(me, [joined(parts_a), joined(parts_b)], fwd, inv, degree_gain, weight)
    parts_c = swap_far(swap_near(back[0], devices), devices)
    parts_d = swap_far(swap_near(back[1], devices), devices)
    result = give(0, after(joined(parts_c), parts_d[len(parts_d) - 3 :]), None)
    return give(1, joined(parts_d), result)


def solution(mesh):
    return jax.shard_map(
        functools.partial(shards, devices=mesh.shape["lat"]),
        mesh=mesh,
        in_specs=(
            P(("ens", "lat"), None, None),
            P(),
            P("lat", None, None),
            P("lat", None, None),
            P(),
            P(),
            P(),
            P(),
            P(),
            P(),
        ),
        out_specs=P(("ens", "lat"), None, None),
        check_vma=False,
    )
```

time: 127 us -> 120 us (0.945)
  the two profiles are of different devices: /device:TPU:15 before, /device:TPU:0 now
where the time goes in v1:
time: 120 us; the launch traced here: 119 us
  starting transfers between devices  46.4 us (39%)
  Pallas kernels  37.3 us (31%)
  waiting for transfers between devices  32.3 us (27%)
  local copies, waits for them, and re-layouts  2.59 us (2%)
    ppermute x32, starting transfers between devices, swap(): return lax.ppermute(part, 'lat', [(a, a ^ offset) for a in range(devices)])  46.4 us
    ppermute x32, waiting for transfers between devices, swap(): return lax.ppermute(part, 'lat', [(a, a ^ offset) for a in range(devices)])  32.3 us
    pallas_call x2, Pallas kernels, finish(): pl.pallas_call(finish_kernel, grid=(rows,), in_specs=specs, out_specs=pla...  21 us
    pallas_call x2, Pallas kernels, analyse(): pl.pallas_call(analyse_kernel, grid=(rows,), in_specs=[pl.BlockSpec(memor...  8.05 us
    pallas_call x1, Pallas kernels, middle(): pl.pallas_call(functools.partial(middle_kernel, chunks=len(arrived)), in_...  7.7 us
  transfers between devices with their start and end apart: 32, of which 12 were waited for; matrix products, arithmetic and copies ran while one was open for 0% of the time, Pallas kernels for 13%

profile of v1, /device:TPU:0, one launch (start us, length us, event | category | flops | bytes accessed | tf_op | source)
XLA Modules:
  0.0 119.2 jit_solution(4694618219434617017)
XLA Ops:
  2.1 4.1 %shard_map.145 = (bf16[16,2,16,768]{3,2,1,0:T(8,128)(2,1)S(1)}, bf16[2,1440,384]{2,1,0:T(8,128)(2,1)S(1)}) custom-call(s32[1]{0:T(128)} %bitcast.me_ref, bf16[4,1440,384]{2,1,0:T(8,128)(2,1)} %field_ref.7, f32[1,384]{1,0:T(1,128)S(1)} %reshape.40.gain_ref, bf16[512,1440]{1,0:T(8,128)(2,1)S(1)} %copy-done.8), custom_call_target="tpu_custom_call" | custom-call | flops 4529848320 | tf_op jit(solution)/shard_map/pallas_call | solution.py:62
  8.2 6.0 %collective-permute-start.7 = (bf16[1,2,2,16,768]{4,3,2,1,0:T(8,128)(2,1)S(1)}, bf16[1,2,2,16,768]{4,3,2,1,0:T(8,128)(2,1)S(1)}, u32[]{:S(2)}, u32[]{:S(2)}) collective-permute-start(bf16[1,2,2,16,768]{4,3,2,1,0:T(8,128)(2,1)S(1)} %get-tuple-element.57), channel_id=1, source_target_pairs={{0,14},{1,15},{2,12},{3,13},{4,10},{5,11},{6,8},{7,9},{8,6},{9,7},... | collective-permute-start | bytes 294920 | tf_op jit(solution)/shard_map/ppermute | solution.py:230
  14.7 2.9 %collective-permute-start.3 = (bf16[1,2,2,16,768]{4,3,2,1,0:T(8,128)(2,1)S(1)}, bf16[1,2,2,16,768]{4,3,2,1,0:T(8,128)(2,1)S(1)}, u32[]{:S(2)}, u32[]{:S(2)}) collective-permute-start(bf16[1,2,2,16,768]{4,3,2,1,0:T(8,128)(2,1)S(1)} %get-tuple-element.61), channel_id=1, source_target_pairs={{0,6},{1,7},{2,4},{3,5},{4,2},{5,3},{6,0},{7,1},{8,14},{9,15},{10,... | collective-permute-start | bytes 294920 | tf_op jit(solution)/shard_map/ppermute | solution.py:230
  17.6 4.0 %shard_map.146 = (bf16[16,2,16,768]{3,2,1,0:T(8,128)(2,1)S(1)}, bf16[2,1440,384]{2,1,0:T(8,128)(2,1)S(1)}) custom-call(s32[1]{0:T(128)} %bitcast.me_ref, bf16[4,1440,384]{2,1,0:T(8,128)(2,1)} %field_ref.7, f32[1,384]{1,0:T(1,128)S(1)} %reshape.40.gain_ref, bf16[512,1440]{1,0:T(8,128)(2,1)S(1)} %copy-done.8), custom_call_target="tpu_custom_call" | custom-call | flops 4529848320 | tf_op jit(solution)/shard_map/pallas_call | solution.py:62
  21.7 3.0 %collective-permute-start.5 = (bf16[1,2,2,16,768]{4,3,2,1,0:T(8,128)(2,1)S(1)}, bf16[1,2,2,16,768]{4,3,2,1,0:T(8,128)(2,1)S(1)}, u32[]{:S(2)}, u32[]{:S(2)}) collective-permute-start(bf16[1,2,2,16,768]{4,3,2,1,0:T(8,128)(2,1)S(1)} %get-tuple-element.63), channel_id=1, source_target_pairs={{0,10},{1,11},{2,8},{3,9},{4,14},{5,15},{6,12},{7,13},{8,2},{9,3},... | collective-permute-start | bytes 294920 | tf_op jit(solution)/shard_map/ppermute | solution.py:230
  25.7 6.7 %collective-permute-done.5 = bf16[1,2,2,16,768]{4,3,2,1,0:T(8,128)(2,1)S(1)} collective-permute-done((bf16[1,2,2,16,768]{4,3,2,1,0:T(8,128)(2,1)S(1)}, bf16[1,2,2,16,768]{4,3,2,1,0:T(8,128)(2,1)S(1)}, u32[]{:S(2)}, u32[]{:S(2)}) %collective-permute-start.5) | collective-permute-done | bytes 98336 | tf_op jit(solution)/shard_map/ppermute | solution.py:230
  33.2 3.4 %collective-permute-start.15 = (bf16[1,2,2,16,768]{4,3,2,1,0:T(8,128)(2,1)S(1)}, bf16[1,2,2,16,768]{4,3,2,1,0:T(8,128)(2,1)S(1)}, u32[]{:S(2)}, u32[]{:S(2)}) collective-permute-start(bf16[1,2,2,16,768]{4,3,2,1,0:T(8,128)(2,1)S(1)} %get-tuple-element.47), channel_id=1, source_target_pairs={{0,14},{1,15},{2,12},{3,13},{4,10},{5,11},{6,8},{7,9},{8,6},{9,7},... | collective-permute-start | bytes 294920 | tf_op jit(solution)/shard_map/ppermute | solution.py:230
  36.9 2.0 %collective-permute-start.11 = (bf16[1,2,2,16,768]{4,3,2,1,0:T(8,128)(2,1)S(1)}, bf16[1,2,2,16,768]{4,3,2,1,0:T(8,128)(2,1)S(1)}, u32[]{:S(2)}, u32[]{:S(2)}) collective-permute-start(bf16[1,2,2,16,768]{4,3,2,1,0:T(8,128)(2,1)S(1)} %get-tuple-element.51), channel_id=1, source_target_pairs={{0,6},{1,7},{2,4},{3,5},{4,2},{5,3},{6,0},{7,1},{8,14},{9,15},{10,... | collective-permute-start | bytes 294920 | tf_op jit(solution)/shard_map/ppermute | solution.py:230
  39.3 3.4 %collective-permute-start.13 = (bf16[1,2,2,16,768]{4,3,2,1,0:T(8,128)(2,1)S(1)}, bf16[1,2,2,16,768]{4,3,2,1,0:T(8,128)(2,1)S(1)}, u32[]{:S(2)}, u32[]{:S(2)}) collective-permute-start(bf16[1,2,2,16,768]{4,3,2,1,0:T(8,128)(2,1)S(1)} %get-tuple-element.53), channel_id=1, source_target_pairs={{0,10},{1,11},{2,8},{3,9},{4,14},{5,15},{6,12},{7,13},{8,2},{9,3},... | collective-permute-start | bytes 294920 | tf_op jit(solution)/shard_map/ppermute | solution.py:230
  42.7 1.7 %collective-permute-start.14 = (bf16[1,2,2,16,768]{4,3,2,1,0:T(8,128)(2,1)S(1)}, bf16[1,2,2,16,768]{4,3,2,1,0:T(8,128)(2,1)S(1)}, u32[]{:S(2)}, u32[]{:S(2)}) collective-permute-start(bf16[1,2,2,16,768]{4,3,2,1,0:T(8,128)(2,1)S(1)} %get-tuple-element.54), channel_id=1, source_target_pairs={{0,12},{1,13},{2,14},{3,15},{4,8},{5,9},{6,10},{7,11},{8,4},{9,5},... | collective-permute-start | bytes 294920 | tf_op jit(solution)/shard_map/ppermute | solution.py:230
  45.3 4.8 %collective-permute-done.12 = bf16[1,2,2,16,768]{4,3,2,1,0:T(8,128)(2,1)S(1)} collective-permute-done((bf16[1,2,2,16,768]{4,3,2,1,0:T(8,128)(2,1)S(1)}, bf16[1,2,2,16,768]{4,3,2,1,0:T(8,128)(2,1)S(1)}, u32[]{:S(2)}, u32[]{:S(2)}) %collective-permute-start.12) | collective-permute-done | bytes 98336 | tf_op jit(solution)/shard_map/ppermute | solution.py:230
  50.1 2.4 %collective-permute-done.13 = bf16[1,2,2,16,768]{4,3,2,1,0:T(8,128)(2,1)S(1)} collective-permute-done((bf16[1,2,2,16,768]{4,3,2,1,0:T(8,128)(2,1)S(1)}, bf16[1,2,2,16,768]{4,3,2,1,0:T(8,128)(2,1)S(1)}, u32[]{:S(2)}, u32[]{:S(2)}) %collective-permute-start.13) | collective-permute-done | bytes 98336 | tf_op jit(solution)/shard_map/ppermute | solution.py:230
  52.6 7.7 %shard_map.148 = (bf16[16,2,16,768]{3,2,1,0:T(8,128)(2,1)S(1)}, bf16[16,2,16,768]{3,2,1,0:T(8,128)(2,1)S(1)}) custom-call(s32[1]{0:T(128)} %bitcast.me_ref, bf16[16,2,16,768]{3,2,1,0:T(8,128)(2,1)S(1)} %bitcast.19, bf16[16,2,16,768]{3,2,1,0:T(8,128)(2,1)S(1)} %bitcast.20, bf16[16,256,64]{2,1,0:T(8,128)(2,1)S(1)} %get-tuple-element.19.refs_2_, ...), custom_call_target="tpu_custom_call" | custom-call | flops 9663676416 | tf_op jit(solution)/shard_map/pallas_call | solution.py:145
  62.2 2.7 %collective-permute-start.31 = (bf16[1,2,2,16,768]{4,3,2,1,0:T(8,128)(2,1)S(1)}, bf16[1,2,2,16,768]{4,3,2,1,0:T(8,128)(2,1)S(1)}, u32[]{:S(2)}, u32[]{:S(2)}) collective-permute-start(bf16[1,2,2,16,768]{4,3,2,1,0:T(8,128)(2,1)S(1)} %get-tuple-element.27), channel_id=1, source_target_pairs={{0,14},{1,15},{2,12},{3,13},{4,10},{5,11},{6,8},{7,9},{8,6},{9,7},... | collective-permute-start | bytes 294920 | tf_op jit(solution)/shard_map/ppermute | solution.py:230
  66.2 2.2 %collective-permute-start.27 = (bf16[1,2,2,16,768]{4,3,2,1,0:T(8,128)(2,1)S(1)}, bf16[1,2,2,16,768]{4,3,2,1,0:T(8,128)(2,1)S(1)}, u32[]{:S(2)}, u32[]{:S(2)}) collective-permute-start(bf16[1,2,2,16,768]{4,3,2,1,0:T(8,128)(2,1)S(1)} %get-tuple-element.31), channel_id=1, source_target_pairs={{0,6},{1,7},{2,4},{3,5},{4,2},{5,3},{6,0},{7,1},{8,14},{9,15},{10,... | collective-permute-start | bytes 294920 | tf_op jit(solution)/shard_map/ppermute | solution.py:230
  68.9 2.7 %collective-permute-done.25 = bf16[1,2,2,16,768]{4,3,2,1,0:T(8,128)(2,1)S(1)} collective-permute-done((bf16[1,2,2,16,768]{4,3,2,1,0:T(8,128)(2,1)S(1)}, bf16[1,2,2,16,768]{4,3,2,1,0:T(8,128)(2,1)S(1)}, u32[]{:S(2)}, u32[]{:S(2)}) %collective-permute-start.25) | collective-permute-done | bytes 98336 | tf_op jit(solution)/shard_map/ppermute | solution.py:230
  76.0 3.0 %collective-permute-start.23 = (bf16[1,2,2,16,768]{4,3,2,1,0:T(8,128)(2,1)S(1)}, bf16[1,2,2,16,768]{4,3,2,1,0:T(8,128)(2,1)S(1)}, u32[]{:S(2)}, u32[]{:S(2)}) collective-permute-start(bf16[1,2,2,16,768]{4,3,2,1,0:T(8,128)(2,1)S(1)} %get-tuple-element.37), channel_id=1, source_target_pairs={{0,14},{1,15},{2,12},{3,13},{4,10},{5,11},{6,8},{7,9},{8,6},{9,7},... | collective-permute-start | bytes 294920 | tf_op jit(solution)/shard_map/ppermute | solution.py:230
  79.0 3.6 %collective-permute-start.17 = (bf16[1,2,2,16,768]{4,3,2,1,0:T(8,128)(2,1)S(1)}, bf16[1,2,2,16,768]{4,3,2,1,0:T(8,128)(2,1)S(1)}, u32[]{:S(2)}, u32[]{:S(2)}) collective-permute-start(bf16[1,2,2,16,768]{4,3,2,1,0:T(8,128)(2,1)S(1)} %get-tuple-element.39), channel_id=1, source_target_pairs={{0,2},{1,3},{2,0},{3,1},{4,6},{5,7},{6,4},{7,5},{8,10},{9,11},{10,... | collective-permute-start | bytes 294920 | tf_op jit(solution)/shard_map/ppermute | solution.py:230
  82.6 2.6 %collective-permute-done.29 = bf16[1,2,2,16,768]{4,3,2,1,0:T(8,128)(2,1)S(1)} collective-permute-done((bf16[1,2,2,16,768]{4,3,2,1,0:T(8,128)(2,1)S(1)}, bf16[1,2,2,16,768]{4,3,2,1,0:T(8,128)(2,1)S(1)}, u32[]{:S(2)}, u32[]{:S(2)}) %collective-permute-start.29) | collective-permute-done | bytes 98336 | tf_op jit(solution)/shard_map/ppermute | solution.py:230
  85.3 3.5 %collective-permute-start.21 = (bf16[1,2,2,16,768]{4,3,2,1,0:T(8,128)(2,1)S(1)}, bf16[1,2,2,16,768]{4,3,2,1,0:T(8,128)(2,1)S(1)}, u32[]{:S(2)}, u32[]{:S(2)}) collective-permute-start(bf16[1,2,2,16,768]{4,3,2,1,0:T(8,128)(2,1)S(1)} %get-tuple-element.43), channel_id=1, source_target_pairs={{0,10},{1,11},{2,8},{3,9},{4,14},{5,15},{6,12},{7,13},{8,2},{9,3},... | collective-permute-start | bytes 294920 | tf_op jit(solution)/shard_map/ppermute | solution.py:230
  88.8 1.6 %collective-permute-start.22 = (bf16[1,2,2,16,768]{4,3,2,1,0:T(8,128)(2,1)S(1)}, bf16[1,2,2,16,768]{4,3,2,1,0:T(8,128)(2,1)S(1)}, u32[]{:S(2)}, u32[]{:S(2)}) collective-permute-start(bf16[1,2,2,16,768]{4,3,2,1,0:T(8,128)(2,1)S(1)} %get-tuple-element.44), channel_id=1, source_target_pairs={{0,12},{1,13},{2,14},{3,15},{4,8},{5,9},{6,10},{7,11},{8,4},{9,5},... | collective-permute-start | bytes 294920 | tf_op jit(solution)/shard_map/ppermute | solution.py:230
  90.4 7.7 %collective-permute-done.21 = bf16[1,2,2,16,768]{4,3,2,1,0:T(8,128)(2,1)S(1)} collective-permute-done((bf16[1,2,2,16,768]{4,3,2,1,0:T(8,128)(2,1)S(1)}, bf16[1,2,2,16,768]{4,3,2,1,0:T(8,128)(2,1)S(1)}, u32[]{:S(2)}, u32[]{:S(2)}) %collective-permute-start.21) | collective-permute-done | bytes 98336 | tf_op jit(solution)/shard_map/ppermute | solution.py:230
  98.1 10.6 %shard_map.149.rest_0_ = bf16[4,1440,384]{2,1,0:T(8,128)(2,1)} custom-call(s32[1]{0:T(128)} %bitcast.me_ref, bf16[16,2,16,768]{3,2,1,0:T(8,128)(2,1)S(1)} %bitcast.18, bf16[2,1440,384]{2,1,0:T(8,128)(2,1)S(1)} %get-tuple-element.26.normed_ref, bf16[4,1440,384]{2,1,0:T(8,128)(2,1)} %field_ref.7, bf16[1440,512]{1,0:T(8,128)(2,1)S(1)} %copy-done.9, ...), custom_call_target="tpu_custom_call" | custom-call | flops 18119393280 | tf_op jit(solution)/shard_map/pallas_call | solution.py:209
  108.8 10.4 %shard_map.150 = bf16[4,1440,384]{2,1,0:T(8,128)(2,1)} custom-call(s32[1]{0:T(128)} %bitcast.me_ref, bf16[16,2,16,768]{3,2,1,0:T(8,128)(2,1)S(1)} %bitcast.17, bf16[2,1440,384]{2,1,0:T(8,128)(2,1)S(1)} %get-tuple-element.23.normed_ref, bf16[4,1440,384]{2,1,0:T(8,128)(2,1)} %field_ref.7, ...), custom_call_target="tpu_custom_call", output_to_operand_aliasing={{}: (9, {})} | custom-call | flops 18119393280 | tf_op jit(solution)/shard_map/pallas_call | solution.py:209
  (111 shorter events, 16.2 us)
Async XLA Ops:
  8.2 25.0 %collective-permute-start.7 = (bf16[1,2,2,16,768]{4,3,2,1,0:T(8,128)(2,1)S(1)}, bf16[1,2,2,16,768]{4,3,2,1,0:T(8,128)(2,1)S(1)}, u32[]{:S(2)}, u32[]{:S(2)}) collective-permute-start(bf16[1,2,2,16,768]{4,3,2,1,0:T(8,128)(2,1)S(1)} %get-tuple-element.57), channel_id=1, source_target_pairs={{0,14},{1,15},{2,12},{3,13},{4,10},{5,11},{6,8},{7,9},{8,6},{9,7},... | collective-permute-start | bytes 294920 | tf_op jit(solution)/shard_map/ppermute | solution.py:230
  14.7 10.0 %collective-permute-start.2 = (bf16[1,2,2,16,768]{4,3,2,1,0:T(8,128)(2,1)S(1)}, bf16[1,2,2,16,768]{4,3,2,1,0:T(8,128)(2,1)S(1)}, u32[]{:S(2)}, u32[]{:S(2)}) collective-permute-start(bf16[1,2,2,16,768]{4,3,2,1,0:T(8,128)(2,1)S(1)} %get-tuple-element.60), channel_id=1, source_target_pairs={{0,4},{1,5},{2,6},{3,7},{4,0},{5,1},{6,2},{7,3},{8,12},{9,13},{10,... | collective-permute-start | bytes 294920 | tf_op jit(solution)/shard_map/ppermute | solution.py:230
  14.7 10.2 %collective-permute-start.3 = (bf16[1,2,2,16,768]{4,3,2,1,0:T(8,128)(2,1)S(1)}, bf16[1,2,2,16,768]{4,3,2,1,0:T(8,128)(2,1)S(1)}, u32[]{:S(2)}, u32[]{:S(2)}) collective-permute-start(bf16[1,2,2,16,768]{4,3,2,1,0:T(8,128)(2,1)S(1)} %get-tuple-element.61), channel_id=1, source_target_pairs={{0,6},{1,7},{2,4},{3,5},{4,2},{5,3},{6,0},{7,1},{8,14},{9,15},{10,... | collective-permute-start | bytes 294920 | tf_op jit(solution)/shard_map/ppermute | solution.py:230
  17.6 8.1 %collective-permute-start.4 = (bf16[1,2,2,16,768]{4,3,2,1,0:T(8,128)(2,1)S(1)}, bf16[1,2,2,16,768]{4,3,2,1,0:T(8,128)(2,1)S(1)}, u32[]{:S(2)}, u32[]{:S(2)}) collective-permute-start(bf16[1,2,2,16,768]{4,3,2,1,0:T(8,128)(2,1)S(1)} %get-tuple-element.62), channel_id=1, source_target_pairs={{0,8},{1,9},{2,10},{3,11},{4,12},{5,13},{6,14},{7,15},{8,0},{9,1},... | collective-permute-start | bytes 294920 | tf_op jit(solution)/shard_map/ppermute | solution.py:230
  21.7 10.8 %collective-permute-start.5 = (bf16[1,2,2,16,768]{4,3,2,1,0:T(8,128)(2,1)S(1)}, bf16[1,2,2,16,768]{4,3,2,1,0:T(8,128)(2,1)S(1)}, u32[]{:S(2)}, u32[]{:S(2)}) collective-permute-start(bf16[1,2,2,16,768]{4,3,2,1,0:T(8,128)(2,1)S(1)} %get-tuple-element.63), channel_id=1, source_target_pairs={{0,10},{1,11},{2,8},{3,9},{4,14},{5,15},{6,12},{7,13},{8,2},{9,3},... | collective-permute-start | bytes 294920 | tf_op jit(solution)/shard_map/ppermute | solution.py:230
  24.7 7.8 %collective-permute-start.6 = (bf16[1,2,2,16,768]{4,3,2,1,0:T(8,128)(2,1)S(1)}, bf16[1,2,2,16,768]{4,3,2,1,0:T(8,128)(2,1)S(1)}, u32[]{:S(2)}, u32[]{:S(2)}) collective-permute-start(bf16[1,2,2,16,768]{4,3,2,1,0:T(8,128)(2,1)S(1)} %get-tuple-element.64), channel_id=1, source_target_pairs={{0,12},{1,13},{2,14},{3,15},{4,8},{5,9},{6,10},{7,11},{8,4},{9,5},... | collective-permute-start | bytes 294920 | tf_op jit(solution)/shard_map/ppermute | solution.py:230
  33.2 19.3 %collective-permute-start.15 = (bf16[1,2,2,16,768]{4,3,2,1,0:T(8,128)(2,1)S(1)}, bf16[1,2,2,16,768]{4,3,2,1,0:T(8,128)(2,1)S(1)}, u32[]{:S(2)}, u32[]{:S(2)}) collective-permute-start(bf16[1,2,2,16,768]{4,3,2,1,0:T(8,128)(2,1)S(1)} %get-tuple-element.47), channel_id=1, source_target_pairs={{0,14},{1,15},{2,12},{3,13},{4,10},{5,11},{6,8},{7,9},{8,6},{9,7},... | collective-permute-start | bytes 294920 | tf_op jit(solution)/shard_map/ppermute | solution.py:230
  36.9 8.3 %collective-permute-start.11 = (bf16[1,2,2,16,768]{4,3,2,1,0:T(8,128)(2,1)S(1)}, bf16[1,2,2,16,768]{4,3,2,1,0:T(8,128)(2,1)S(1)}, u32[]{:S(2)}, u32[]{:S(2)}) collective-permute-start(bf16[1,2,2,16,768]{4,3,2,1,0:T(8,128)(2,1)S(1)} %get-tuple-element.51), channel_id=1, source_target_pairs={{0,6},{1,7},{2,4},{3,5},{4,2},{5,3},{6,0},{7,1},{8,14},{9,15},{10,... | collective-permute-start | bytes 294920 | tf_op jit(solution)/shard_map/ppermute | solution.py:230
  38.9 11.2 %collective-permute-start.12 = (bf16[1,2,2,16,768]{4,3,2,1,0:T(8,128)(2,1)S(1)}, bf16[1,2,2,16,768]{4,3,2,1,0:T(8,128)(2,1)S(1)}, u32[]{:S(2)}, u32[]{:S(2)}) collective-permute-start(bf16[1,2,2,16,768]{4,3,2,1,0:T(8,128)(2,1)S(1)} %get-tuple-element.52), channel_id=1, source_target_pairs={{0,8},{1,9},{2,10},{3,11},{4,12},{5,13},{6,14},{7,15},{8,0},{9,1},... | collective-permute-start | bytes 294920 | tf_op jit(solution)/shard_map/ppermute | solution.py:230
  39.3 13.2 %collective-permute-start.13 = (bf16[1,2,2,16,768]{4,3,2,1,0:T(8,128)(2,1)S(1)}, bf16[1,2,2,16,768]{4,3,2,1,0:T(8,128)(2,1)S(1)}, u32[]{:S(2)}, u32[]{:S(2)}) collective-permute-start(bf16[1,2,2,16,768]{4,3,2,1,0:T(8,128)(2,1)S(1)} %get-tuple-element.53), channel_id=1, source_target_pairs={{0,10},{1,11},{2,8},{3,9},{4,14},{5,15},{6,12},{7,13},{8,2},{9,3},... | collective-permute-start | bytes 294920 | tf_op jit(solution)/shard_map/ppermute | solution.py:230
  42.7 9.8 %collective-permute-start.14 = (bf16[1,2,2,16,768]{4,3,2,1,0:T(8,128)(2,1)S(1)}, bf16[1,2,2,16,768]{4,3,2,1,0:T(8,128)(2,1)S(1)}, u32[]{:S(2)}, u32[]{:S(2)}) collective-permute-start(bf16[1,2,2,16,768]{4,3,2,1,0:T(8,128)(2,1)S(1)} %get-tuple-element.54), channel_id=1, source_target_pairs={{0,12},{1,13},{2,14},{3,15},{4,8},{5,9},{6,10},{7,11},{8,4},{9,5},... | collective-permute-start | bytes 294920 | tf_op jit(solution)/shard_map/ppermute | solution.py:230
  60.5 7.9 %collective-permute-start.16 = (bf16[8,1,2,16,768]{4,3,2,1,0:T(8,128)(2,1)S(1)}, bf16[8,1,2,16,768]{4,3,2,1,0:T(8,128)(2,1)S(1)}, u32[]{:S(2)}, u32[]{:S(2)}) collective-permute-start(bf16[8,1,2,16,768]{4,3,2,1,0:T(8,128)(2,1)S(1)} %get-tuple-element.46), channel_id=1, source_target_pairs={{0,1},{1,0},{2,3},{3,2},{4,5},{5,4},{6,7},{7,6},{8,9},{9,8},{10,11... | collective-permute-start | bytes 1179656 | tf_op jit(solution)/shard_map/ppermute | solution.py:230
  62.2 26.6 %collective-permute-start.31 = (bf16[1,2,2,16,768]{4,3,2,1,0:T(8,128)(2,1)S(1)}, bf16[1,2,2,16,768]{4,3,2,1,0:T(8,128)(2,1)S(1)}, u32[]{:S(2)}, u32[]{:S(2)}) collective-permute-start(bf16[1,2,2,16,768]{4,3,2,1,0:T(8,128)(2,1)S(1)} %get-tuple-element.27), channel_id=1, source_target_pairs={{0,14},{1,15},{2,12},{3,13},{4,10},{5,11},{6,8},{7,9},{8,6},{9,7},... | collective-permute-start | bytes 294920 | tf_op jit(solution)/shard_map/ppermute | solution.py:230
  66.2 9.8 %collective-permute-start.27 = (bf16[1,2,2,16,768]{4,3,2,1,0:T(8,128)(2,1)S(1)}, bf16[1,2,2,16,768]{4,3,2,1,0:T(8,128)(2,1)S(1)}, u32[]{:S(2)}, u32[]{:S(2)}) collective-permute-start(bf16[1,2,2,16,768]{4,3,2,1,0:T(8,128)(2,1)S(1)} %get-tuple-element.31), channel_id=1, source_target_pairs={{0,6},{1,7},{2,4},{3,5},{4,2},{5,3},{6,0},{7,1},{8,14},{9,15},{10,... | collective-permute-start | bytes 294920 | tf_op jit(solution)/shard_map/ppermute | solution.py:230
  68.4 10.6 %collective-permute-start.28 = (bf16[1,2,2,16,768]{4,3,2,1,0:T(8,128)(2,1)S(1)}, bf16[1,2,2,16,768]{4,3,2,1,0:T(8,128)(2,1)S(1)}, u32[]{:S(2)}, u32[]{:S(2)}) collective-permute-start(bf16[1,2,2,16,768]{4,3,2,1,0:T(8,128)(2,1)S(1)} %get-tuple-element.32), channel_id=1, source_target_pairs={{0,8},{1,9},{2,10},{3,11},{4,12},{5,13},{6,14},{7,15},{8,0},{9,1},... | collective-permute-start | bytes 294920 | tf_op jit(solution)/shard_map/ppermute | solution.py:230
  71.6 13.7 %collective-permute-start.29 = (bf16[1,2,2,16,768]{4,3,2,1,0:T(8,128)(2,1)S(1)}, bf16[1,2,2,16,768]{4,3,2,1,0:T(8,128)(2,1)S(1)}, u32[]{:S(2)}, u32[]{:S(2)}) collective-permute-start(bf16[1,2,2,16,768]{4,3,2,1,0:T(8,128)(2,1)S(1)} %get-tuple-element.33), channel_id=1, source_target_pairs={{0,10},{1,11},{2,8},{3,9},{4,14},{5,15},{6,12},{7,13},{8,2},{9,3},... | collective-permute-start | bytes 294920 | tf_op jit(solution)/shard_map/ppermute | solution.py:230
  73.9 11.4 %collective-permute-start.30 = (bf16[1,2,2,16,768]{4,3,2,1,0:T(8,128)(2,1)S(1)}, bf16[1,2,2,16,768]{4,3,2,1,0:T(8,128)(2,1)S(1)}, u32[]{:S(2)}, u32[]{:S(2)}) collective-permute-start(bf16[1,2,2,16,768]{4,3,2,1,0:T(8,128)(2,1)S(1)} %get-tuple-element.34), channel_id=1, source_target_pairs={{0,12},{1,13},{2,14},{3,15},{4,8},{5,9},{6,10},{7,11},{8,4},{9,5},... | collective-permute-start | bytes 294920 | tf_op jit(solution)/shard_map/ppermute | solution.py:230
  76.0 14.4 %collective-permute-start.23 = (bf16[1,2,2,16,768]{4,3,2,1,0:T(8,128)(2,1)S(1)}, bf16[1,2,2,16,768]{4,3,2,1,0:T(8,128)(2,1)S(1)}, u32[]{:S(2)}, u32[]{:S(2)}) collective-permute-start(bf16[1,2,2,16,768]{4,3,2,1,0:T(8,128)(2,1)S(1)} %get-tuple-element.37), channel_id=1, source_target_pairs={{0,14},{1,15},{2,12},{3,13},{4,10},{5,11},{6,8},{7,9},{8,6},{9,7},... | collective-permute-start | bytes 294920 | tf_op jit(solution)/shard_map/ppermute | solution.py:230
  79.0 29.7 %collective-permute-start.17 = (bf16[1,2,2,16,768]{4,3,2,1,0:T(8,128)(2,1)S(1)}, bf16[1,2,2,16,768]{4,3,2,1,0:T(8,128)(2,1)S(1)}, u32[]{:S(2)}, u32[]{:S(2)}) collective-permute-start(bf16[1,2,2,16,768]{4,3,2,1,0:T(8,128)(2,1)S(1)} %get-tuple-element.39), channel_id=1, source_target_pairs={{0,2},{1,3},{2,0},{3,1},{4,6},{5,7},{6,4},{7,5},{8,10},{9,11},{10,... | collective-permute-start | bytes 294920 | tf_op jit(solution)/shard_map/ppermute | solution.py:230
  85.2 23.5 %collective-permute-start.18 = (bf16[1,2,2,16,768]{4,3,2,1,0:T(8,128)(2,1)S(1)}, bf16[1,2,2,16,768]{4,3,2,1,0:T(8,128)(2,1)S(1)}, u32[]{:S(2)}, u32[]{:S(2)}) collective-permute-start(bf16[1,2,2,16,768]{4,3,2,1,0:T(8,128)(2,1)S(1)} %get-tuple-element.40), channel_id=1, source_target_pairs={{0,4},{1,5},{2,6},{3,7},{4,0},{5,1},{6,2},{7,3},{8,12},{9,13},{10,... | collective-permute-start | bytes 294920 | tf_op jit(solution)/shard_map/ppermute | solution.py:230
  85.3 12.8 %collective-permute-start.21 = (bf16[1,2,2,16,768]{4,3,2,1,0:T(8,128)(2,1)S(1)}, bf16[1,2,2,16,768]{4,3,2,1,0:T(8,128)(2,1)S(1)}, u32[]{:S(2)}, u32[]{:S(2)}) collective-permute-start(bf16[1,2,2,16,768]{4,3,2,1,0:T(8,128)(2,1)S(1)} %get-tuple-element.43), channel_id=1, source_target_pairs={{0,10},{1,11},{2,8},{3,9},{4,14},{5,15},{6,12},{7,13},{8,2},{9,3},... | collective-permute-start | bytes 294920 | tf_op jit(solution)/shard_map/ppermute | solution.py:230
  88.8 9.3 %collective-permute-start.22 = (bf16[1,2,2,16,768]{4,3,2,1,0:T(8,128)(2,1)S(1)}, bf16[1,2,2,16,768]{4,3,2,1,0:T(8,128)(2,1)S(1)}, u32[]{:S(2)}, u32[]{:S(2)}) collective-permute-start(bf16[1,2,2,16,768]{4,3,2,1,0:T(8,128)(2,1)S(1)} %get-tuple-element.44), channel_id=1, source_target_pairs={{0,12},{1,13},{2,14},{3,15},{4,8},{5,9},{6,10},{7,11},{8,4},{9,5},... | collective-permute-start | bytes 294920 | tf_op jit(solution)/shard_map/ppermute | solution.py:230
  90.4 18.4 %collective-permute-start.19 = (bf16[1,2,2,16,768]{4,3,2,1,0:T(8,128)(2,1)S(1)}, bf16[1,2,2,16,768]{4,3,2,1,0:T(8,128)(2,1)S(1)}, u32[]{:S(2)}, u32[]{:S(2)}) collective-permute-start(bf16[1,2,2,16,768]{4,3,2,1,0:T(8,128)(2,1)S(1)} %get-tuple-element.41), channel_id=1, source_target_pairs={{0,6},{1,7},{2,4},{3,5},{4,2},{5,3},{6,0},{7,1},{8,14},{9,15},{10,... | collective-permute-start | bytes 294920 | tf_op jit(solution)/shard_map/ppermute | solution.py:230
  98.1 10.7 %collective-permute-start.20 = (bf16[1,2,2,16,768]{4,3,2,1,0:T(8,128)(2,1)S(1)}, bf16[1,2,2,16,768]{4,3,2,1,0:T(8,128)(2,1)S(1)}, u32[]{:S(2)}, u32[]{:S(2)}) collective-permute-start(bf16[1,2,2,16,768]{4,3,2,1,0:T(8,128)(2,1)S(1)} %get-tuple-element.42), channel_id=1, source_target_pairs={{0,8},{1,9},{2,10},{3,11},{4,12},{5,13},{6,14},{7,15},{8,0},{9,1},... | collective-permute-start | bytes 294920 | tf_op jit(solution)/shard_map/ppermute | solution.py:230
  (21 other events, 247.6 us)

commit v2 on v1

--- a/solution.py
+++ b/solution.py
@@ -13,7 +13,9 @@
 BF = jnp.bfloat16
 F32 = jnp.float32
 EPS = 1e-05
-VMEM_LIMIT = 48 * 1024 * 1024
+GELU_LINEAR = math.sqrt(2.0 / math.pi)
+GELU_CUBIC = 0.044715 * GELU_LINEAR
+VMEM_LIMIT = 16 * 1024 * 1024
 
 
 def tables(nlon, modes):
@@ -78,7 +80,7 @@
         ],
         compiler_params=pltpu.CompilerParams(vmem_limit_bytes=VMEM_LIMIT),
         cost_estimate=cost(2 * rows * modes2 * nlon * chan),
-    )(me, field, gain.reshape(1, chan), table)
+    )(me, pltpu.with_memory_space_constraint(field, pltpu.HBM), gain.reshape(1, chan), pltpu.with_memory_space_constraint(table, pltpu.HBM))
 
 
 def prepare_kernel(fwd_ref, inv_ref, mix_ref, order_ref, fwd_out, inv_out, weight_out):
@@ -165,6 +167,12 @@
     )
 
 
+def gelu(x):
+    inner = x * (GELU_LINEAR + GELU_CUBIC * (x * x))
+    half = 0.5 * x
+    return half + half * jnp.tanh(inner)
+
+
 def finish_kernel(me_ref, synth_ref, normed_ref, field_ref, table_ref, gain_ref, up_ref, bias_ref, down_ref, *rest):
     out_ref, stacked = rest[-2:]
     devices, unused, modes_here, width = synth_ref.shape
@@ -177,8 +185,11 @@
         stacked[modes + at : modes + at + modes_here] = synth_ref[slot, 0, :, chan:]
     inner = dot(table_ref[...], stacked[...]) + normed_ref[0].astype(F32)
     post = norm(inner, gain_ref[...]).astype(BF)
-    hidden = jax.nn.gelu(dot(post, up_ref[...]) + bias_ref[...]).astype(BF)
-    out_ref[0] = (field_ref[0].astype(F32) + dot(hidden, down_ref[...])).astype(BF)
+    size = post.shape[0] // 2
+    for at in (0, size):
+        here = slice(at, at + size)
+        hidden = gelu((dot(post[here], up_ref[...]) + bias_ref[...]).astype(BF))
+        out_ref[0, here] = (field_ref[0, here].astype(F32) + dot(hidden, down_ref[...])).astype(BF)
 
 
 def finish(me, synth, normed, field, table, gain, up, bias, down, first, result):

time: 120 us -> 112 us (0.933)
  Pallas kernels: 37.3 us -> 32.7 us
  starting transfers between devices: 46.4 us -> 44.3 us
  local copies, waits for them, and re-layouts: 2.59 us -> 1.19 us
    pallas_call x2, Pallas kernels: 21 us -> 16.8 us  [finish(): pl.pallas_call(finish_kernel, grid=(rows,), in_specs=specs, out_specs=pla...]
    ppermute x32, starting transfers between devices: 46.4 us -> 44.3 us  [swap(): return lax.ppermute(part, 'lat', [(a, a ^ offset) for a in range(devices)])]
    unnamed x50, local copies, waits for them, and re-layouts: 1.65 us -> 0.26 us
    pallas_call x1, Pallas kernels: 7.7 us -> 6.43 us  [middle(): pl.pallas_call(functools.partial(middle_kernel, chunks=len(arrived)), in_...]
  transfers between devices with their start and end apart: 32 -> 32, of which waited for: 12 -> 11; matrix products, arithmetic and copies ran while one was open for 0% -> 0% of each run, Pallas kernels for 13% -> 12%
where the time goes in v2:
time: 112 us
  starting transfers between devices  44.3 us (40%)
  waiting for transfers between devices  33.2 us (30%)
  Pallas kernels  32.7 us (29%)
  local copies, waits for them, and re-layouts  1.19 us (1%)
    ppermute x32, starting transfers between devices, swap(): return lax.ppermute(part, 'lat', [(a, a ^ offset) for a in range(devices)])  44.3 us
    ppermute x32, waiting for transfers between devices, swap(): return lax.ppermute(part, 'lat', [(a, a ^ offset) for a in range(devices)])  33.2 us
    pallas_call x2, Pallas kernels, finish(): pl.pallas_call(finish_kernel, grid=(rows,), in_specs=specs, out_specs=pla...  16.8 us
    pallas_call x2, Pallas kernels, analyse(): pl.pallas_call(analyse_kernel, grid=(rows,), in_specs=[pl.BlockSpec(memor...  8.93 us
    pallas_call x1, Pallas kernels, middle(): pl.pallas_call(functools.partial(middle_kernel, chunks=len(arrived)), in_...  6.43 us
  transfers between devices with their start and end apart: 32, of which 11 were waited for; matrix products, arithmetic and copies ran while one was open for 0% of the time, Pallas kernels for 12%

profile of v2, /device:TPU:0, one launch (start us, length us, event | category | flops | bytes accessed | tf_op | source)
XLA Modules:
  0.0 112.1 jit_solution(8729549781339610373)
XLA Ops:
  0.7 4.5 %shard_map.145 = (bf16[16,2,16,768]{3,2,1,0:T(8,128)(2,1)S(1)}, bf16[2,1440,384]{2,1,0:T(8,128)(2,1)S(1)}) custom-call(s32[1]{0:T(128)} %bitcast.me_ref, bf16[4,1440,384]{2,1,0:T(8,128)(2,1)} %field_ref.7, f32[1,384]{1,0:T(1,128)S(1)} %reshape.40.gain_ref, bf16[512,1440]{1,0:T(8,128)(2,1)} %constant.12.clone.table_ref), custom_call_target="tpu_custom_call" | custom-call | flops 4529848320 | tf_op jit(solution)/shard_map/pallas_call | solution.py:64
  7.2 6.0 %collective-permute-start.7 = (bf16[1,2,2,16,768]{4,3,2,1,0:T(8,128)(2,1)S(1)}, bf16[1,2,2,16,768]{4,3,2,1,0:T(8,128)(2,1)S(1)}, u32[]{:S(2)}, u32[]{:S(2)}) collective-permute-start(bf16[1,2,2,16,768]{4,3,2,1,0:T(8,128)(2,1)S(1)} %get-tuple-element.57), channel_id=1, source_target_pairs={{0,14},{1,15},{2,12},{3,13},{4,10},{5,11},{6,8},{7,9},{8,6},{9,7},... | collective-permute-start | bytes 294920 | tf_op jit(solution)/shard_map/ppermute | solution.py:241
  13.7 3.0 %collective-permute-start.3 = (bf16[1,2,2,16,768]{4,3,2,1,0:T(8,128)(2,1)S(1)}, bf16[1,2,2,16,768]{4,3,2,1,0:T(8,128)(2,1)S(1)}, u32[]{:S(2)}, u32[]{:S(2)}) collective-permute-start(bf16[1,2,2,16,768]{4,3,2,1,0:T(8,128)(2,1)S(1)} %get-tuple-element.61), channel_id=1, source_target_pairs={{0,6},{1,7},{2,4},{3,5},{4,2},{5,3},{6,0},{7,1},{8,14},{9,15},{10,... | collective-permute-start | bytes 294920 | tf_op jit(solution)/shard_map/ppermute | solution.py:241
  16.7 4.4 %shard_map.146 = (bf16[16,2,16,768]{3,2,1,0:T(8,128)(2,1)S(1)}, bf16[2,1440,384]{2,1,0:T(8,128)(2,1)S(1)}) custom-call(s32[1]{0:T(128)} %bitcast.me_ref, bf16[4,1440,384]{2,1,0:T(8,128)(2,1)} %field_ref.7, f32[1,384]{1,0:T(1,128)S(1)} %reshape.40.gain_ref, bf16[512,1440]{1,0:T(8,128)(2,1)} %constant.12.clone.table_ref), custom_call_target="tpu_custom_call" | custom-call | flops 4529848320 | tf_op jit(solution)/shard_map/pallas_call | solution.py:64
  21.2 3.0 %collective-permute-start.5 = (bf16[1,2,2,16,768]{4,3,2,1,0:T(8,128)(2,1)S(1)}, bf16[1,2,2,16,768]{4,3,2,1,0:T(8,128)(2,1)S(1)}, u32[]{:S(2)}, u32[]{:S(2)}) collective-permute-start(bf16[1,2,2,16,768]{4,3,2,1,0:T(8,128)(2,1)S(1)} %get-tuple-element.63), channel_id=1, source_target_pairs={{0,10},{1,11},{2,8},{3,9},{4,14},{5,15},{6,12},{7,13},{8,2},{9,3},... | collective-permute-start | bytes 294920 | tf_op jit(solution)/shard_map/ppermute | solution.py:241
  24.5 7.5 %collective-permute-done.5 = bf16[1,2,2,16,768]{4,3,2,1,0:T(8,128)(2,1)S(1)} collective-permute-done((bf16[1,2,2,16,768]{4,3,2,1,0:T(8,128)(2,1)S(1)}, bf16[1,2,2,16,768]{4,3,2,1,0:T(8,128)(2,1)S(1)}, u32[]{:S(2)}, u32[]{:S(2)}) %collective-permute-start.5) | collective-permute-done | bytes 98336 | tf_op jit(solution)/shard_map/ppermute | solution.py:241
  32.7 3.5 %collective-permute-start.15 = (bf16[1,2,2,16,768]{4,3,2,1,0:T(8,128)(2,1)S(1)}, bf16[1,2,2,16,768]{4,3,2,1,0:T(8,128)(2,1)S(1)}, u32[]{:S(2)}, u32[]{:S(2)}) collective-permute-start(bf16[1,2,2,16,768]{4,3,2,1,0:T(8,128)(2,1)S(1)} %get-tuple-element.47), channel_id=1, source_target_pairs={{0,14},{1,15},{2,12},{3,13},{4,10},{5,11},{6,8},{7,9},{8,6},{9,7},... | collective-permute-start | bytes 294920 | tf_op jit(solution)/shard_map/ppermute | solution.py:241
  36.2 2.1 %collective-permute-start.11 = (bf16[1,2,2,16,768]{4,3,2,1,0:T(8,128)(2,1)S(1)}, bf16[1,2,2,16,768]{4,3,2,1,0:T(8,128)(2,1)S(1)}, u32[]{:S(2)}, u32[]{:S(2)}) collective-permute-start(bf16[1,2,2,16,768]{4,3,2,1,0:T(8,128)(2,1)S(1)} %get-tuple-element.51), channel_id=1, source_target_pairs={{0,6},{1,7},{2,4},{3,5},{4,2},{5,3},{6,0},{7,1},{8,14},{9,15},{10,... | collective-permute-start | bytes 294920 | tf_op jit(solution)/shard_map/ppermute | solution.py:241
  38.8 3.3 %collective-permute-start.13 = (bf16[1,2,2,16,768]{4,3,2,1,0:T(8,128)(2,1)S(1)}, bf16[1,2,2,16,768]{4,3,2,1,0:T(8,128)(2,1)S(1)}, u32[]{:S(2)}, u32[]{:S(2)}) collective-permute-start(bf16[1,2,2,16,768]{4,3,2,1,0:T(8,128)(2,1)S(1)} %get-tuple-element.53), channel_id=1, source_target_pairs={{0,10},{1,11},{2,8},{3,9},{4,14},{5,15},{6,12},{7,13},{8,2},{9,3},... | collective-permute-start | bytes 294920 | tf_op jit(solution)/shard_map/ppermute | solution.py:241
  42.1 1.4 %collective-permute-start.14 = (bf16[1,2,2,16,768]{4,3,2,1,0:T(8,128)(2,1)S(1)}, bf16[1,2,2,16,768]{4,3,2,1,0:T(8,128)(2,1)S(1)}, u32[]{:S(2)}, u32[]{:S(2)}) collective-permute-start(bf16[1,2,2,16,768]{4,3,2,1,0:T(8,128)(2,1)S(1)} %get-tuple-element.54), channel_id=1, source_target_pairs={{0,12},{1,13},{2,14},{3,15},{4,8},{5,9},{6,10},{7,11},{8,4},{9,5},... | collective-permute-start | bytes 294920 | tf_op jit(solution)/shard_map/ppermute | solution.py:241
  43.5 6.0 %collective-permute-done.12 = bf16[1,2,2,16,768]{4,3,2,1,0:T(8,128)(2,1)S(1)} collective-permute-done((bf16[1,2,2,16,768]{4,3,2,1,0:T(8,128)(2,1)S(1)}, bf16[1,2,2,16,768]{4,3,2,1,0:T(8,128)(2,1)S(1)}, u32[]{:S(2)}, u32[]{:S(2)}) %collective-permute-start.12) | collective-permute-done | bytes 98336 | tf_op jit(solution)/shard_map/ppermute | solution.py:241
  49.5 2.3 %collective-permute-done.13 = bf16[1,2,2,16,768]{4,3,2,1,0:T(8,128)(2,1)S(1)} collective-permute-done((bf16[1,2,2,16,768]{4,3,2,1,0:T(8,128)(2,1)S(1)}, bf16[1,2,2,16,768]{4,3,2,1,0:T(8,128)(2,1)S(1)}, u32[]{:S(2)}, u32[]{:S(2)}) %collective-permute-start.13) | collective-permute-done | bytes 98336 | tf_op jit(solution)/shard_map/ppermute | solution.py:241
  51.9 6.4 %shard_map.148 = (bf16[16,2,16,768]{3,2,1,0:T(8,128)(2,1)S(1)}, bf16[16,2,16,768]{3,2,1,0:T(8,128)(2,1)S(1)}) custom-call(s32[1]{0:T(128)} %bitcast.me_ref, bf16[16,2,16,768]{3,2,1,0:T(8,128)(2,1)S(1)} %bitcast.19, bf16[16,2,16,768]{3,2,1,0:T(8,128)(2,1)S(1)} %bitcast.20, bf16[16,256,64]{2,1,0:T(8,128)(2,1)S(1)} %get-tuple-element.19.refs_2_, ...), custom_call_target="tpu_custom_call" | custom-call | flops 9663676416 | tf_op jit(solution)/shard_map/pallas_call | solution.py:147
  60.3 2.7 %collective-permute-start.31 = (bf16[1,2,2,16,768]{4,3,2,1,0:T(8,128)(2,1)S(1)}, bf16[1,2,2,16,768]{4,3,2,1,0:T(8,128)(2,1)S(1)}, u32[]{:S(2)}, u32[]{:S(2)}) collective-permute-start(bf16[1,2,2,16,768]{4,3,2,1,0:T(8,128)(2,1)S(1)} %get-tuple-element.27), channel_id=1, source_target_pairs={{0,14},{1,15},{2,12},{3,13},{4,10},{5,11},{6,8},{7,9},{8,6},{9,7},... | collective-permute-start | bytes 294920 | tf_op jit(solution)/shard_map/ppermute | solution.py:241
  64.2 2.2 %collective-permute-start.27 = (bf16[1,2,2,16,768]{4,3,2,1,0:T(8,128)(2,1)S(1)}, bf16[1,2,2,16,768]{4,3,2,1,0:T(8,128)(2,1)S(1)}, u32[]{:S(2)}, u32[]{:S(2)}) collective-permute-start(bf16[1,2,2,16,768]{4,3,2,1,0:T(8,128)(2,1)S(1)} %get-tuple-element.31), channel_id=1, source_target_pairs={{0,6},{1,7},{2,4},{3,5},{4,2},{5,3},{6,0},{7,1},{8,14},{9,15},{10,... | collective-permute-start | bytes 294920 | tf_op jit(solution)/shard_map/ppermute | solution.py:241
  66.9 2.7 %collective-permute-done.25 = bf16[1,2,2,16,768]{4,3,2,1,0:T(8,128)(2,1)S(1)} collective-permute-done((bf16[1,2,2,16,768]{4,3,2,1,0:T(8,128)(2,1)S(1)}, bf16[1,2,2,16,768]{4,3,2,1,0:T(8,128)(2,1)S(1)}, u32[]{:S(2)}, u32[]{:S(2)}) %collective-permute-start.25) | collective-permute-done | bytes 98336 | tf_op jit(solution)/shard_map/ppermute | solution.py:241
  70.9 3.3 %collective-permute-start.30 = (bf16[1,2,2,16,768]{4,3,2,1,0:T(8,128)(2,1)S(1)}, bf16[1,2,2,16,768]{4,3,2,1,0:T(8,128)(2,1)S(1)}, u32[]{:S(2)}, u32[]{:S(2)}) collective-permute-start(bf16[1,2,2,16,768]{4,3,2,1,0:T(8,128)(2,1)S(1)} %get-tuple-element.34), channel_id=1, source_target_pairs={{0,12},{1,13},{2,14},{3,15},{4,8},{5,9},{6,10},{7,11},{8,4},{9,5},... | collective-permute-start | bytes 294920 | tf_op jit(solution)/shard_map/ppermute | solution.py:241
  74.3 3.1 %collective-permute-start.23 = (bf16[1,2,2,16,768]{4,3,2,1,0:T(8,128)(2,1)S(1)}, bf16[1,2,2,16,768]{4,3,2,1,0:T(8,128)(2,1)S(1)}, u32[]{:S(2)}, u32[]{:S(2)}) collective-permute-start(bf16[1,2,2,16,768]{4,3,2,1,0:T(8,128)(2,1)S(1)} %get-tuple-element.37), channel_id=1, source_target_pairs={{0,14},{1,15},{2,12},{3,13},{4,10},{5,11},{6,8},{7,9},{8,6},{9,7},... | collective-permute-start | bytes 294920 | tf_op jit(solution)/shard_map/ppermute | solution.py:241
  78.4 4.5 %collective-permute-done.29 = bf16[1,2,2,16,768]{4,3,2,1,0:T(8,128)(2,1)S(1)} collective-permute-done((bf16[1,2,2,16,768]{4,3,2,1,0:T(8,128)(2,1)S(1)}, bf16[1,2,2,16,768]{4,3,2,1,0:T(8,128)(2,1)S(1)}, u32[]{:S(2)}, u32[]{:S(2)}) %collective-permute-start.29) | collective-permute-done | bytes 98336 | tf_op jit(solution)/shard_map/ppermute | solution.py:241
  82.9 3.5 %collective-permute-start.21 = (bf16[1,2,2,16,768]{4,3,2,1,0:T(8,128)(2,1)S(1)}, bf16[1,2,2,16,768]{4,3,2,1,0:T(8,128)(2,1)S(1)}, u32[]{:S(2)}, u32[]{:S(2)}) collective-permute-start(bf16[1,2,2,16,768]{4,3,2,1,0:T(8,128)(2,1)S(1)} %get-tuple-element.43), channel_id=1, source_target_pairs={{0,10},{1,11},{2,8},{3,9},{4,14},{5,15},{6,12},{7,13},{8,2},{9,3},... | collective-permute-start | bytes 294920 | tf_op jit(solution)/shard_map/ppermute | solution.py:241
  86.4 1.6 %collective-permute-start.22 = (bf16[1,2,2,16,768]{4,3,2,1,0:T(8,128)(2,1)S(1)}, bf16[1,2,2,16,768]{4,3,2,1,0:T(8,128)(2,1)S(1)}, u32[]{:S(2)}, u32[]{:S(2)}) collective-permute-start(bf16[1,2,2,16,768]{4,3,2,1,0:T(8,128)(2,1)S(1)} %get-tuple-element.44), channel_id=1, source_target_pairs={{0,12},{1,13},{2,14},{3,15},{4,8},{5,9},{6,10},{7,11},{8,4},{9,5},... | collective-permute-start | bytes 294920 | tf_op jit(solution)/shard_map/ppermute | solution.py:241
  88.1 7.0 %collective-permute-done.21 = bf16[1,2,2,16,768]{4,3,2,1,0:T(8,128)(2,1)S(1)} collective-permute-done((bf16[1,2,2,16,768]{4,3,2,1,0:T(8,128)(2,1)S(1)}, bf16[1,2,2,16,768]{4,3,2,1,0:T(8,128)(2,1)S(1)}, u32[]{:S(2)}, u32[]{:S(2)}) %collective-permute-start.21) | collective-permute-done | bytes 98336 | tf_op jit(solution)/shard_map/ppermute | solution.py:241
  95.1 8.5 %shard_map.149.rest_0_ = bf16[4,1440,384]{2,1,0:T(8,128)(2,1)} custom-call(s32[1]{0:T(128)} %bitcast.me_ref, bf16[16,2,16,768]{3,2,1,0:T(8,128)(2,1)S(1)} %bitcast.18, bf16[2,1440,384]{2,1,0:T(8,128)(2,1)S(1)} %get-tuple-element.26.normed_ref, bf16[4,1440,384]{2,1,0:T(8,128)(2,1)S(1)} %bitcast.22, bf16[1440,512]{1,0:T(8,128)(2,1)S(1)} %copy-done.7, ...), custom_call_target="tpu_custom_call" | custom-call | flops 18119393280 | tf_op jit(solution)/shard_map/pallas_call | solution.py:220
  103.8 8.3 %shard_map.150 = bf16[4,1440,384]{2,1,0:T(8,128)(2,1)} custom-call(s32[1]{0:T(128)} %bitcast.me_ref, bf16[16,2,16,768]{3,2,1,0:T(8,128)(2,1)S(1)} %bitcast.17, bf16[2,1440,384]{2,1,0:T(8,128)(2,1)S(1)} %get-tuple-element.23.normed_ref, bf16[4,1440,384]{2,1,0:T(8,128)(2,1)S(1)} %bitcast.22, ...), custom_call_target="tpu_custom_call", output_to_operand_aliasing={{}: (9, {})} | custom-call | flops 18119393280 | tf_op jit(solution)/shard_map/pallas_call | solution.py:220
  (112 shorter events, 11.1 us)
Async XLA Ops:
  7.2 25.5 %collective-permute-start.7 = (bf16[1,2,2,16,768]{4,3,2,1,0:T(8,128)(2,1)S(1)}, bf16[1,2,2,16,768]{4,3,2,1,0:T(8,128)(2,1)S(1)}, u32[]{:S(2)}, u32[]{:S(2)}) collective-permute-start(bf16[1,2,2,16,768]{4,3,2,1,0:T(8,128)(2,1)S(1)} %get-tuple-element.57), channel_id=1, source_target_pairs={{0,14},{1,15},{2,12},{3,13},{4,10},{5,11},{6,8},{7,9},{8,6},{9,7},... | collective-permute-start | bytes 294920 | tf_op jit(solution)/shard_map/ppermute | solution.py:241
  13.2 8.0 %collective-permute-start.1 = (bf16[1,2,2,16,768]{4,3,2,1,0:T(8,128)(2,1)S(1)}, bf16[1,2,2,16,768]{4,3,2,1,0:T(8,128)(2,1)S(1)}, u32[]{:S(2)}, u32[]{:S(2)}) collective-permute-start(bf16[1,2,2,16,768]{4,3,2,1,0:T(8,128)(2,1)S(1)} %get-tuple-element.59), channel_id=1, source_target_pairs={{0,2},{1,3},{2,0},{3,1},{4,6},{5,7},{6,4},{7,5},{8,10},{9,11},{10,... | collective-permute-start | bytes 294920 | tf_op jit(solution)/shard_map/ppermute | solution.py:241
  13.7 10.4 %collective-permute-start.2 = (bf16[1,2,2,16,768]{4,3,2,1,0:T(8,128)(2,1)S(1)}, bf16[1,2,2,16,768]{4,3,2,1,0:T(8,128)(2,1)S(1)}, u32[]{:S(2)}, u32[]{:S(2)}) collective-permute-start(bf16[1,2,2,16,768]{4,3,2,1,0:T(8,128)(2,1)S(1)} %get-tuple-element.60), channel_id=1, source_target_pairs={{0,4},{1,5},{2,6},{3,7},{4,0},{5,1},{6,2},{7,3},{8,12},{9,13},{10,... | collective-permute-start | bytes 294920 | tf_op jit(solution)/shard_map/ppermute | solution.py:241
  13.7 10.6 %collective-permute-start.3 = (bf16[1,2,2,16,768]{4,3,2,1,0:T(8,128)(2,1)S(1)}, bf16[1,2,2,16,768]{4,3,2,1,0:T(8,128)(2,1)S(1)}, u32[]{:S(2)}, u32[]{:S(2)}) collective-permute-start(bf16[1,2,2,16,768]{4,3,2,1,0:T(8,128)(2,1)S(1)} %get-tuple-element.61), channel_id=1, source_target_pairs={{0,6},{1,7},{2,4},{3,5},{4,2},{5,3},{6,0},{7,1},{8,14},{9,15},{10,... | collective-permute-start | bytes 294920 | tf_op jit(solution)/shard_map/ppermute | solution.py:241
  16.7 7.8 %collective-permute-start.4 = (bf16[1,2,2,16,768]{4,3,2,1,0:T(8,128)(2,1)S(1)}, bf16[1,2,2,16,768]{4,3,2,1,0:T(8,128)(2,1)S(1)}, u32[]{:S(2)}, u32[]{:S(2)}) collective-permute-start(bf16[1,2,2,16,768]{4,3,2,1,0:T(8,128)(2,1)S(1)} %get-tuple-element.62), channel_id=1, source_target_pairs={{0,8},{1,9},{2,10},{3,11},{4,12},{5,13},{6,14},{7,15},{8,0},{9,1},... | collective-permute-start | bytes 294920 | tf_op jit(solution)/shard_map/ppermute | solution.py:241
  21.2 10.8 %collective-permute-start.5 = (bf16[1,2,2,16,768]{4,3,2,1,0:T(8,128)(2,1)S(1)}, bf16[1,2,2,16,768]{4,3,2,1,0:T(8,128)(2,1)S(1)}, u32[]{:S(2)}, u32[]{:S(2)}) collective-permute-start(bf16[1,2,2,16,768]{4,3,2,1,0:T(8,128)(2,1)S(1)} %get-tuple-element.63), channel_id=1, source_target_pairs={{0,10},{1,11},{2,8},{3,9},{4,14},{5,15},{6,12},{7,13},{8,2},{9,3},... | collective-permute-start | bytes 294920 | tf_op jit(solution)/shard_map/ppermute | solution.py:241
  24.2 7.8 %collective-permute-start.6 = (bf16[1,2,2,16,768]{4,3,2,1,0:T(8,128)(2,1)S(1)}, bf16[1,2,2,16,768]{4,3,2,1,0:T(8,128)(2,1)S(1)}, u32[]{:S(2)}, u32[]{:S(2)}) collective-permute-start(bf16[1,2,2,16,768]{4,3,2,1,0:T(8,128)(2,1)S(1)} %get-tuple-element.64), channel_id=1, source_target_pairs={{0,12},{1,13},{2,14},{3,15},{4,8},{5,9},{6,10},{7,11},{8,4},{9,5},... | collective-permute-start | bytes 294920 | tf_op jit(solution)/shard_map/ppermute | solution.py:241
  32.7 19.1 %collective-permute-start.15 = (bf16[1,2,2,16,768]{4,3,2,1,0:T(8,128)(2,1)S(1)}, bf16[1,2,2,16,768]{4,3,2,1,0:T(8,128)(2,1)S(1)}, u32[]{:S(2)}, u32[]{:S(2)}) collective-permute-start(bf16[1,2,2,16,768]{4,3,2,1,0:T(8,128)(2,1)S(1)} %get-tuple-element.47), channel_id=1, source_target_pairs={{0,14},{1,15},{2,12},{3,13},{4,10},{5,11},{6,8},{7,9},{8,6},{9,7},... | collective-permute-start | bytes 294920 | tf_op jit(solution)/shard_map/ppermute | solution.py:241
  38.3 11.1 %collective-permute-start.12 = (bf16[1,2,2,16,768]{4,3,2,1,0:T(8,128)(2,1)S(1)}, bf16[1,2,2,16,768]{4,3,2,1,0:T(8,128)(2,1)S(1)}, u32[]{:S(2)}, u32[]{:S(2)}) collective-permute-start(bf16[1,2,2,16,768]{4,3,2,1,0:T(8,128)(2,1)S(1)} %get-tuple-element.52), channel_id=1, source_target_pairs={{0,8},{1,9},{2,10},{3,11},{4,12},{5,13},{6,14},{7,15},{8,0},{9,1},... | collective-permute-start | bytes 294920 | tf_op jit(solution)/shard_map/ppermute | solution.py:241
  38.8 13.0 %collective-permute-start.13 = (bf16[1,2,2,16,768]{4,3,2,1,0:T(8,128)(2,1)S(1)}, bf16[1,2,2,16,768]{4,3,2,1,0:T(8,128)(2,1)S(1)}, u32[]{:S(2)}, u32[]{:S(2)}) collective-permute-start(bf16[1,2,2,16,768]{4,3,2,1,0:T(8,128)(2,1)S(1)} %get-tuple-element.53), channel_id=1, source_target_pairs={{0,10},{1,11},{2,8},{3,9},{4,14},{5,15},{6,12},{7,13},{8,2},{9,3},... | collective-permute-start | bytes 294920 | tf_op jit(solution)/shard_map/ppermute | solution.py:241
  42.1 9.7 %collective-permute-start.14 = (bf16[1,2,2,16,768]{4,3,2,1,0:T(8,128)(2,1)S(1)}, bf16[1,2,2,16,768]{4,3,2,1,0:T(8,128)(2,1)S(1)}, u32[]{:S(2)}, u32[]{:S(2)}) collective-permute-start(bf16[1,2,2,16,768]{4,3,2,1,0:T(8,128)(2,1)S(1)} %get-tuple-element.54), channel_id=1, source_target_pairs={{0,12},{1,13},{2,14},{3,15},{4,8},{5,9},{6,10},{7,11},{8,4},{9,5},... | collective-permute-start | bytes 294920 | tf_op jit(solution)/shard_map/ppermute | solution.py:241
  58.5 7.9 %collective-permute-start.16 = (bf16[8,1,2,16,768]{4,3,2,1,0:T(8,128)(2,1)S(1)}, bf16[8,1,2,16,768]{4,3,2,1,0:T(8,128)(2,1)S(1)}, u32[]{:S(2)}, u32[]{:S(2)}) collective-permute-start(bf16[8,1,2,16,768]{4,3,2,1,0:T(8,128)(2,1)S(1)} %get-tuple-element.46), channel_id=1, source_target_pairs={{0,1},{1,0},{2,3},{3,2},{4,5},{5,4},{6,7},{7,6},{8,9},{9,8},{10,11... | collective-permute-start | bytes 1179656 | tf_op jit(solution)/shard_map/ppermute | solution.py:241
  60.3 26.1 %collective-permute-start.31 = (bf16[1,2,2,16,768]{4,3,2,1,0:T(8,128)(2,1)S(1)}, bf16[1,2,2,16,768]{4,3,2,1,0:T(8,128)(2,1)S(1)}, u32[]{:S(2)}, u32[]{:S(2)}) collective-permute-start(bf16[1,2,2,16,768]{4,3,2,1,0:T(8,128)(2,1)S(1)} %get-tuple-element.27), channel_id=1, source_target_pairs={{0,14},{1,15},{2,12},{3,13},{4,10},{5,11},{6,8},{7,9},{8,6},{9,7},... | collective-permute-start | bytes 294920 | tf_op jit(solution)/shard_map/ppermute | solution.py:241
  64.2 10.0 %collective-permute-start.27 = (bf16[1,2,2,16,768]{4,3,2,1,0:T(8,128)(2,1)S(1)}, bf16[1,2,2,16,768]{4,3,2,1,0:T(8,128)(2,1)S(1)}, u32[]{:S(2)}, u32[]{:S(2)}) collective-permute-start(bf16[1,2,2,16,768]{4,3,2,1,0:T(8,128)(2,1)S(1)} %get-tuple-element.31), channel_id=1, source_target_pairs={{0,6},{1,7},{2,4},{3,5},{4,2},{5,3},{6,0},{7,1},{8,14},{9,15},{10,... | collective-permute-start | bytes 294920 | tf_op jit(solution)/shard_map/ppermute | solution.py:241
  66.4 11.9 %collective-permute-start.28 = (bf16[1,2,2,16,768]{4,3,2,1,0:T(8,128)(2,1)S(1)}, bf16[1,2,2,16,768]{4,3,2,1,0:T(8,128)(2,1)S(1)}, u32[]{:S(2)}, u32[]{:S(2)}) collective-permute-start(bf16[1,2,2,16,768]{4,3,2,1,0:T(8,128)(2,1)S(1)} %get-tuple-element.32), channel_id=1, source_target_pairs={{0,8},{1,9},{2,10},{3,11},{4,12},{5,13},{6,14},{7,15},{8,0},{9,1},... | collective-permute-start | bytes 294920 | tf_op jit(solution)/shard_map/ppermute | solution.py:241
  69.6 13.2 %collective-permute-start.29 = (bf16[1,2,2,16,768]{4,3,2,1,0:T(8,128)(2,1)S(1)}, bf16[1,2,2,16,768]{4,3,2,1,0:T(8,128)(2,1)S(1)}, u32[]{:S(2)}, u32[]{:S(2)}) collective-permute-start(bf16[1,2,2,16,768]{4,3,2,1,0:T(8,128)(2,1)S(1)} %get-tuple-element.33), channel_id=1, source_target_pairs={{0,10},{1,11},{2,8},{3,9},{4,14},{5,15},{6,12},{7,13},{8,2},{9,3},... | collective-permute-start | bytes 294920 | tf_op jit(solution)/shard_map/ppermute | solution.py:241
  70.9 11.9 %collective-permute-start.30 = (bf16[1,2,2,16,768]{4,3,2,1,0:T(8,128)(2,1)S(1)}, bf16[1,2,2,16,768]{4,3,2,1,0:T(8,128)(2,1)S(1)}, u32[]{:S(2)}, u32[]{:S(2)}) collective-permute-start(bf16[1,2,2,16,768]{4,3,2,1,0:T(8,128)(2,1)S(1)} %get-tuple-element.34), channel_id=1, source_target_pairs={{0,12},{1,13},{2,14},{3,15},{4,8},{5,9},{6,10},{7,11},{8,4},{9,5},... | collective-permute-start | bytes 294920 | tf_op jit(solution)/shard_map/ppermute | solution.py:241
  74.3 13.7 %collective-permute-start.23 = (bf16[1,2,2,16,768]{4,3,2,1,0:T(8,128)(2,1)S(1)}, bf16[1,2,2,16,768]{4,3,2,1,0:T(8,128)(2,1)S(1)}, u32[]{:S(2)}, u32[]{:S(2)}) collective-permute-start(bf16[1,2,2,16,768]{4,3,2,1,0:T(8,128)(2,1)S(1)} %get-tuple-element.37), channel_id=1, source_target_pairs={{0,14},{1,15},{2,12},{3,13},{4,10},{5,11},{6,8},{7,9},{8,6},{9,7},... | collective-permute-start | bytes 294920 | tf_op jit(solution)/shard_map/ppermute | solution.py:241
  78.3 25.3 %collective-permute-start.17 = (bf16[1,2,2,16,768]{4,3,2,1,0:T(8,128)(2,1)S(1)}, bf16[1,2,2,16,768]{4,3,2,1,0:T(8,128)(2,1)S(1)}, u32[]{:S(2)}, u32[]{:S(2)}) collective-permute-start(bf16[1,2,2,16,768]{4,3,2,1,0:T(8,128)(2,1)S(1)} %get-tuple-element.39), channel_id=1, source_target_pairs={{0,2},{1,3},{2,0},{3,1},{4,6},{5,7},{6,4},{7,5},{8,10},{9,11},{10,... | collective-permute-start | bytes 294920 | tf_op jit(solution)/shard_map/ppermute | solution.py:241
  82.8 20.8 %collective-permute-start.18 = (bf16[1,2,2,16,768]{4,3,2,1,0:T(8,128)(2,1)S(1)}, bf16[1,2,2,16,768]{4,3,2,1,0:T(8,128)(2,1)S(1)}, u32[]{:S(2)}, u32[]{:S(2)}) collective-permute-start(bf16[1,2,2,16,768]{4,3,2,1,0:T(8,128)(2,1)S(1)} %get-tuple-element.40), channel_id=1, source_target_pairs={{0,4},{1,5},{2,6},{3,7},{4,0},{5,1},{6,2},{7,3},{8,12},{9,13},{10,... | collective-permute-start | bytes 294920 | tf_op jit(solution)/shard_map/ppermute | solution.py:241
  82.9 12.2 %collective-permute-start.21 = (bf16[1,2,2,16,768]{4,3,2,1,0:T(8,128)(2,1)S(1)}, bf16[1,2,2,16,768]{4,3,2,1,0:T(8,128)(2,1)S(1)}, u32[]{:S(2)}, u32[]{:S(2)}) collective-permute-start(bf16[1,2,2,16,768]{4,3,2,1,0:T(8,128)(2,1)S(1)} %get-tuple-element.43), channel_id=1, source_target_pairs={{0,10},{1,11},{2,8},{3,9},{4,14},{5,15},{6,12},{7,13},{8,2},{9,3},... | collective-permute-start | bytes 294920 | tf_op jit(solution)/shard_map/ppermute | solution.py:241
  86.4 8.7 %collective-permute-start.22 = (bf16[1,2,2,16,768]{4,3,2,1,0:T(8,128)(2,1)S(1)}, bf16[1,2,2,16,768]{4,3,2,1,0:T(8,128)(2,1)S(1)}, u32[]{:S(2)}, u32[]{:S(2)}) collective-permute-start(bf16[1,2,2,16,768]{4,3,2,1,0:T(8,128)(2,1)S(1)} %get-tuple-element.44), channel_id=1, source_target_pairs={{0,12},{1,13},{2,14},{3,15},{4,8},{5,9},{6,10},{7,11},{8,4},{9,5},... | collective-permute-start | bytes 294920 | tf_op jit(solution)/shard_map/ppermute | solution.py:241
  88.0 15.7 %collective-permute-start.19 = (bf16[1,2,2,16,768]{4,3,2,1,0:T(8,128)(2,1)S(1)}, bf16[1,2,2,16,768]{4,3,2,1,0:T(8,128)(2,1)S(1)}, u32[]{:S(2)}, u32[]{:S(2)}) collective-permute-start(bf16[1,2,2,16,768]{4,3,2,1,0:T(8,128)(2,1)S(1)} %get-tuple-element.41), channel_id=1, source_target_pairs={{0,6},{1,7},{2,4},{3,5},{4,2},{5,3},{6,0},{7,1},{8,14},{9,15},{10,... | collective-permute-start | bytes 294920 | tf_op jit(solution)/shard_map/ppermute | solution.py:241
  95.1 8.6 %collective-permute-start.20 = (bf16[1,2,2,16,768]{4,3,2,1,0:T(8,128)(2,1)S(1)}, bf16[1,2,2,16,768]{4,3,2,1,0:T(8,128)(2,1)S(1)}, u32[]{:S(2)}, u32[]{:S(2)}) collective-permute-start(bf16[1,2,2,16,768]{4,3,2,1,0:T(8,128)(2,1)S(1)} %get-tuple-element.42), channel_id=1, source_target_pairs={{0,8},{1,9},{2,10},{3,11},{4,12},{5,13},{6,14},{7,15},{8,0},{9,1},... | collective-permute-start | bytes 294920 | tf_op jit(solution)/shard_map/ppermute | solution.py:241
  (21 other events, 328.0 us)

commit v3 on v2

--- a/solution.py
+++ b/solution.py
@@ -255,7 +255,7 @@
 def swap_far(blocks, devices):
     count = blocks.shape[0]
     parts = [blocks[:1]] + [None] * (count - 1)
-    for k in range(count - 1, 0, -1):
+    for k in (6, 1, 5, 2, 4, 3, 7):
         parts[k] = swap(blocks[k : k + 1], k * NEAR, devices)
     return parts
 
@@ -311,7 +311,7 @@
     back = middle(me, [joined(parts_a), joined(parts_b)], fwd, inv, degree_gain, weight)
     parts_c = swap_far(swap_near(back[0], devices), devices)
     parts_d = swap_far(swap_near(back[1], devices), devices)
-    result = give(0, after(joined(parts_c), parts_d[len(parts_d) - 3 :]), None)
+    result = give(0, after(joined(parts_c), [parts_d[k] for k in (1,7,)]), None)
     return give(1, joined(parts_d), result)
 
 

time: 112 us -> 109 us (0.973)
  waiting for transfers between devices: 33.2 us -> 26.6 us
  starting transfers between devices: 44.3 us -> 47.4 us
    ppermute x32, waiting for transfers between devices: 33.2 us -> 26.6 us  [swap(): return lax.ppermute(part, 'lat', [(a, a ^ offset) for a in range(devices)])]
    ppermute x32, starting transfers between devices: 44.3 us -> 47.4 us  [swap(): return lax.ppermute(part, 'lat', [(a, a ^ offset) for a in range(devices)])]
where the time goes in v3:
time: 109 us
  starting transfers between devices  47.4 us (43%)
  Pallas kernels  32.7 us (30%)
  waiting for transfers between devices  26.6 us (24%)
  local copies, waits for them, and re-layouts  1.19 us (1%)
    ppermute x32, starting transfers between devices, swap(): return lax.ppermute(part, 'lat', [(a, a ^ offset) for a in range(devices)])  47.4 us
    ppermute x32, waiting for transfers between devices, swap(): return lax.ppermute(part, 'lat', [(a, a ^ offset) for a in range(devices)])  26.6 us
    pallas_call x2, Pallas kernels, finish(): pl.pallas_call(finish_kernel, grid=(rows,), in_specs=specs, out_specs=pla...  16.8 us
    pallas_call x2, Pallas kernels, analyse(): pl.pallas_call(analyse_kernel, grid=(rows,), in_specs=[pl.BlockSpec(memor...  8.93 us
    pallas_call x1, Pallas kernels, middle(): pl.pallas_call(functools.partial(middle_kernel, chunks=len(arrived)), in_...  6.43 us
  transfers between devices with their start and end apart: 32, of which 11 were waited for; matrix products, arithmetic and copies ran while one was open for 0% of the time, Pallas kernels for 12%

profile of v3, /device:TPU:0, one launch (start us, length us, event | category | flops | bytes accessed | tf_op | source)
XLA Modules:
  0.0 108.6 jit_solution(6987101712901224737)
XLA Ops:
  0.7 4.5 %shard_map.145 = (bf16[16,2,16,768]{3,2,1,0:T(8,128)(2,1)S(1)}, bf16[2,1440,384]{2,1,0:T(8,128)(2,1)S(1)}) custom-call(s32[1]{0:T(128)} %bitcast.me_ref, bf16[4,1440,384]{2,1,0:T(8,128)(2,1)} %field_ref.7, f32[1,384]{1,0:T(1,128)S(1)} %reshape.40.gain_ref, bf16[512,1440]{1,0:T(8,128)(2,1)} %constant.12.clone.table_ref), custom_call_target="tpu_custom_call" | custom-call | flops 4529848320 | tf_op jit(solution)/shard_map/pallas_call | solution.py:64
  7.2 6.0 %collective-permute-start.7 = (bf16[1,2,2,16,768]{4,3,2,1,0:T(8,128)(2,1)S(1)}, bf16[1,2,2,16,768]{4,3,2,1,0:T(8,128)(2,1)S(1)}, u32[]{:S(2)}, u32[]{:S(2)}) collective-permute-start(bf16[1,2,2,16,768]{4,3,2,1,0:T(8,128)(2,1)S(1)} %get-tuple-element.57), channel_id=1, source_target_pairs={{0,14},{1,15},{2,12},{3,13},{4,10},{5,11},{6,8},{7,9},{8,6},{9,7},... | collective-permute-start | bytes 294920 | tf_op jit(solution)/shard_map/ppermute | solution.py:241
  13.7 3.0 %collective-permute-start.3 = (bf16[1,2,2,16,768]{4,3,2,1,0:T(8,128)(2,1)S(1)}, bf16[1,2,2,16,768]{4,3,2,1,0:T(8,128)(2,1)S(1)}, u32[]{:S(2)}, u32[]{:S(2)}) collective-permute-start(bf16[1,2,2,16,768]{4,3,2,1,0:T(8,128)(2,1)S(1)} %get-tuple-element.61), channel_id=1, source_target_pairs={{0,6},{1,7},{2,4},{3,5},{4,2},{5,3},{6,0},{7,1},{8,14},{9,15},{10,... | collective-permute-start | bytes 294920 | tf_op jit(solution)/shard_map/ppermute | solution.py:241
  16.7 4.4 %shard_map.146 = (bf16[16,2,16,768]{3,2,1,0:T(8,128)(2,1)S(1)}, bf16[2,1440,384]{2,1,0:T(8,128)(2,1)S(1)}) custom-call(s32[1]{0:T(128)} %bitcast.me_ref, bf16[4,1440,384]{2,1,0:T(8,128)(2,1)} %field_ref.7, f32[1,384]{1,0:T(1,128)S(1)} %reshape.40.gain_ref, bf16[512,1440]{1,0:T(8,128)(2,1)} %constant.12.clone.table_ref), custom_call_target="tpu_custom_call" | custom-call | flops 4529848320 | tf_op jit(solution)/shard_map/pallas_call | solution.py:64
  21.2 3.0 %collective-permute-start.5 = (bf16[1,2,2,16,768]{4,3,2,1,0:T(8,128)(2,1)S(1)}, bf16[1,2,2,16,768]{4,3,2,1,0:T(8,128)(2,1)S(1)}, u32[]{:S(2)}, u32[]{:S(2)}) collective-permute-start(bf16[1,2,2,16,768]{4,3,2,1,0:T(8,128)(2,1)S(1)} %get-tuple-element.63), channel_id=1, source_target_pairs={{0,10},{1,11},{2,8},{3,9},{4,14},{5,15},{6,12},{7,13},{8,2},{9,3},... | collective-permute-start | bytes 294920 | tf_op jit(solution)/shard_map/ppermute | solution.py:241
  24.5 7.5 %collective-permute-done.5 = bf16[1,2,2,16,768]{4,3,2,1,0:T(8,128)(2,1)S(1)} collective-permute-done((bf16[1,2,2,16,768]{4,3,2,1,0:T(8,128)(2,1)S(1)}, bf16[1,2,2,16,768]{4,3,2,1,0:T(8,128)(2,1)S(1)}, u32[]{:S(2)}, u32[]{:S(2)}) %collective-permute-start.5) | collective-permute-done | bytes 98336 | tf_op jit(solution)/shard_map/ppermute | solution.py:241
  32.7 3.5 %collective-permute-start.15 = (bf16[1,2,2,16,768]{4,3,2,1,0:T(8,128)(2,1)S(1)}, bf16[1,2,2,16,768]{4,3,2,1,0:T(8,128)(2,1)S(1)}, u32[]{:S(2)}, u32[]{:S(2)}) collective-permute-start(bf16[1,2,2,16,768]{4,3,2,1,0:T(8,128)(2,1)S(1)} %get-tuple-element.47), channel_id=1, source_target_pairs={{0,14},{1,15},{2,12},{3,13},{4,10},{5,11},{6,8},{7,9},{8,6},{9,7},... | collective-permute-start | bytes 294920 | tf_op jit(solution)/shard_map/ppermute | solution.py:241
  36.2 2.1 %collective-permute-start.11 = (bf16[1,2,2,16,768]{4,3,2,1,0:T(8,128)(2,1)S(1)}, bf16[1,2,2,16,768]{4,3,2,1,0:T(8,128)(2,1)S(1)}, u32[]{:S(2)}, u32[]{:S(2)}) collective-permute-start(bf16[1,2,2,16,768]{4,3,2,1,0:T(8,128)(2,1)S(1)} %get-tuple-element.51), channel_id=1, source_target_pairs={{0,6},{1,7},{2,4},{3,5},{4,2},{5,3},{6,0},{7,1},{8,14},{9,15},{10,... | collective-permute-start | bytes 294920 | tf_op jit(solution)/shard_map/ppermute | solution.py:241
  38.8 3.3 %collective-permute-start.13 = (bf16[1,2,2,16,768]{4,3,2,1,0:T(8,128)(2,1)S(1)}, bf16[1,2,2,16,768]{4,3,2,1,0:T(8,128)(2,1)S(1)}, u32[]{:S(2)}, u32[]{:S(2)}) collective-permute-start(bf16[1,2,2,16,768]{4,3,2,1,0:T(8,128)(2,1)S(1)} %get-tuple-element.53), channel_id=1, source_target_pairs={{0,10},{1,11},{2,8},{3,9},{4,14},{5,15},{6,12},{7,13},{8,2},{9,3},... | collective-permute-start | bytes 294920 | tf_op jit(solution)/shard_map/ppermute | solution.py:241
  42.1 1.4 %collective-permute-start.14 = (bf16[1,2,2,16,768]{4,3,2,1,0:T(8,128)(2,1)S(1)}, bf16[1,2,2,16,768]{4,3,2,1,0:T(8,128)(2,1)S(1)}, u32[]{:S(2)}, u32[]{:S(2)}) collective-permute-start(bf16[1,2,2,16,768]{4,3,2,1,0:T(8,128)(2,1)S(1)} %get-tuple-element.54), channel_id=1, source_target_pairs={{0,12},{1,13},{2,14},{3,15},{4,8},{5,9},{6,10},{7,11},{8,4},{9,5},... | collective-permute-start | bytes 294920 | tf_op jit(solution)/shard_map/ppermute | solution.py:241
  43.5 6.0 %collective-permute-done.12 = bf16[1,2,2,16,768]{4,3,2,1,0:T(8,128)(2,1)S(1)} collective-permute-done((bf16[1,2,2,16,768]{4,3,2,1,0:T(8,128)(2,1)S(1)}, bf16[1,2,2,16,768]{4,3,2,1,0:T(8,128)(2,1)S(1)}, u32[]{:S(2)}, u32[]{:S(2)}) %collective-permute-start.12) | collective-permute-done | bytes 98336 | tf_op jit(solution)/shard_map/ppermute | solution.py:241
  49.5 2.3 %collective-permute-done.13 = bf16[1,2,2,16,768]{4,3,2,1,0:T(8,128)(2,1)S(1)} collective-permute-done((bf16[1,2,2,16,768]{4,3,2,1,0:T(8,128)(2,1)S(1)}, bf16[1,2,2,16,768]{4,3,2,1,0:T(8,128)(2,1)S(1)}, u32[]{:S(2)}, u32[]{:S(2)}) %collective-permute-start.13) | collective-permute-done | bytes 98336 | tf_op jit(solution)/shard_map/ppermute | solution.py:241
  51.9 6.4 %shard_map.148 = (bf16[16,2,16,768]{3,2,1,0:T(8,128)(2,1)S(1)}, bf16[16,2,16,768]{3,2,1,0:T(8,128)(2,1)S(1)}) custom-call(s32[1]{0:T(128)} %bitcast.me_ref, bf16[16,2,16,768]{3,2,1,0:T(8,128)(2,1)S(1)} %bitcast.19, bf16[16,2,16,768]{3,2,1,0:T(8,128)(2,1)S(1)} %bitcast.20, bf16[16,256,64]{2,1,0:T(8,128)(2,1)S(1)} %get-tuple-element.19.refs_2_, ...), custom_call_target="tpu_custom_call" | custom-call | flops 9663676416 | tf_op jit(solution)/shard_map/pallas_call | solution.py:147
  60.3 2.7 %collective-permute-start.31 = (bf16[1,2,2,16,768]{4,3,2,1,0:T(8,128)(2,1)S(1)}, bf16[1,2,2,16,768]{4,3,2,1,0:T(8,128)(2,1)S(1)}, u32[]{:S(2)}, u32[]{:S(2)}) collective-permute-start(bf16[1,2,2,16,768]{4,3,2,1,0:T(8,128)(2,1)S(1)} %get-tuple-element.27), channel_id=1, source_target_pairs={{0,14},{1,15},{2,12},{3,13},{4,10},{5,11},{6,8},{7,9},{8,6},{9,7},... | collective-permute-start | bytes 294920 | tf_op jit(solution)/shard_map/ppermute | solution.py:241
  64.2 2.2 %collective-permute-start.27 = (bf16[1,2,2,16,768]{4,3,2,1,0:T(8,128)(2,1)S(1)}, bf16[1,2,2,16,768]{4,3,2,1,0:T(8,128)(2,1)S(1)}, u32[]{:S(2)}, u32[]{:S(2)}) collective-permute-start(bf16[1,2,2,16,768]{4,3,2,1,0:T(8,128)(2,1)S(1)} %get-tuple-element.31), channel_id=1, source_target_pairs={{0,6},{1,7},{2,4},{3,5},{4,2},{5,3},{6,0},{7,1},{8,14},{9,15},{10,... | collective-permute-start | bytes 294920 | tf_op jit(solution)/shard_map/ppermute | solution.py:241
  66.9 2.7 %collective-permute-done.25 = bf16[1,2,2,16,768]{4,3,2,1,0:T(8,128)(2,1)S(1)} collective-permute-done((bf16[1,2,2,16,768]{4,3,2,1,0:T(8,128)(2,1)S(1)}, bf16[1,2,2,16,768]{4,3,2,1,0:T(8,128)(2,1)S(1)}, u32[]{:S(2)}, u32[]{:S(2)}) %collective-permute-start.25) | collective-permute-done | bytes 98336 | tf_op jit(solution)/shard_map/ppermute | solution.py:241
  70.9 3.3 %collective-permute-start.30 = (bf16[1,2,2,16,768]{4,3,2,1,0:T(8,128)(2,1)S(1)}, bf16[1,2,2,16,768]{4,3,2,1,0:T(8,128)(2,1)S(1)}, u32[]{:S(2)}, u32[]{:S(2)}) collective-permute-start(bf16[1,2,2,16,768]{4,3,2,1,0:T(8,128)(2,1)S(1)} %get-tuple-element.34), channel_id=1, source_target_pairs={{0,12},{1,13},{2,14},{3,15},{4,8},{5,9},{6,10},{7,11},{8,4},{9,5},... | collective-permute-start | bytes 294920 | tf_op jit(solution)/shard_map/ppermute | solution.py:241
  74.3 3.1 %collective-permute-start.23 = (bf16[1,2,2,16,768]{4,3,2,1,0:T(8,128)(2,1)S(1)}, bf16[1,2,2,16,768]{4,3,2,1,0:T(8,128)(2,1)S(1)}, u32[]{:S(2)}, u32[]{:S(2)}) collective-permute-start(bf16[1,2,2,16,768]{4,3,2,1,0:T(8,128)(2,1)S(1)} %get-tuple-element.37), channel_id=1, source_target_pairs={{0,14},{1,15},{2,12},{3,13},{4,10},{5,11},{6,8},{7,9},{8,6},{9,7},... | collective-permute-start | bytes 294920 | tf_op jit(solution)/shard_map/ppermute | solution.py:241
  78.4 4.5 %collective-permute-done.29 = bf16[1,2,2,16,768]{4,3,2,1,0:T(8,128)(2,1)S(1)} collective-permute-done((bf16[1,2,2,16,768]{4,3,2,1,0:T(8,128)(2,1)S(1)}, bf16[1,2,2,16,768]{4,3,2,1,0:T(8,128)(2,1)S(1)}, u32[]{:S(2)}, u32[]{:S(2)}) %collective-permute-start.29) | collective-permute-done | bytes 98336 | tf_op jit(solution)/shard_map/ppermute | solution.py:241
  82.9 2.7 %collective-permute-start.19 = (bf16[1,2,2,16,768]{4,3,2,1,0:T(8,128)(2,1)S(1)}, bf16[1,2,2,16,768]{4,3,2,1,0:T(8,128)(2,1)S(1)}, u32[]{:S(2)}, u32[]{:S(2)}) collective-permute-start(bf16[1,2,2,16,768]{4,3,2,1,0:T(8,128)(2,1)S(1)} %get-tuple-element.41), channel_id=1, source_target_pairs={{0,6},{1,7},{2,4},{3,5},{4,2},{5,3},{6,0},{7,1},{8,14},{9,15},{10,... | collective-permute-start | bytes 294920 | tf_op jit(solution)/shard_map/ppermute | solution.py:241
  86.2 3.0 %collective-permute-start.21 = (bf16[1,2,2,16,768]{4,3,2,1,0:T(8,128)(2,1)S(1)}, bf16[1,2,2,16,768]{4,3,2,1,0:T(8,128)(2,1)S(1)}, u32[]{:S(2)}, u32[]{:S(2)}) collective-permute-start(bf16[1,2,2,16,768]{4,3,2,1,0:T(8,128)(2,1)S(1)} %get-tuple-element.43), channel_id=1, source_target_pairs={{0,10},{1,11},{2,8},{3,9},{4,14},{5,15},{6,12},{7,13},{8,2},{9,3},... | collective-permute-start | bytes 294920 | tf_op jit(solution)/shard_map/ppermute | solution.py:241
  89.2 2.0 %collective-permute-start.22 = (bf16[1,2,2,16,768]{4,3,2,1,0:T(8,128)(2,1)S(1)}, bf16[1,2,2,16,768]{4,3,2,1,0:T(8,128)(2,1)S(1)}, u32[]{:S(2)}, u32[]{:S(2)}) collective-permute-start(bf16[1,2,2,16,768]{4,3,2,1,0:T(8,128)(2,1)S(1)} %get-tuple-element.44), channel_id=1, source_target_pairs={{0,12},{1,13},{2,14},{3,15},{4,8},{5,9},{6,10},{7,11},{8,4},{9,5},... | collective-permute-start | bytes 294920 | tf_op jit(solution)/shard_map/ppermute | solution.py:241
  91.3 8.5 %shard_map.149.rest_0_ = bf16[4,1440,384]{2,1,0:T(8,128)(2,1)} custom-call(s32[1]{0:T(128)} %bitcast.me_ref, bf16[16,2,16,768]{3,2,1,0:T(8,128)(2,1)S(1)} %bitcast.18, bf16[2,1440,384]{2,1,0:T(8,128)(2,1)S(1)} %get-tuple-element.26.normed_ref, bf16[4,1440,384]{2,1,0:T(8,128)(2,1)S(1)} %bitcast.22, bf16[1440,512]{1,0:T(8,128)(2,1)S(1)} %copy-done.7, ...), custom_call_target="tpu_custom_call" | custom-call | flops 18119393280 | tf_op jit(solution)/shard_map/pallas_call | solution.py:220
  100.3 8.3 %shard_map.150 = bf16[4,1440,384]{2,1,0:T(8,128)(2,1)} custom-call(s32[1]{0:T(128)} %bitcast.me_ref, bf16[16,2,16,768]{3,2,1,0:T(8,128)(2,1)S(1)} %bitcast.17, bf16[2,1440,384]{2,1,0:T(8,128)(2,1)S(1)} %get-tuple-element.23.normed_ref, bf16[4,1440,384]{2,1,0:T(8,128)(2,1)S(1)} %bitcast.22, ...), custom_call_target="tpu_custom_call", output_to_operand_aliasing={{}: (9, {})} | custom-call | flops 18119393280 | tf_op jit(solution)/shard_map/pallas_call | solution.py:220
  (112 shorter events, 11.9 us)
Async XLA Ops:
  7.2 25.5 %collective-permute-start.7 = (bf16[1,2,2,16,768]{4,3,2,1,0:T(8,128)(2,1)S(1)}, bf16[1,2,2,16,768]{4,3,2,1,0:T(8,128)(2,1)S(1)}, u32[]{:S(2)}, u32[]{:S(2)}) collective-permute-start(bf16[1,2,2,16,768]{4,3,2,1,0:T(8,128)(2,1)S(1)} %get-tuple-element.57), channel_id=1, source_target_pairs={{0,14},{1,15},{2,12},{3,13},{4,10},{5,11},{6,8},{7,9},{8,6},{9,7},... | collective-permute-start | bytes 294920 | tf_op jit(solution)/shard_map/ppermute | solution.py:241
  13.2 8.0 %collective-permute-start.1 = (bf16[1,2,2,16,768]{4,3,2,1,0:T(8,128)(2,1)S(1)}, bf16[1,2,2,16,768]{4,3,2,1,0:T(8,128)(2,1)S(1)}, u32[]{:S(2)}, u32[]{:S(2)}) collective-permute-start(bf16[1,2,2,16,768]{4,3,2,1,0:T(8,128)(2,1)S(1)} %get-tuple-element.59), channel_id=1, source_target_pairs={{0,2},{1,3},{2,0},{3,1},{4,6},{5,7},{6,4},{7,5},{8,10},{9,11},{10,... | collective-permute-start | bytes 294920 | tf_op jit(solution)/shard_map/ppermute | solution.py:241
  13.7 10.4 %collective-permute-start.2 = (bf16[1,2,2,16,768]{4,3,2,1,0:T(8,128)(2,1)S(1)}, bf16[1,2,2,16,768]{4,3,2,1,0:T(8,128)(2,1)S(1)}, u32[]{:S(2)}, u32[]{:S(2)}) collective-permute-start(bf16[1,2,2,16,768]{4,3,2,1,0:T(8,128)(2,1)S(1)} %get-tuple-element.60), channel_id=1, source_target_pairs={{0,4},{1,5},{2,6},{3,7},{4,0},{5,1},{6,2},{7,3},{8,12},{9,13},{10,... | collective-permute-start | bytes 294920 | tf_op jit(solution)/shard_map/ppermute | solution.py:241
  13.7 10.6 %collective-permute-start.3 = (bf16[1,2,2,16,768]{4,3,2,1,0:T(8,128)(2,1)S(1)}, bf16[1,2,2,16,768]{4,3,2,1,0:T(8,128)(2,1)S(1)}, u32[]{:S(2)}, u32[]{:S(2)}) collective-permute-start(bf16[1,2,2,16,768]{4,3,2,1,0:T(8,128)(2,1)S(1)} %get-tuple-element.61), channel_id=1, source_target_pairs={{0,6},{1,7},{2,4},{3,5},{4,2},{5,3},{6,0},{7,1},{8,14},{9,15},{10,... | collective-permute-start | bytes 294920 | tf_op jit(solution)/shard_map/ppermute | solution.py:241
  16.7 7.8 %collective-permute-start.4 = (bf16[1,2,2,16,768]{4,3,2,1,0:T(8,128)(2,1)S(1)}, bf16[1,2,2,16,768]{4,3,2,1,0:T(8,128)(2,1)S(1)}, u32[]{:S(2)}, u32[]{:S(2)}) collective-permute-start(bf16[1,2,2,16,768]{4,3,2,1,0:T(8,128)(2,1)S(1)} %get-tuple-element.62), channel_id=1, source_target_pairs={{0,8},{1,9},{2,10},{3,11},{4,12},{5,13},{6,14},{7,15},{8,0},{9,1},... | collective-permute-start | bytes 294920 | tf_op jit(solution)/shard_map/ppermute | solution.py:241
  21.2 10.8 %collective-permute-start.5 = (bf16[1,2,2,16,768]{4,3,2,1,0:T(8,128)(2,1)S(1)}, bf16[1,2,2,16,768]{4,3,2,1,0:T(8,128)(2,1)S(1)}, u32[]{:S(2)}, u32[]{:S(2)}) collective-permute-start(bf16[1,2,2,16,768]{4,3,2,1,0:T(8,128)(2,1)S(1)} %get-tuple-element.63), channel_id=1, source_target_pairs={{0,10},{1,11},{2,8},{3,9},{4,14},{5,15},{6,12},{7,13},{8,2},{9,3},... | collective-permute-start | bytes 294920 | tf_op jit(solution)/shard_map/ppermute | solution.py:241
  24.2 7.8 %collective-permute-start.6 = (bf16[1,2,2,16,768]{4,3,2,1,0:T(8,128)(2,1)S(1)}, bf16[1,2,2,16,768]{4,3,2,1,0:T(8,128)(2,1)S(1)}, u32[]{:S(2)}, u32[]{:S(2)}) collective-permute-start(bf16[1,2,2,16,768]{4,3,2,1,0:T(8,128)(2,1)S(1)} %get-tuple-element.64), channel_id=1, source_target_pairs={{0,12},{1,13},{2,14},{3,15},{4,8},{5,9},{6,10},{7,11},{8,4},{9,5},... | collective-permute-start | bytes 294920 | tf_op jit(solution)/shard_map/ppermute | solution.py:241
  32.7 19.1 %collective-permute-start.15 = (bf16[1,2,2,16,768]{4,3,2,1,0:T(8,128)(2,1)S(1)}, bf16[1,2,2,16,768]{4,3,2,1,0:T(8,128)(2,1)S(1)}, u32[]{:S(2)}, u32[]{:S(2)}) collective-permute-start(bf16[1,2,2,16,768]{4,3,2,1,0:T(8,128)(2,1)S(1)} %get-tuple-element.47), channel_id=1, source_target_pairs={{0,14},{1,15},{2,12},{3,13},{4,10},{5,11},{6,8},{7,9},{8,6},{9,7},... | collective-permute-start | bytes 294920 | tf_op jit(solution)/shard_map/ppermute | solution.py:241
  38.3 11.1 %collective-permute-start.12 = (bf16[1,2,2,16,768]{4,3,2,1,0:T(8,128)(2,1)S(1)}, bf16[1,2,2,16,768]{4,3,2,1,0:T(8,128)(2,1)S(1)}, u32[]{:S(2)}, u32[]{:S(2)}) collective-permute-start(bf16[1,2,2,16,768]{4,3,2,1,0:T(8,128)(2,1)S(1)} %get-tuple-element.52), channel_id=1, source_target_pairs={{0,8},{1,9},{2,10},{3,11},{4,12},{5,13},{6,14},{7,15},{8,0},{9,1},... | collective-permute-start | bytes 294920 | tf_op jit(solution)/shard_map/ppermute | solution.py:241
  38.8 13.0 %collective-permute-start.13 = (bf16[1,2,2,16,768]{4,3,2,1,0:T(8,128)(2,1)S(1)}, bf16[1,2,2,16,768]{4,3,2,1,0:T(8,128)(2,1)S(1)}, u32[]{:S(2)}, u32[]{:S(2)}) collective-permute-start(bf16[1,2,2,16,768]{4,3,2,1,0:T(8,128)(2,1)S(1)} %get-tuple-element.53), channel_id=1, source_target_pairs={{0,10},{1,11},{2,8},{3,9},{4,14},{5,15},{6,12},{7,13},{8,2},{9,3},... | collective-permute-start | bytes 294920 | tf_op jit(solution)/shard_map/ppermute | solution.py:241
  42.1 9.7 %collective-permute-start.14 = (bf16[1,2,2,16,768]{4,3,2,1,0:T(8,128)(2,1)S(1)}, bf16[1,2,2,16,768]{4,3,2,1,0:T(8,128)(2,1)S(1)}, u32[]{:S(2)}, u32[]{:S(2)}) collective-permute-start(bf16[1,2,2,16,768]{4,3,2,1,0:T(8,128)(2,1)S(1)} %get-tuple-element.54), channel_id=1, source_target_pairs={{0,12},{1,13},{2,14},{3,15},{4,8},{5,9},{6,10},{7,11},{8,4},{9,5},... | collective-permute-start | bytes 294920 | tf_op jit(solution)/shard_map/ppermute | solution.py:241
  58.5 7.9 %collective-permute-start.16 = (bf16[8,1,2,16,768]{4,3,2,1,0:T(8,128)(2,1)S(1)}, bf16[8,1,2,16,768]{4,3,2,1,0:T(8,128)(2,1)S(1)}, u32[]{:S(2)}, u32[]{:S(2)}) collective-permute-start(bf16[8,1,2,16,768]{4,3,2,1,0:T(8,128)(2,1)S(1)} %get-tuple-element.46), channel_id=1, source_target_pairs={{0,1},{1,0},{2,3},{3,2},{4,5},{5,4},{6,7},{7,6},{8,9},{9,8},{10,11... | collective-permute-start | bytes 1179656 | tf_op jit(solution)/shard_map/ppermute | solution.py:241
  60.3 25.3 %collective-permute-start.31 = (bf16[1,2,2,16,768]{4,3,2,1,0:T(8,128)(2,1)S(1)}, bf16[1,2,2,16,768]{4,3,2,1,0:T(8,128)(2,1)S(1)}, u32[]{:S(2)}, u32[]{:S(2)}) collective-permute-start(bf16[1,2,2,16,768]{4,3,2,1,0:T(8,128)(2,1)S(1)} %get-tuple-element.27), channel_id=1, source_target_pairs={{0,14},{1,15},{2,12},{3,13},{4,10},{5,11},{6,8},{7,9},{8,6},{9,7},... | collective-permute-start | bytes 294920 | tf_op jit(solution)/shard_map/ppermute | solution.py:241
  64.2 10.0 %collective-permute-start.27 = (bf16[1,2,2,16,768]{4,3,2,1,0:T(8,128)(2,1)S(1)}, bf16[1,2,2,16,768]{4,3,2,1,0:T(8,128)(2,1)S(1)}, u32[]{:S(2)}, u32[]{:S(2)}) collective-permute-start(bf16[1,2,2,16,768]{4,3,2,1,0:T(8,128)(2,1)S(1)} %get-tuple-element.31), channel_id=1, source_target_pairs={{0,6},{1,7},{2,4},{3,5},{4,2},{5,3},{6,0},{7,1},{8,14},{9,15},{10,... | collective-permute-start | bytes 294920 | tf_op jit(solution)/shard_map/ppermute | solution.py:241
  66.4 11.9 %collective-permute-start.28 = (bf16[1,2,2,16,768]{4,3,2,1,0:T(8,128)(2,1)S(1)}, bf16[1,2,2,16,768]{4,3,2,1,0:T(8,128)(2,1)S(1)}, u32[]{:S(2)}, u32[]{:S(2)}) collective-permute-start(bf16[1,2,2,16,768]{4,3,2,1,0:T(8,128)(2,1)S(1)} %get-tuple-element.32), channel_id=1, source_target_pairs={{0,8},{1,9},{2,10},{3,11},{4,12},{5,13},{6,14},{7,15},{8,0},{9,1},... | collective-permute-start | bytes 294920 | tf_op jit(solution)/shard_map/ppermute | solution.py:241
  69.6 13.2 %collective-permute-start.29 = (bf16[1,2,2,16,768]{4,3,2,1,0:T(8,128)(2,1)S(1)}, bf16[1,2,2,16,768]{4,3,2,1,0:T(8,128)(2,1)S(1)}, u32[]{:S(2)}, u32[]{:S(2)}) collective-permute-start(bf16[1,2,2,16,768]{4,3,2,1,0:T(8,128)(2,1)S(1)} %get-tuple-element.33), channel_id=1, source_target_pairs={{0,10},{1,11},{2,8},{3,9},{4,14},{5,15},{6,12},{7,13},{8,2},{9,3},... | collective-permute-start | bytes 294920 | tf_op jit(solution)/shard_map/ppermute | solution.py:241
  70.9 11.9 %collective-permute-start.30 = (bf16[1,2,2,16,768]{4,3,2,1,0:T(8,128)(2,1)S(1)}, bf16[1,2,2,16,768]{4,3,2,1,0:T(8,128)(2,1)S(1)}, u32[]{:S(2)}, u32[]{:S(2)}) collective-permute-start(bf16[1,2,2,16,768]{4,3,2,1,0:T(8,128)(2,1)S(1)} %get-tuple-element.34), channel_id=1, source_target_pairs={{0,12},{1,13},{2,14},{3,15},{4,8},{5,9},{6,10},{7,11},{8,4},{9,5},... | collective-permute-start | bytes 294920 | tf_op jit(solution)/shard_map/ppermute | solution.py:241
  74.3 11.9 %collective-permute-start.23 = (bf16[1,2,2,16,768]{4,3,2,1,0:T(8,128)(2,1)S(1)}, bf16[1,2,2,16,768]{4,3,2,1,0:T(8,128)(2,1)S(1)}, u32[]{:S(2)}, u32[]{:S(2)}) collective-permute-start(bf16[1,2,2,16,768]{4,3,2,1,0:T(8,128)(2,1)S(1)} %get-tuple-element.37), channel_id=1, source_target_pairs={{0,14},{1,15},{2,12},{3,13},{4,10},{5,11},{6,8},{7,9},{8,6},{9,7},... | collective-permute-start | bytes 294920 | tf_op jit(solution)/shard_map/ppermute | solution.py:241
  78.3 10.9 %collective-permute-start.17 = (bf16[1,2,2,16,768]{4,3,2,1,0:T(8,128)(2,1)S(1)}, bf16[1,2,2,16,768]{4,3,2,1,0:T(8,128)(2,1)S(1)}, u32[]{:S(2)}, u32[]{:S(2)}) collective-permute-start(bf16[1,2,2,16,768]{4,3,2,1,0:T(8,128)(2,1)S(1)} %get-tuple-element.39), channel_id=1, source_target_pairs={{0,2},{1,3},{2,0},{3,1},{4,6},{5,7},{6,4},{7,5},{8,10},{9,11},{10,... | collective-permute-start | bytes 294920 | tf_op jit(solution)/shard_map/ppermute | solution.py:241
  82.8 16.9 %collective-permute-start.18 = (bf16[1,2,2,16,768]{4,3,2,1,0:T(8,128)(2,1)S(1)}, bf16[1,2,2,16,768]{4,3,2,1,0:T(8,128)(2,1)S(1)}, u32[]{:S(2)}, u32[]{:S(2)}) collective-permute-start(bf16[1,2,2,16,768]{4,3,2,1,0:T(8,128)(2,1)S(1)} %get-tuple-element.40), channel_id=1, source_target_pairs={{0,4},{1,5},{2,6},{3,7},{4,0},{5,1},{6,2},{7,3},{8,12},{9,13},{10,... | collective-permute-start | bytes 294920 | tf_op jit(solution)/shard_map/ppermute | solution.py:241
  82.9 16.9 %collective-permute-start.19 = (bf16[1,2,2,16,768]{4,3,2,1,0:T(8,128)(2,1)S(1)}, bf16[1,2,2,16,768]{4,3,2,1,0:T(8,128)(2,1)S(1)}, u32[]{:S(2)}, u32[]{:S(2)}) collective-permute-start(bf16[1,2,2,16,768]{4,3,2,1,0:T(8,128)(2,1)S(1)} %get-tuple-element.41), channel_id=1, source_target_pairs={{0,6},{1,7},{2,4},{3,5},{4,2},{5,3},{6,0},{7,1},{8,14},{9,15},{10,... | collective-permute-start | bytes 294920 | tf_op jit(solution)/shard_map/ppermute | solution.py:241
  85.6 14.2 %collective-permute-start.20 = (bf16[1,2,2,16,768]{4,3,2,1,0:T(8,128)(2,1)S(1)}, bf16[1,2,2,16,768]{4,3,2,1,0:T(8,128)(2,1)S(1)}, u32[]{:S(2)}, u32[]{:S(2)}) collective-permute-start(bf16[1,2,2,16,768]{4,3,2,1,0:T(8,128)(2,1)S(1)} %get-tuple-element.42), channel_id=1, source_target_pairs={{0,8},{1,9},{2,10},{3,11},{4,12},{5,13},{6,14},{7,15},{8,0},{9,1},... | collective-permute-start | bytes 294920 | tf_op jit(solution)/shard_map/ppermute | solution.py:241
  86.2 14.0 %collective-permute-start.21 = (bf16[1,2,2,16,768]{4,3,2,1,0:T(8,128)(2,1)S(1)}, bf16[1,2,2,16,768]{4,3,2,1,0:T(8,128)(2,1)S(1)}, u32[]{:S(2)}, u32[]{:S(2)}) collective-permute-start(bf16[1,2,2,16,768]{4,3,2,1,0:T(8,128)(2,1)S(1)} %get-tuple-element.43), channel_id=1, source_target_pairs={{0,10},{1,11},{2,8},{3,9},{4,14},{5,15},{6,12},{7,13},{8,2},{9,3},... | collective-permute-start | bytes 294920 | tf_op jit(solution)/shard_map/ppermute | solution.py:241
  89.2 11.0 %collective-permute-start.22 = (bf16[1,2,2,16,768]{4,3,2,1,0:T(8,128)(2,1)S(1)}, bf16[1,2,2,16,768]{4,3,2,1,0:T(8,128)(2,1)S(1)}, u32[]{:S(2)}, u32[]{:S(2)}) collective-permute-start(bf16[1,2,2,16,768]{4,3,2,1,0:T(8,128)(2,1)S(1)} %get-tuple-element.44), channel_id=1, source_target_pairs={{0,12},{1,13},{2,14},{3,15},{4,8},{5,9},{6,10},{7,11},{8,4},{9,5},... | collective-permute-start | bytes 294920 | tf_op jit(solution)/shard_map/ppermute | solution.py:241
  (21 other events, 308.7 us)

commit v4 on v3

--- a/solution.py
+++ b/solution.py
@@ -67,7 +67,7 @@
         in_specs=[
             pl.BlockSpec(memory_space=pltpu.SMEM),
             pl.BlockSpec((1, nlon, chan), lambda j: (j + first, 0, 0)),
-            pl.BlockSpec((1, chan), lambda j: (0, 0)),
+            pl.BlockSpec((chan,), lambda j: (0,)),
             pl.BlockSpec((modes2, nlon), lambda j: (0, 0)),
         ],
         out_specs=[
@@ -80,7 +80,7 @@
         ],
         compiler_params=pltpu.CompilerParams(vmem_limit_bytes=VMEM_LIMIT),
         cost_estimate=cost(2 * rows * modes2 * nlon * chan),
-    )(me, pltpu.with_memory_space_constraint(field, pltpu.HBM), gain.reshape(1, chan), pltpu.with_memory_space_constraint(table, pltpu.HBM))
+    )(me, pltpu.with_memory_space_constraint(field, pltpu.HBM), pltpu.with_memory_space_constraint(gain, pltpu.HBM), pltpu.with_memory_space_constraint(table, pltpu.HBM))
 
 
 def prepare_kernel(fwd_ref, inv_ref, mix_ref, order_ref, fwd_out, inv_out, weight_out):

time: 109 us -> 108 us (level)
  no operation moved by 1% of the time
where the time goes in v4:
time: 108 us
  starting transfers between devices  48 us (44%)
  Pallas kernels  32.8 us (30%)
  waiting for transfers between devices  26 us (24%)
    ppermute x32, starting transfers between devices, swap(): return lax.ppermute(part, 'lat', [(a, a ^ offset) for a in range(devices)])  48 us
    ppermute x32, waiting for transfers between devices, swap(): return lax.ppermute(part, 'lat', [(a, a ^ offset) for a in range(devices)])  26 us
    pallas_call x2, Pallas kernels, finish(): pl.pallas_call(finish_kernel, grid=(rows,), in_specs=specs, out_specs=pla...  16.8 us
    pallas_call x2, Pallas kernels, analyse(): pl.pallas_call(analyse_kernel, grid=(rows,), in_specs=[pl.BlockSpec(memor...  8.99 us
    pallas_call x1, Pallas kernels, middle(): pl.pallas_call(functools.partial(middle_kernel, chunks=len(arrived)), in_...  6.43 us
  transfers between devices with their start and end apart: 32, of which 11 were waited for; matrix products, arithmetic and copies ran while one was open for 0% of the time, Pallas kernels for 12%

profile of v4, /device:TPU:0, one launch (start us, length us, event | category | flops | bytes accessed | tf_op | source)
XLA Modules:
  0.0 107.9 jit_solution(12579818140320309786)
XLA Ops:
  0.0 4.6 %shard_map.145 = (bf16[16,2,16,768]{3,2,1,0:T(8,128)(2,1)S(1)}, bf16[2,1440,384]{2,1,0:T(8,128)(2,1)S(1)}) custom-call(s32[1]{0:T(128)} %bitcast.me_ref, bf16[4,1440,384]{2,1,0:T(8,128)(2,1)} %field_ref.7, f32[384]{0:T(512)} %gain_ref.3, bf16[512,1440]{1,0:T(8,128)(2,1)} %constant.12.clone.table_ref), custom_call_target="tpu_custom_call" | custom-call | flops 4529848320 | tf_op jit(solution)/shard_map/pallas_call | solution.py:64
  6.6 6.0 %collective-permute-start.7 = (bf16[1,2,2,16,768]{4,3,2,1,0:T(8,128)(2,1)S(1)}, bf16[1,2,2,16,768]{4,3,2,1,0:T(8,128)(2,1)S(1)}, u32[]{:S(2)}, u32[]{:S(2)}) collective-permute-start(bf16[1,2,2,16,768]{4,3,2,1,0:T(8,128)(2,1)S(1)} %get-tuple-element.57), channel_id=1, source_target_pairs={{0,14},{1,15},{2,12},{3,13},{4,10},{5,11},{6,8},{7,9},{8,6},{9,7},... | collective-permute-start | bytes 294920 | tf_op jit(solution)/shard_map/ppermute | solution.py:241
  13.1 3.0 %collective-permute-start.3 = (bf16[1,2,2,16,768]{4,3,2,1,0:T(8,128)(2,1)S(1)}, bf16[1,2,2,16,768]{4,3,2,1,0:T(8,128)(2,1)S(1)}, u32[]{:S(2)}, u32[]{:S(2)}) collective-permute-start(bf16[1,2,2,16,768]{4,3,2,1,0:T(8,128)(2,1)S(1)} %get-tuple-element.61), channel_id=1, source_target_pairs={{0,6},{1,7},{2,4},{3,5},{4,2},{5,3},{6,0},{7,1},{8,14},{9,15},{10,... | collective-permute-start | bytes 294920 | tf_op jit(solution)/shard_map/ppermute | solution.py:241
  16.0 4.4 %shard_map.146 = (bf16[16,2,16,768]{3,2,1,0:T(8,128)(2,1)S(1)}, bf16[2,1440,384]{2,1,0:T(8,128)(2,1)S(1)}) custom-call(s32[1]{0:T(128)} %bitcast.me_ref, bf16[4,1440,384]{2,1,0:T(8,128)(2,1)} %field_ref.7, f32[384]{0:T(512)} %gain_ref.3, bf16[512,1440]{1,0:T(8,128)(2,1)} %constant.12.clone.table_ref), custom_call_target="tpu_custom_call" | custom-call | flops 4529848320 | tf_op jit(solution)/shard_map/pallas_call | solution.py:64
  20.6 3.0 %collective-permute-start.5 = (bf16[1,2,2,16,768]{4,3,2,1,0:T(8,128)(2,1)S(1)}, bf16[1,2,2,16,768]{4,3,2,1,0:T(8,128)(2,1)S(1)}, u32[]{:S(2)}, u32[]{:S(2)}) collective-permute-start(bf16[1,2,2,16,768]{4,3,2,1,0:T(8,128)(2,1)S(1)} %get-tuple-element.63), channel_id=1, source_target_pairs={{0,10},{1,11},{2,8},{3,9},{4,14},{5,15},{6,12},{7,13},{8,2},{9,3},... | collective-permute-start | bytes 294920 | tf_op jit(solution)/shard_map/ppermute | solution.py:241
  23.9 7.5 %collective-permute-done.5 = bf16[1,2,2,16,768]{4,3,2,1,0:T(8,128)(2,1)S(1)} collective-permute-done((bf16[1,2,2,16,768]{4,3,2,1,0:T(8,128)(2,1)S(1)}, bf16[1,2,2,16,768]{4,3,2,1,0:T(8,128)(2,1)S(1)}, u32[]{:S(2)}, u32[]{:S(2)}) %collective-permute-start.5) | collective-permute-done | bytes 98336 | tf_op jit(solution)/shard_map/ppermute | solution.py:241
  32.1 3.5 %collective-permute-start.15 = (bf16[1,2,2,16,768]{4,3,2,1,0:T(8,128)(2,1)S(1)}, bf16[1,2,2,16,768]{4,3,2,1,0:T(8,128)(2,1)S(1)}, u32[]{:S(2)}, u32[]{:S(2)}) collective-permute-start(bf16[1,2,2,16,768]{4,3,2,1,0:T(8,128)(2,1)S(1)} %get-tuple-element.47), channel_id=1, source_target_pairs={{0,14},{1,15},{2,12},{3,13},{4,10},{5,11},{6,8},{7,9},{8,6},{9,7},... | collective-permute-start | bytes 294920 | tf_op jit(solution)/shard_map/ppermute | solution.py:241
  35.6 2.1 %collective-permute-start.11 = (bf16[1,2,2,16,768]{4,3,2,1,0:T(8,128)(2,1)S(1)}, bf16[1,2,2,16,768]{4,3,2,1,0:T(8,128)(2,1)S(1)}, u32[]{:S(2)}, u32[]{:S(2)}) collective-permute-start(bf16[1,2,2,16,768]{4,3,2,1,0:T(8,128)(2,1)S(1)} %get-tuple-element.51), channel_id=1, source_target_pairs={{0,6},{1,7},{2,4},{3,5},{4,2},{5,3},{6,0},{7,1},{8,14},{9,15},{10,... | collective-permute-start | bytes 294920 | tf_op jit(solution)/shard_map/ppermute | solution.py:241
  38.2 3.3 %collective-permute-start.13 = (bf16[1,2,2,16,768]{4,3,2,1,0:T(8,128)(2,1)S(1)}, bf16[1,2,2,16,768]{4,3,2,1,0:T(8,128)(2,1)S(1)}, u32[]{:S(2)}, u32[]{:S(2)}) collective-permute-start(bf16[1,2,2,16,768]{4,3,2,1,0:T(8,128)(2,1)S(1)} %get-tuple-element.53), channel_id=1, source_target_pairs={{0,10},{1,11},{2,8},{3,9},{4,14},{5,15},{6,12},{7,13},{8,2},{9,3},... | collective-permute-start | bytes 294920 | tf_op jit(solution)/shard_map/ppermute | solution.py:241
  41.5 1.4 %collective-permute-start.14 = (bf16[1,2,2,16,768]{4,3,2,1,0:T(8,128)(2,1)S(1)}, bf16[1,2,2,16,768]{4,3,2,1,0:T(8,128)(2,1)S(1)}, u32[]{:S(2)}, u32[]{:S(2)}) collective-permute-start(bf16[1,2,2,16,768]{4,3,2,1,0:T(8,128)(2,1)S(1)} %get-tuple-element.54), channel_id=1, source_target_pairs={{0,12},{1,13},{2,14},{3,15},{4,8},{5,9},{6,10},{7,11},{8,4},{9,5},... | collective-permute-start | bytes 294920 | tf_op jit(solution)/shard_map/ppermute | solution.py:241
  42.9 5.9 %collective-permute-done.12 = bf16[1,2,2,16,768]{4,3,2,1,0:T(8,128)(2,1)S(1)} collective-permute-done((bf16[1,2,2,16,768]{4,3,2,1,0:T(8,128)(2,1)S(1)}, bf16[1,2,2,16,768]{4,3,2,1,0:T(8,128)(2,1)S(1)}, u32[]{:S(2)}, u32[]{:S(2)}) %collective-permute-start.12) | collective-permute-done | bytes 98336 | tf_op jit(solution)/shard_map/ppermute | solution.py:241
  48.8 2.3 %collective-permute-done.13 = bf16[1,2,2,16,768]{4,3,2,1,0:T(8,128)(2,1)S(1)} collective-permute-done((bf16[1,2,2,16,768]{4,3,2,1,0:T(8,128)(2,1)S(1)}, bf16[1,2,2,16,768]{4,3,2,1,0:T(8,128)(2,1)S(1)}, u32[]{:S(2)}, u32[]{:S(2)}) %collective-permute-start.13) | collective-permute-done | bytes 98336 | tf_op jit(solution)/shard_map/ppermute | solution.py:241
  51.2 6.4 %shard_map.148 = (bf16[16,2,16,768]{3,2,1,0:T(8,128)(2,1)S(1)}, bf16[16,2,16,768]{3,2,1,0:T(8,128)(2,1)S(1)}) custom-call(s32[1]{0:T(128)} %bitcast.me_ref, bf16[16,2,16,768]{3,2,1,0:T(8,128)(2,1)S(1)} %bitcast.19, bf16[16,2,16,768]{3,2,1,0:T(8,128)(2,1)S(1)} %bitcast.20, bf16[16,256,64]{2,1,0:T(8,128)(2,1)S(1)} %get-tuple-element.19.refs_2_, ...), custom_call_target="tpu_custom_call" | custom-call | flops 9663676416 | tf_op jit(solution)/shard_map/pallas_call | solution.py:147
  59.6 2.7 %collective-permute-start.31 = (bf16[1,2,2,16,768]{4,3,2,1,0:T(8,128)(2,1)S(1)}, bf16[1,2,2,16,768]{4,3,2,1,0:T(8,128)(2,1)S(1)}, u32[]{:S(2)}, u32[]{:S(2)}) collective-permute-start(bf16[1,2,2,16,768]{4,3,2,1,0:T(8,128)(2,1)S(1)} %get-tuple-element.27), channel_id=1, source_target_pairs={{0,14},{1,15},{2,12},{3,13},{4,10},{5,11},{6,8},{7,9},{8,6},{9,7},... | collective-permute-start | bytes 294920 | tf_op jit(solution)/shard_map/ppermute | solution.py:241
  63.6 2.1 %collective-permute-start.27 = (bf16[1,2,2,16,768]{4,3,2,1,0:T(8,128)(2,1)S(1)}, bf16[1,2,2,16,768]{4,3,2,1,0:T(8,128)(2,1)S(1)}, u32[]{:S(2)}, u32[]{:S(2)}) collective-permute-start(bf16[1,2,2,16,768]{4,3,2,1,0:T(8,128)(2,1)S(1)} %get-tuple-element.31), channel_id=1, source_target_pairs={{0,6},{1,7},{2,4},{3,5},{4,2},{5,3},{6,0},{7,1},{8,14},{9,15},{10,... | collective-permute-start | bytes 294920 | tf_op jit(solution)/shard_map/ppermute | solution.py:241
  66.3 2.7 %collective-permute-done.25 = bf16[1,2,2,16,768]{4,3,2,1,0:T(8,128)(2,1)S(1)} collective-permute-done((bf16[1,2,2,16,768]{4,3,2,1,0:T(8,128)(2,1)S(1)}, bf16[1,2,2,16,768]{4,3,2,1,0:T(8,128)(2,1)S(1)}, u32[]{:S(2)}, u32[]{:S(2)}) %collective-permute-start.25) | collective-permute-done | bytes 98336 | tf_op jit(solution)/shard_map/ppermute | solution.py:241
  70.4 3.0 %collective-permute-start.30 = (bf16[1,2,2,16,768]{4,3,2,1,0:T(8,128)(2,1)S(1)}, bf16[1,2,2,16,768]{4,3,2,1,0:T(8,128)(2,1)S(1)}, u32[]{:S(2)}, u32[]{:S(2)}) collective-permute-start(bf16[1,2,2,16,768]{4,3,2,1,0:T(8,128)(2,1)S(1)} %get-tuple-element.34), channel_id=1, source_target_pairs={{0,12},{1,13},{2,14},{3,15},{4,8},{5,9},{6,10},{7,11},{8,4},{9,5},... | collective-permute-start | bytes 294920 | tf_op jit(solution)/shard_map/ppermute | solution.py:241
  73.6 3.1 %collective-permute-start.23 = (bf16[1,2,2,16,768]{4,3,2,1,0:T(8,128)(2,1)S(1)}, bf16[1,2,2,16,768]{4,3,2,1,0:T(8,128)(2,1)S(1)}, u32[]{:S(2)}, u32[]{:S(2)}) collective-permute-start(bf16[1,2,2,16,768]{4,3,2,1,0:T(8,128)(2,1)S(1)} %get-tuple-element.37), channel_id=1, source_target_pairs={{0,14},{1,15},{2,12},{3,13},{4,10},{5,11},{6,8},{7,9},{8,6},{9,7},... | collective-permute-start | bytes 294920 | tf_op jit(solution)/shard_map/ppermute | solution.py:241
  78.5 3.7 %collective-permute-done.29 = bf16[1,2,2,16,768]{4,3,2,1,0:T(8,128)(2,1)S(1)} collective-permute-done((bf16[1,2,2,16,768]{4,3,2,1,0:T(8,128)(2,1)S(1)}, bf16[1,2,2,16,768]{4,3,2,1,0:T(8,128)(2,1)S(1)}, u32[]{:S(2)}, u32[]{:S(2)}) %collective-permute-start.29) | collective-permute-done | bytes 98336 | tf_op jit(solution)/shard_map/ppermute | solution.py:241
  82.2 2.7 %collective-permute-start.19 = (bf16[1,2,2,16,768]{4,3,2,1,0:T(8,128)(2,1)S(1)}, bf16[1,2,2,16,768]{4,3,2,1,0:T(8,128)(2,1)S(1)}, u32[]{:S(2)}, u32[]{:S(2)}) collective-permute-start(bf16[1,2,2,16,768]{4,3,2,1,0:T(8,128)(2,1)S(1)} %get-tuple-element.41), channel_id=1, source_target_pairs={{0,6},{1,7},{2,4},{3,5},{4,2},{5,3},{6,0},{7,1},{8,14},{9,15},{10,... | collective-permute-start | bytes 294920 | tf_op jit(solution)/shard_map/ppermute | solution.py:241
  85.5 3.0 %collective-permute-start.21 = (bf16[1,2,2,16,768]{4,3,2,1,0:T(8,128)(2,1)S(1)}, bf16[1,2,2,16,768]{4,3,2,1,0:T(8,128)(2,1)S(1)}, u32[]{:S(2)}, u32[]{:S(2)}) collective-permute-start(bf16[1,2,2,16,768]{4,3,2,1,0:T(8,128)(2,1)S(1)} %get-tuple-element.43), channel_id=1, source_target_pairs={{0,10},{1,11},{2,8},{3,9},{4,14},{5,15},{6,12},{7,13},{8,2},{9,3},... | collective-permute-start | bytes 294920 | tf_op jit(solution)/shard_map/ppermute | solution.py:241
  88.6 2.0 %collective-permute-start.22 = (bf16[1,2,2,16,768]{4,3,2,1,0:T(8,128)(2,1)S(1)}, bf16[1,2,2,16,768]{4,3,2,1,0:T(8,128)(2,1)S(1)}, u32[]{:S(2)}, u32[]{:S(2)}) collective-permute-start(bf16[1,2,2,16,768]{4,3,2,1,0:T(8,128)(2,1)S(1)} %get-tuple-element.44), channel_id=1, source_target_pairs={{0,12},{1,13},{2,14},{3,15},{4,8},{5,9},{6,10},{7,11},{8,4},{9,5},... | collective-permute-start | bytes 294920 | tf_op jit(solution)/shard_map/ppermute | solution.py:241
  90.6 8.5 %shard_map.149.rest_0_ = bf16[4,1440,384]{2,1,0:T(8,128)(2,1)} custom-call(s32[1]{0:T(128)} %bitcast.me_ref, bf16[16,2,16,768]{3,2,1,0:T(8,128)(2,1)S(1)} %bitcast.18, bf16[2,1440,384]{2,1,0:T(8,128)(2,1)S(1)} %get-tuple-element.26.normed_ref, bf16[4,1440,384]{2,1,0:T(8,128)(2,1)S(1)} %bitcast.22, bf16[1440,512]{1,0:T(8,128)(2,1)S(1)} %copy-done.7, ...), custom_call_target="tpu_custom_call" | custom-call | flops 18119393280 | tf_op jit(solution)/shard_map/pallas_call | solution.py:220
  99.6 8.3 %shard_map.150 = bf16[4,1440,384]{2,1,0:T(8,128)(2,1)} custom-call(s32[1]{0:T(128)} %bitcast.me_ref, bf16[16,2,16,768]{3,2,1,0:T(8,128)(2,1)S(1)} %bitcast.17, bf16[2,1440,384]{2,1,0:T(8,128)(2,1)S(1)} %get-tuple-element.23.normed_ref, bf16[4,1440,384]{2,1,0:T(8,128)(2,1)S(1)} %bitcast.22, ...), custom_call_target="tpu_custom_call", output_to_operand_aliasing={{}: (9, {})} | custom-call | flops 18119393280 | tf_op jit(solution)/shard_map/pallas_call | solution.py:220
  (111 shorter events, 12.4 us)
Async XLA Ops:
  6.6 25.5 %collective-permute-start.7 = (bf16[1,2,2,16,768]{4,3,2,1,0:T(8,128)(2,1)S(1)}, bf16[1,2,2,16,768]{4,3,2,1,0:T(8,128)(2,1)S(1)}, u32[]{:S(2)}, u32[]{:S(2)}) collective-permute-start(bf16[1,2,2,16,768]{4,3,2,1,0:T(8,128)(2,1)S(1)} %get-tuple-element.57), channel_id=1, source_target_pairs={{0,14},{1,15},{2,12},{3,13},{4,10},{5,11},{6,8},{7,9},{8,6},{9,7},... | collective-permute-start | bytes 294920 | tf_op jit(solution)/shard_map/ppermute | solution.py:241
  12.5 8.0 %collective-permute-start.1 = (bf16[1,2,2,16,768]{4,3,2,1,0:T(8,128)(2,1)S(1)}, bf16[1,2,2,16,768]{4,3,2,1,0:T(8,128)(2,1)S(1)}, u32[]{:S(2)}, u32[]{:S(2)}) collective-permute-start(bf16[1,2,2,16,768]{4,3,2,1,0:T(8,128)(2,1)S(1)} %get-tuple-element.59), channel_id=1, source_target_pairs={{0,2},{1,3},{2,0},{3,1},{4,6},{5,7},{6,4},{7,5},{8,10},{9,11},{10,... | collective-permute-start | bytes 294920 | tf_op jit(solution)/shard_map/ppermute | solution.py:241
  13.1 10.5 %collective-permute-start.2 = (bf16[1,2,2,16,768]{4,3,2,1,0:T(8,128)(2,1)S(1)}, bf16[1,2,2,16,768]{4,3,2,1,0:T(8,128)(2,1)S(1)}, u32[]{:S(2)}, u32[]{:S(2)}) collective-permute-start(bf16[1,2,2,16,768]{4,3,2,1,0:T(8,128)(2,1)S(1)} %get-tuple-element.60), channel_id=1, source_target_pairs={{0,4},{1,5},{2,6},{3,7},{4,0},{5,1},{6,2},{7,3},{8,12},{9,13},{10,... | collective-permute-start | bytes 294920 | tf_op jit(solution)/shard_map/ppermute | solution.py:241
  13.1 10.7 %collective-permute-start.3 = (bf16[1,2,2,16,768]{4,3,2,1,0:T(8,128)(2,1)S(1)}, bf16[1,2,2,16,768]{4,3,2,1,0:T(8,128)(2,1)S(1)}, u32[]{:S(2)}, u32[]{:S(2)}) collective-permute-start(bf16[1,2,2,16,768]{4,3,2,1,0:T(8,128)(2,1)S(1)} %get-tuple-element.61), channel_id=1, source_target_pairs={{0,6},{1,7},{2,4},{3,5},{4,2},{5,3},{6,0},{7,1},{8,14},{9,15},{10,... | collective-permute-start | bytes 294920 | tf_op jit(solution)/shard_map/ppermute | solution.py:241
  16.0 7.8 %collective-permute-start.4 = (bf16[1,2,2,16,768]{4,3,2,1,0:T(8,128)(2,1)S(1)}, bf16[1,2,2,16,768]{4,3,2,1,0:T(8,128)(2,1)S(1)}, u32[]{:S(2)}, u32[]{:S(2)}) collective-permute-start(bf16[1,2,2,16,768]{4,3,2,1,0:T(8,128)(2,1)S(1)} %get-tuple-element.62), channel_id=1, source_target_pairs={{0,8},{1,9},{2,10},{3,11},{4,12},{5,13},{6,14},{7,15},{8,0},{9,1},... | collective-permute-start | bytes 294920 | tf_op jit(solution)/shard_map/ppermute | solution.py:241
  20.6 10.8 %collective-permute-start.5 = (bf16[1,2,2,16,768]{4,3,2,1,0:T(8,128)(2,1)S(1)}, bf16[1,2,2,16,768]{4,3,2,1,0:T(8,128)(2,1)S(1)}, u32[]{:S(2)}, u32[]{:S(2)}) collective-permute-start(bf16[1,2,2,16,768]{4,3,2,1,0:T(8,128)(2,1)S(1)} %get-tuple-element.63), channel_id=1, source_target_pairs={{0,10},{1,11},{2,8},{3,9},{4,14},{5,15},{6,12},{7,13},{8,2},{9,3},... | collective-permute-start | bytes 294920 | tf_op jit(solution)/shard_map/ppermute | solution.py:241
  23.5 7.8 %collective-permute-start.6 = (bf16[1,2,2,16,768]{4,3,2,1,0:T(8,128)(2,1)S(1)}, bf16[1,2,2,16,768]{4,3,2,1,0:T(8,128)(2,1)S(1)}, u32[]{:S(2)}, u32[]{:S(2)}) collective-permute-start(bf16[1,2,2,16,768]{4,3,2,1,0:T(8,128)(2,1)S(1)} %get-tuple-element.64), channel_id=1, source_target_pairs={{0,12},{1,13},{2,14},{3,15},{4,8},{5,9},{6,10},{7,11},{8,4},{9,5},... | collective-permute-start | bytes 294920 | tf_op jit(solution)/shard_map/ppermute | solution.py:241
  32.1 19.1 %collective-permute-start.15 = (bf16[1,2,2,16,768]{4,3,2,1,0:T(8,128)(2,1)S(1)}, bf16[1,2,2,16,768]{4,3,2,1,0:T(8,128)(2,1)S(1)}, u32[]{:S(2)}, u32[]{:S(2)}) collective-permute-start(bf16[1,2,2,16,768]{4,3,2,1,0:T(8,128)(2,1)S(1)} %get-tuple-element.47), channel_id=1, source_target_pairs={{0,14},{1,15},{2,12},{3,13},{4,10},{5,11},{6,8},{7,9},{8,6},{9,7},... | collective-permute-start | bytes 294920 | tf_op jit(solution)/shard_map/ppermute | solution.py:241
  37.7 11.2 %collective-permute-start.12 = (bf16[1,2,2,16,768]{4,3,2,1,0:T(8,128)(2,1)S(1)}, bf16[1,2,2,16,768]{4,3,2,1,0:T(8,128)(2,1)S(1)}, u32[]{:S(2)}, u32[]{:S(2)}) collective-permute-start(bf16[1,2,2,16,768]{4,3,2,1,0:T(8,128)(2,1)S(1)} %get-tuple-element.52), channel_id=1, source_target_pairs={{0,8},{1,9},{2,10},{3,11},{4,12},{5,13},{6,14},{7,15},{8,0},{9,1},... | collective-permute-start | bytes 294920 | tf_op jit(solution)/shard_map/ppermute | solution.py:241
  38.2 13.0 %collective-permute-start.13 = (bf16[1,2,2,16,768]{4,3,2,1,0:T(8,128)(2,1)S(1)}, bf16[1,2,2,16,768]{4,3,2,1,0:T(8,128)(2,1)S(1)}, u32[]{:S(2)}, u32[]{:S(2)}) collective-permute-start(bf16[1,2,2,16,768]{4,3,2,1,0:T(8,128)(2,1)S(1)} %get-tuple-element.53), channel_id=1, source_target_pairs={{0,10},{1,11},{2,8},{3,9},{4,14},{5,15},{6,12},{7,13},{8,2},{9,3},... | collective-permute-start | bytes 294920 | tf_op jit(solution)/shard_map/ppermute | solution.py:241
  41.5 9.7 %collective-permute-start.14 = (bf16[1,2,2,16,768]{4,3,2,1,0:T(8,128)(2,1)S(1)}, bf16[1,2,2,16,768]{4,3,2,1,0:T(8,128)(2,1)S(1)}, u32[]{:S(2)}, u32[]{:S(2)}) collective-permute-start(bf16[1,2,2,16,768]{4,3,2,1,0:T(8,128)(2,1)S(1)} %get-tuple-element.54), channel_id=1, source_target_pairs={{0,12},{1,13},{2,14},{3,15},{4,8},{5,9},{6,10},{7,11},{8,4},{9,5},... | collective-permute-start | bytes 294920 | tf_op jit(solution)/shard_map/ppermute | solution.py:241
  57.9 7.9 %collective-permute-start.16 = (bf16[8,1,2,16,768]{4,3,2,1,0:T(8,128)(2,1)S(1)}, bf16[8,1,2,16,768]{4,3,2,1,0:T(8,128)(2,1)S(1)}, u32[]{:S(2)}, u32[]{:S(2)}) collective-permute-start(bf16[8,1,2,16,768]{4,3,2,1,0:T(8,128)(2,1)S(1)} %get-tuple-element.46), channel_id=1, source_target_pairs={{0,1},{1,0},{2,3},{3,2},{4,5},{5,4},{6,7},{7,6},{8,9},{9,8},{10,11... | collective-permute-start | bytes 1179656 | tf_op jit(solution)/shard_map/ppermute | solution.py:241
  59.6 25.3 %collective-permute-start.31 = (bf16[1,2,2,16,768]{4,3,2,1,0:T(8,128)(2,1)S(1)}, bf16[1,2,2,16,768]{4,3,2,1,0:T(8,128)(2,1)S(1)}, u32[]{:S(2)}, u32[]{:S(2)}) collective-permute-start(bf16[1,2,2,16,768]{4,3,2,1,0:T(8,128)(2,1)S(1)} %get-tuple-element.27), channel_id=1, source_target_pairs={{0,14},{1,15},{2,12},{3,13},{4,10},{5,11},{6,8},{7,9},{8,6},{9,7},... | collective-permute-start | bytes 294920 | tf_op jit(solution)/shard_map/ppermute | solution.py:241
  63.6 9.9 %collective-permute-start.27 = (bf16[1,2,2,16,768]{4,3,2,1,0:T(8,128)(2,1)S(1)}, bf16[1,2,2,16,768]{4,3,2,1,0:T(8,128)(2,1)S(1)}, u32[]{:S(2)}, u32[]{:S(2)}) collective-permute-start(bf16[1,2,2,16,768]{4,3,2,1,0:T(8,128)(2,1)S(1)} %get-tuple-element.31), channel_id=1, source_target_pairs={{0,6},{1,7},{2,4},{3,5},{4,2},{5,3},{6,0},{7,1},{8,14},{9,15},{10,... | collective-permute-start | bytes 294920 | tf_op jit(solution)/shard_map/ppermute | solution.py:241
  65.8 11.9 %collective-permute-start.28 = (bf16[1,2,2,16,768]{4,3,2,1,0:T(8,128)(2,1)S(1)}, bf16[1,2,2,16,768]{4,3,2,1,0:T(8,128)(2,1)S(1)}, u32[]{:S(2)}, u32[]{:S(2)}) collective-permute-start(bf16[1,2,2,16,768]{4,3,2,1,0:T(8,128)(2,1)S(1)} %get-tuple-element.32), channel_id=1, source_target_pairs={{0,8},{1,9},{2,10},{3,11},{4,12},{5,13},{6,14},{7,15},{8,0},{9,1},... | collective-permute-start | bytes 294920 | tf_op jit(solution)/shard_map/ppermute | solution.py:241
  68.9 13.3 %collective-permute-start.29 = (bf16[1,2,2,16,768]{4,3,2,1,0:T(8,128)(2,1)S(1)}, bf16[1,2,2,16,768]{4,3,2,1,0:T(8,128)(2,1)S(1)}, u32[]{:S(2)}, u32[]{:S(2)}) collective-permute-start(bf16[1,2,2,16,768]{4,3,2,1,0:T(8,128)(2,1)S(1)} %get-tuple-element.33), channel_id=1, source_target_pairs={{0,10},{1,11},{2,8},{3,9},{4,14},{5,15},{6,12},{7,13},{8,2},{9,3},... | collective-permute-start | bytes 294920 | tf_op jit(solution)/shard_map/ppermute | solution.py:241
  70.4 11.8 %collective-permute-start.30 = (bf16[1,2,2,16,768]{4,3,2,1,0:T(8,128)(2,1)S(1)}, bf16[1,2,2,16,768]{4,3,2,1,0:T(8,128)(2,1)S(1)}, u32[]{:S(2)}, u32[]{:S(2)}) collective-permute-start(bf16[1,2,2,16,768]{4,3,2,1,0:T(8,128)(2,1)S(1)} %get-tuple-element.34), channel_id=1, source_target_pairs={{0,12},{1,13},{2,14},{3,15},{4,8},{5,9},{6,10},{7,11},{8,4},{9,5},... | collective-permute-start | bytes 294920 | tf_op jit(solution)/shard_map/ppermute | solution.py:241
  73.6 11.9 %collective-permute-start.23 = (bf16[1,2,2,16,768]{4,3,2,1,0:T(8,128)(2,1)S(1)}, bf16[1,2,2,16,768]{4,3,2,1,0:T(8,128)(2,1)S(1)}, u32[]{:S(2)}, u32[]{:S(2)}) collective-permute-start(bf16[1,2,2,16,768]{4,3,2,1,0:T(8,128)(2,1)S(1)} %get-tuple-element.37), channel_id=1, source_target_pairs={{0,14},{1,15},{2,12},{3,13},{4,10},{5,11},{6,8},{7,9},{8,6},{9,7},... | collective-permute-start | bytes 294920 | tf_op jit(solution)/shard_map/ppermute | solution.py:241
  77.7 10.9 %collective-permute-start.17 = (bf16[1,2,2,16,768]{4,3,2,1,0:T(8,128)(2,1)S(1)}, bf16[1,2,2,16,768]{4,3,2,1,0:T(8,128)(2,1)S(1)}, u32[]{:S(2)}, u32[]{:S(2)}) collective-permute-start(bf16[1,2,2,16,768]{4,3,2,1,0:T(8,128)(2,1)S(1)} %get-tuple-element.39), channel_id=1, source_target_pairs={{0,2},{1,3},{2,0},{3,1},{4,6},{5,7},{6,4},{7,5},{8,10},{9,11},{10,... | collective-permute-start | bytes 294920 | tf_op jit(solution)/shard_map/ppermute | solution.py:241
  82.2 16.9 %collective-permute-start.18 = (bf16[1,2,2,16,768]{4,3,2,1,0:T(8,128)(2,1)S(1)}, bf16[1,2,2,16,768]{4,3,2,1,0:T(8,128)(2,1)S(1)}, u32[]{:S(2)}, u32[]{:S(2)}) collective-permute-start(bf16[1,2,2,16,768]{4,3,2,1,0:T(8,128)(2,1)S(1)} %get-tuple-element.40), channel_id=1, source_target_pairs={{0,4},{1,5},{2,6},{3,7},{4,0},{5,1},{6,2},{7,3},{8,12},{9,13},{10,... | collective-permute-start | bytes 294920 | tf_op jit(solution)/shard_map/ppermute | solution.py:241
  82.2 16.9 %collective-permute-start.19 = (bf16[1,2,2,16,768]{4,3,2,1,0:T(8,128)(2,1)S(1)}, bf16[1,2,2,16,768]{4,3,2,1,0:T(8,128)(2,1)S(1)}, u32[]{:S(2)}, u32[]{:S(2)}) collective-permute-start(bf16[1,2,2,16,768]{4,3,2,1,0:T(8,128)(2,1)S(1)} %get-tuple-element.41), channel_id=1, source_target_pairs={{0,6},{1,7},{2,4},{3,5},{4,2},{5,3},{6,0},{7,1},{8,14},{9,15},{10,... | collective-permute-start | bytes 294920 | tf_op jit(solution)/shard_map/ppermute | solution.py:241
  84.9 14.2 %collective-permute-start.20 = (bf16[1,2,2,16,768]{4,3,2,1,0:T(8,128)(2,1)S(1)}, bf16[1,2,2,16,768]{4,3,2,1,0:T(8,128)(2,1)S(1)}, u32[]{:S(2)}, u32[]{:S(2)}) collective-permute-start(bf16[1,2,2,16,768]{4,3,2,1,0:T(8,128)(2,1)S(1)} %get-tuple-element.42), channel_id=1, source_target_pairs={{0,8},{1,9},{2,10},{3,11},{4,12},{5,13},{6,14},{7,15},{8,0},{9,1},... | collective-permute-start | bytes 294920 | tf_op jit(solution)/shard_map/ppermute | solution.py:241
  85.5 14.0 %collective-permute-start.21 = (bf16[1,2,2,16,768]{4,3,2,1,0:T(8,128)(2,1)S(1)}, bf16[1,2,2,16,768]{4,3,2,1,0:T(8,128)(2,1)S(1)}, u32[]{:S(2)}, u32[]{:S(2)}) collective-permute-start(bf16[1,2,2,16,768]{4,3,2,1,0:T(8,128)(2,1)S(1)} %get-tuple-element.43), channel_id=1, source_target_pairs={{0,10},{1,11},{2,8},{3,9},{4,14},{5,15},{6,12},{7,13},{8,2},{9,3},... | collective-permute-start | bytes 294920 | tf_op jit(solution)/shard_map/ppermute | solution.py:241
  88.6 11.0 %collective-permute-start.22 = (bf16[1,2,2,16,768]{4,3,2,1,0:T(8,128)(2,1)S(1)}, bf16[1,2,2,16,768]{4,3,2,1,0:T(8,128)(2,1)S(1)}, u32[]{:S(2)}, u32[]{:S(2)}) collective-permute-start(bf16[1,2,2,16,768]{4,3,2,1,0:T(8,128)(2,1)S(1)} %get-tuple-element.44), channel_id=1, source_target_pairs={{0,12},{1,13},{2,14},{3,15},{4,8},{5,9},{6,10},{7,11},{8,4},{9,5},... | collective-permute-start | bytes 294920 | tf_op jit(solution)/shard_map/ppermute | solution.py:241
  (21 other events, 308.6 us)

commit v5 on v4

--- a/solution.py
+++ b/solution.py
@@ -185,8 +185,8 @@
         stacked[modes + at : modes + at + modes_here] = synth_ref[slot, 0, :, chan:]
     inner = dot(table_ref[...], stacked[...]) + normed_ref[0].astype(F32)
     post = norm(inner, gain_ref[...]).astype(BF)
-    size = post.shape[0] // 2
-    for at in (0, size):
+    size = post.shape[0] // 3
+    for at in (0, size, 2 * size):
         here = slice(at, at + size)
         hidden = gelu((dot(post[here], up_ref[...]) + bias_ref[...]).astype(BF))
         out_ref[0, here] = (field_ref[0, here].astype(F32) + dot(hidden, down_ref[...])).astype(BF)

time: 108 us -> 108 us (level)
  no operation moved by 1% of the time
where the time goes in v5:
time: 108 us
  starting transfers between devices  48 us (44%)
  Pallas kernels  32.6 us (30%)
  waiting for transfers between devices  26 us (24%)
    ppermute x32, starting transfers between devices, swap(): return lax.ppermute(part, 'lat', [(a, a ^ offset) for a in range(devices)])  48 us
    ppermute x32, waiting for transfers between devices, swap(): return lax.ppermute(part, 'lat', [(a, a ^ offset) for a in range(devices)])  26 us
    pallas_call x2, Pallas kernels, finish(): pl.pallas_call(finish_kernel, grid=(rows,), in_specs=specs, out_specs=pla...  16.7 us
    pallas_call x2, Pallas kernels, analyse(): pl.pallas_call(analyse_kernel, grid=(rows,), in_specs=[pl.BlockSpec(memor...  8.99 us
    pallas_call x1, Pallas kernels, middle(): pl.pallas_call(functools.partial(middle_kernel, chunks=len(arrived)), in_...  6.43 us
  transfers between devices with their start and end apart: 32, of which 11 were waited for; matrix products, arithmetic and copies ran while one was open for 0% of the time, Pallas kernels for 12%

profile of v5, /device:TPU:0, one launch (start us, length us, event | category | flops | bytes accessed | tf_op | source)
XLA Modules:
  0.0 107.8 jit_solution(18158130252590768428)
XLA Ops:
  0.0 4.6 %shard_map.145 = (bf16[16,2,16,768]{3,2,1,0:T(8,128)(2,1)S(1)}, bf16[2,1440,384]{2,1,0:T(8,128)(2,1)S(1)}) custom-call(s32[1]{0:T(128)} %bitcast.me_ref, bf16[4,1440,384]{2,1,0:T(8,128)(2,1)} %field_ref.7, f32[384]{0:T(512)} %gain_ref.3, bf16[512,1440]{1,0:T(8,128)(2,1)} %constant.12.clone.table_ref), custom_call_target="tpu_custom_call" | custom-call | flops 4529848320 | tf_op jit(solution)/shard_map/pallas_call | solution.py:64
  6.6 6.0 %collective-permute-start.7 = (bf16[1,2,2,16,768]{4,3,2,1,0:T(8,128)(2,1)S(1)}, bf16[1,2,2,16,768]{4,3,2,1,0:T(8,128)(2,1)S(1)}, u32[]{:S(2)}, u32[]{:S(2)}) collective-permute-start(bf16[1,2,2,16,768]{4,3,2,1,0:T(8,128)(2,1)S(1)} %get-tuple-element.57), channel_id=1, source_target_pairs={{0,14},{1,15},{2,12},{3,13},{4,10},{5,11},{6,8},{7,9},{8,6},{9,7},... | collective-permute-start | bytes 294920 | tf_op jit(solution)/shard_map/ppermute | solution.py:241
  13.1 3.0 %collective-permute-start.3 = (bf16[1,2,2,16,768]{4,3,2,1,0:T(8,128)(2,1)S(1)}, bf16[1,2,2,16,768]{4,3,2,1,0:T(8,128)(2,1)S(1)}, u32[]{:S(2)}, u32[]{:S(2)}) collective-permute-start(bf16[1,2,2,16,768]{4,3,2,1,0:T(8,128)(2,1)S(1)} %get-tuple-element.61), channel_id=1, source_target_pairs={{0,6},{1,7},{2,4},{3,5},{4,2},{5,3},{6,0},{7,1},{8,14},{9,15},{10,... | collective-permute-start | bytes 294920 | tf_op jit(solution)/shard_map/ppermute | solution.py:241
  16.0 4.4 %shard_map.146 = (bf16[16,2,16,768]{3,2,1,0:T(8,128)(2,1)S(1)}, bf16[2,1440,384]{2,1,0:T(8,128)(2,1)S(1)}) custom-call(s32[1]{0:T(128)} %bitcast.me_ref, bf16[4,1440,384]{2,1,0:T(8,128)(2,1)} %field_ref.7, f32[384]{0:T(512)} %gain_ref.3, bf16[512,1440]{1,0:T(8,128)(2,1)} %constant.12.clone.table_ref), custom_call_target="tpu_custom_call" | custom-call | flops 4529848320 | tf_op jit(solution)/shard_map/pallas_call | solution.py:64
  20.6 3.0 %collective-permute-start.5 = (bf16[1,2,2,16,768]{4,3,2,1,0:T(8,128)(2,1)S(1)}, bf16[1,2,2,16,768]{4,3,2,1,0:T(8,128)(2,1)S(1)}, u32[]{:S(2)}, u32[]{:S(2)}) collective-permute-start(bf16[1,2,2,16,768]{4,3,2,1,0:T(8,128)(2,1)S(1)} %get-tuple-element.63), channel_id=1, source_target_pairs={{0,10},{1,11},{2,8},{3,9},{4,14},{5,15},{6,12},{7,13},{8,2},{9,3},... | collective-permute-start | bytes 294920 | tf_op jit(solution)/shard_map/ppermute | solution.py:241
  23.9 7.5 %collective-permute-done.5 = bf16[1,2,2,16,768]{4,3,2,1,0:T(8,128)(2,1)S(1)} collective-permute-done((bf16[1,2,2,16,768]{4,3,2,1,0:T(8,128)(2,1)S(1)}, bf16[1,2,2,16,768]{4,3,2,1,0:T(8,128)(2,1)S(1)}, u32[]{:S(2)}, u32[]{:S(2)}) %collective-permute-start.5) | collective-permute-done | bytes 98336 | tf_op jit(solution)/shard_map/ppermute | solution.py:241
  32.1 3.5 %collective-permute-start.15 = (bf16[1,2,2,16,768]{4,3,2,1,0:T(8,128)(2,1)S(1)}, bf16[1,2,2,16,768]{4,3,2,1,0:T(8,128)(2,1)S(1)}, u32[]{:S(2)}, u32[]{:S(2)}) collective-permute-start(bf16[1,2,2,16,768]{4,3,2,1,0:T(8,128)(2,1)S(1)} %get-tuple-element.47), channel_id=1, source_target_pairs={{0,14},{1,15},{2,12},{3,13},{4,10},{5,11},{6,8},{7,9},{8,6},{9,7},... | collective-permute-start | bytes 294920 | tf_op jit(solution)/shard_map/ppermute | solution.py:241
  35.6 2.1 %collective-permute-start.11 = (bf16[1,2,2,16,768]{4,3,2,1,0:T(8,128)(2,1)S(1)}, bf16[1,2,2,16,768]{4,3,2,1,0:T(8,128)(2,1)S(1)}, u32[]{:S(2)}, u32[]{:S(2)}) collective-permute-start(bf16[1,2,2,16,768]{4,3,2,1,0:T(8,128)(2,1)S(1)} %get-tuple-element.51), channel_id=1, source_target_pairs={{0,6},{1,7},{2,4},{3,5},{4,2},{5,3},{6,0},{7,1},{8,14},{9,15},{10,... | collective-permute-start | bytes 294920 | tf_op jit(solution)/shard_map/ppermute | solution.py:241
  38.2 3.3 %collective-permute-start.13 = (bf16[1,2,2,16,768]{4,3,2,1,0:T(8,128)(2,1)S(1)}, bf16[1,2,2,16,768]{4,3,2,1,0:T(8,128)(2,1)S(1)}, u32[]{:S(2)}, u32[]{:S(2)}) collective-permute-start(bf16[1,2,2,16,768]{4,3,2,1,0:T(8,128)(2,1)S(1)} %get-tuple-element.53), channel_id=1, source_target_pairs={{0,10},{1,11},{2,8},{3,9},{4,14},{5,15},{6,12},{7,13},{8,2},{9,3},... | collective-permute-start | bytes 294920 | tf_op jit(solution)/shard_map/ppermute | solution.py:241
  41.5 1.4 %collective-permute-start.14 = (bf16[1,2,2,16,768]{4,3,2,1,0:T(8,128)(2,1)S(1)}, bf16[1,2,2,16,768]{4,3,2,1,0:T(8,128)(2,1)S(1)}, u32[]{:S(2)}, u32[]{:S(2)}) collective-permute-start(bf16[1,2,2,16,768]{4,3,2,1,0:T(8,128)(2,1)S(1)} %get-tuple-element.54), channel_id=1, source_target_pairs={{0,12},{1,13},{2,14},{3,15},{4,8},{5,9},{6,10},{7,11},{8,4},{9,5},... | collective-permute-start | bytes 294920 | tf_op jit(solution)/shard_map/ppermute | solution.py:241
  42.9 5.9 %collective-permute-done.12 = bf16[1,2,2,16,768]{4,3,2,1,0:T(8,128)(2,1)S(1)} collective-permute-done((bf16[1,2,2,16,768]{4,3,2,1,0:T(8,128)(2,1)S(1)}, bf16[1,2,2,16,768]{4,3,2,1,0:T(8,128)(2,1)S(1)}, u32[]{:S(2)}, u32[]{:S(2)}) %collective-permute-start.12) | collective-permute-done | bytes 98336 | tf_op jit(solution)/shard_map/ppermute | solution.py:241
  48.8 2.3 %collective-permute-done.13 = bf16[1,2,2,16,768]{4,3,2,1,0:T(8,128)(2,1)S(1)} collective-permute-done((bf16[1,2,2,16,768]{4,3,2,1,0:T(8,128)(2,1)S(1)}, bf16[1,2,2,16,768]{4,3,2,1,0:T(8,128)(2,1)S(1)}, u32[]{:S(2)}, u32[]{:S(2)}) %collective-permute-start.13) | collective-permute-done | bytes 98336 | tf_op jit(solution)/shard_map/ppermute | solution.py:241
  51.2 6.4 %shard_map.148 = (bf16[16,2,16,768]{3,2,1,0:T(8,128)(2,1)S(1)}, bf16[16,2,16,768]{3,2,1,0:T(8,128)(2,1)S(1)}) custom-call(s32[1]{0:T(128)} %bitcast.me_ref, bf16[16,2,16,768]{3,2,1,0:T(8,128)(2,1)S(1)} %bitcast.19, bf16[16,2,16,768]{3,2,1,0:T(8,128)(2,1)S(1)} %bitcast.20, bf16[16,256,64]{2,1,0:T(8,128)(2,1)S(1)} %get-tuple-element.19.refs_2_, ...), custom_call_target="tpu_custom_call" | custom-call | flops 9663676416 | tf_op jit(solution)/shard_map/pallas_call | solution.py:147
  59.6 2.7 %collective-permute-start.31 = (bf16[1,2,2,16,768]{4,3,2,1,0:T(8,128)(2,1)S(1)}, bf16[1,2,2,16,768]{4,3,2,1,0:T(8,128)(2,1)S(1)}, u32[]{:S(2)}, u32[]{:S(2)}) collective-permute-start(bf16[1,2,2,16,768]{4,3,2,1,0:T(8,128)(2,1)S(1)} %get-tuple-element.27), channel_id=1, source_target_pairs={{0,14},{1,15},{2,12},{3,13},{4,10},{5,11},{6,8},{7,9},{8,6},{9,7},... | collective-permute-start | bytes 294920 | tf_op jit(solution)/shard_map/ppermute | solution.py:241
  63.6 2.1 %collective-permute-start.27 = (bf16[1,2,2,16,768]{4,3,2,1,0:T(8,128)(2,1)S(1)}, bf16[1,2,2,16,768]{4,3,2,1,0:T(8,128)(2,1)S(1)}, u32[]{:S(2)}, u32[]{:S(2)}) collective-permute-start(bf16[1,2,2,16,768]{4,3,2,1,0:T(8,128)(2,1)S(1)} %get-tuple-element.31), channel_id=1, source_target_pairs={{0,6},{1,7},{2,4},{3,5},{4,2},{5,3},{6,0},{7,1},{8,14},{9,15},{10,... | collective-permute-start | bytes 294920 | tf_op jit(solution)/shard_map/ppermute | solution.py:241
  66.3 2.7 %collective-permute-done.25 = bf16[1,2,2,16,768]{4,3,2,1,0:T(8,128)(2,1)S(1)} collective-permute-done((bf16[1,2,2,16,768]{4,3,2,1,0:T(8,128)(2,1)S(1)}, bf16[1,2,2,16,768]{4,3,2,1,0:T(8,128)(2,1)S(1)}, u32[]{:S(2)}, u32[]{:S(2)}) %collective-permute-start.25) | collective-permute-done | bytes 98336 | tf_op jit(solution)/shard_map/ppermute | solution.py:241
  70.4 3.0 %collective-permute-start.30 = (bf16[1,2,2,16,768]{4,3,2,1,0:T(8,128)(2,1)S(1)}, bf16[1,2,2,16,768]{4,3,2,1,0:T(8,128)(2,1)S(1)}, u32[]{:S(2)}, u32[]{:S(2)}) collective-permute-start(bf16[1,2,2,16,768]{4,3,2,1,0:T(8,128)(2,1)S(1)} %get-tuple-element.34), channel_id=1, source_target_pairs={{0,12},{1,13},{2,14},{3,15},{4,8},{5,9},{6,10},{7,11},{8,4},{9,5},... | collective-permute-start | bytes 294920 | tf_op jit(solution)/shard_map/ppermute | solution.py:241
  73.6 3.1 %collective-permute-start.23 = (bf16[1,2,2,16,768]{4,3,2,1,0:T(8,128)(2,1)S(1)}, bf16[1,2,2,16,768]{4,3,2,1,0:T(8,128)(2,1)S(1)}, u32[]{:S(2)}, u32[]{:S(2)}) collective-permute-start(bf16[1,2,2,16,768]{4,3,2,1,0:T(8,128)(2,1)S(1)} %get-tuple-element.37), channel_id=1, source_target_pairs={{0,14},{1,15},{2,12},{3,13},{4,10},{5,11},{6,8},{7,9},{8,6},{9,7},... | collective-permute-start | bytes 294920 | tf_op jit(solution)/shard_map/ppermute | solution.py:241
  78.5 3.7 %collective-permute-done.29 = bf16[1,2,2,16,768]{4,3,2,1,0:T(8,128)(2,1)S(1)} collective-permute-done((bf16[1,2,2,16,768]{4,3,2,1,0:T(8,128)(2,1)S(1)}, bf16[1,2,2,16,768]{4,3,2,1,0:T(8,128)(2,1)S(1)}, u32[]{:S(2)}, u32[]{:S(2)}) %collective-permute-start.29) | collective-permute-done | bytes 98336 | tf_op jit(solution)/shard_map/ppermute | solution.py:241
  82.2 2.7 %collective-permute-start.19 = (bf16[1,2,2,16,768]{4,3,2,1,0:T(8,128)(2,1)S(1)}, bf16[1,2,2,16,768]{4,3,2,1,0:T(8,128)(2,1)S(1)}, u32[]{:S(2)}, u32[]{:S(2)}) collective-permute-start(bf16[1,2,2,16,768]{4,3,2,1,0:T(8,128)(2,1)S(1)} %get-tuple-element.41), channel_id=1, source_target_pairs={{0,6},{1,7},{2,4},{3,5},{4,2},{5,3},{6,0},{7,1},{8,14},{9,15},{10,... | collective-permute-start | bytes 294920 | tf_op jit(solution)/shard_map/ppermute | solution.py:241
  85.5 3.0 %collective-permute-start.21 = (bf16[1,2,2,16,768]{4,3,2,1,0:T(8,128)(2,1)S(1)}, bf16[1,2,2,16,768]{4,3,2,1,0:T(8,128)(2,1)S(1)}, u32[]{:S(2)}, u32[]{:S(2)}) collective-permute-start(bf16[1,2,2,16,768]{4,3,2,1,0:T(8,128)(2,1)S(1)} %get-tuple-element.43), channel_id=1, source_target_pairs={{0,10},{1,11},{2,8},{3,9},{4,14},{5,15},{6,12},{7,13},{8,2},{9,3},... | collective-permute-start | bytes 294920 | tf_op jit(solution)/shard_map/ppermute | solution.py:241
  88.6 2.0 %collective-permute-start.22 = (bf16[1,2,2,16,768]{4,3,2,1,0:T(8,128)(2,1)S(1)}, bf16[1,2,2,16,768]{4,3,2,1,0:T(8,128)(2,1)S(1)}, u32[]{:S(2)}, u32[]{:S(2)}) collective-permute-start(bf16[1,2,2,16,768]{4,3,2,1,0:T(8,128)(2,1)S(1)} %get-tuple-element.44), channel_id=1, source_target_pairs={{0,12},{1,13},{2,14},{3,15},{4,8},{5,9},{6,10},{7,11},{8,4},{9,5},... | collective-permute-start | bytes 294920 | tf_op jit(solution)/shard_map/ppermute | solution.py:241
  90.6 8.4 %shard_map.149.rest_0_ = bf16[4,1440,384]{2,1,0:T(8,128)(2,1)} custom-call(s32[1]{0:T(128)} %bitcast.me_ref, bf16[16,2,16,768]{3,2,1,0:T(8,128)(2,1)S(1)} %bitcast.18, bf16[2,1440,384]{2,1,0:T(8,128)(2,1)S(1)} %get-tuple-element.26.normed_ref, bf16[4,1440,384]{2,1,0:T(8,128)(2,1)S(1)} %bitcast.22, bf16[1440,512]{1,0:T(8,128)(2,1)S(1)} %copy-done.7, ...), custom_call_target="tpu_custom_call" | custom-call | flops 18119393280 | tf_op jit(solution)/shard_map/pallas_call | solution.py:220
  99.6 8.2 %shard_map.150 = bf16[4,1440,384]{2,1,0:T(8,128)(2,1)} custom-call(s32[1]{0:T(128)} %bitcast.me_ref, bf16[16,2,16,768]{3,2,1,0:T(8,128)(2,1)S(1)} %bitcast.17, bf16[2,1440,384]{2,1,0:T(8,128)(2,1)S(1)} %get-tuple-element.23.normed_ref, bf16[4,1440,384]{2,1,0:T(8,128)(2,1)S(1)} %bitcast.22, ...), custom_call_target="tpu_custom_call", output_to_operand_aliasing={{}: (9, {})} | custom-call | flops 18119393280 | tf_op jit(solution)/shard_map/pallas_call | solution.py:220
  (111 shorter events, 12.5 us)
Async XLA Ops:
  6.6 25.5 %collective-permute-start.7 = (bf16[1,2,2,16,768]{4,3,2,1,0:T(8,128)(2,1)S(1)}, bf16[1,2,2,16,768]{4,3,2,1,0:T(8,128)(2,1)S(1)}, u32[]{:S(2)}, u32[]{:S(2)}) collective-permute-start(bf16[1,2,2,16,768]{4,3,2,1,0:T(8,128)(2,1)S(1)} %get-tuple-element.57), channel_id=1, source_target_pairs={{0,14},{1,15},{2,12},{3,13},{4,10},{5,11},{6,8},{7,9},{8,6},{9,7},... | collective-permute-start | bytes 294920 | tf_op jit(solution)/shard_map/ppermute | solution.py:241
  12.5 8.0 %collective-permute-start.1 = (bf16[1,2,2,16,768]{4,3,2,1,0:T(8,128)(2,1)S(1)}, bf16[1,2,2,16,768]{4,3,2,1,0:T(8,128)(2,1)S(1)}, u32[]{:S(2)}, u32[]{:S(2)}) collective-permute-start(bf16[1,2,2,16,768]{4,3,2,1,0:T(8,128)(2,1)S(1)} %get-tuple-element.59), channel_id=1, source_target_pairs={{0,2},{1,3},{2,0},{3,1},{4,6},{5,7},{6,4},{7,5},{8,10},{9,11},{10,... | collective-permute-start | bytes 294920 | tf_op jit(solution)/shard_map/ppermute | solution.py:241
  13.1 10.5 %collective-permute-start.2 = (bf16[1,2,2,16,768]{4,3,2,1,0:T(8,128)(2,1)S(1)}, bf16[1,2,2,16,768]{4,3,2,1,0:T(8,128)(2,1)S(1)}, u32[]{:S(2)}, u32[]{:S(2)}) collective-permute-start(bf16[1,2,2,16,768]{4,3,2,1,0:T(8,128)(2,1)S(1)} %get-tuple-element.60), channel_id=1, source_target_pairs={{0,4},{1,5},{2,6},{3,7},{4,0},{5,1},{6,2},{7,3},{8,12},{9,13},{10,... | collective-permute-start | bytes 294920 | tf_op jit(solution)/shard_map/ppermute | solution.py:241
  13.1 10.7 %collective-permute-start.3 = (bf16[1,2,2,16,768]{4,3,2,1,0:T(8,128)(2,1)S(1)}, bf16[1,2,2,16,768]{4,3,2,1,0:T(8,128)(2,1)S(1)}, u32[]{:S(2)}, u32[]{:S(2)}) collective-permute-start(bf16[1,2,2,16,768]{4,3,2,1,0:T(8,128)(2,1)S(1)} %get-tuple-element.61), channel_id=1, source_target_pairs={{0,6},{1,7},{2,4},{3,5},{4,2},{5,3},{6,0},{7,1},{8,14},{9,15},{10,... | collective-permute-start | bytes 294920 | tf_op jit(solution)/shard_map/ppermute | solution.py:241
  16.0 7.8 %collective-permute-start.4 = (bf16[1,2,2,16,768]{4,3,2,1,0:T(8,128)(2,1)S(1)}, bf16[1,2,2,16,768]{4,3,2,1,0:T(8,128)(2,1)S(1)}, u32[]{:S(2)}, u32[]{:S(2)}) collective-permute-start(bf16[1,2,2,16,768]{4,3,2,1,0:T(8,128)(2,1)S(1)} %get-tuple-element.62), channel_id=1, source_target_pairs={{0,8},{1,9},{2,10},{3,11},{4,12},{5,13},{6,14},{7,15},{8,0},{9,1},... | collective-permute-start | bytes 294920 | tf_op jit(solution)/shard_map/ppermute | solution.py:241
  20.6 10.8 %collective-permute-start.5 = (bf16[1,2,2,16,768]{4,3,2,1,0:T(8,128)(2,1)S(1)}, bf16[1,2,2,16,768]{4,3,2,1,0:T(8,128)(2,1)S(1)}, u32[]{:S(2)}, u32[]{:S(2)}) collective-permute-start(bf16[1,2,2,16,768]{4,3,2,1,0:T(8,128)(2,1)S(1)} %get-tuple-element.63), channel_id=1, source_target_pairs={{0,10},{1,11},{2,8},{3,9},{4,14},{5,15},{6,12},{7,13},{8,2},{9,3},... | collective-permute-start | bytes 294920 | tf_op jit(solution)/shard_map/ppermute | solution.py:241
  23.5 7.8 %collective-permute-start.6 = (bf16[1,2,2,16,768]{4,3,2,1,0:T(8,128)(2,1)S(1)}, bf16[1,2,2,16,768]{4,3,2,1,0:T(8,128)(2,1)S(1)}, u32[]{:S(2)}, u32[]{:S(2)}) collective-permute-start(bf16[1,2,2,16,768]{4,3,2,1,0:T(8,128)(2,1)S(1)} %get-tuple-element.64), channel_id=1, source_target_pairs={{0,12},{1,13},{2,14},{3,15},{4,8},{5,9},{6,10},{7,11},{8,4},{9,5},... | collective-permute-start | bytes 294920 | tf_op jit(solution)/shard_map/ppermute | solution.py:241
  32.1 19.1 %collective-permute-start.15 = (bf16[1,2,2,16,768]{4,3,2,1,0:T(8,128)(2,1)S(1)}, bf16[1,2,2,16,768]{4,3,2,1,0:T(8,128)(2,1)S(1)}, u32[]{:S(2)}, u32[]{:S(2)}) collective-permute-start(bf16[1,2,2,16,768]{4,3,2,1,0:T(8,128)(2,1)S(1)} %get-tuple-element.47), channel_id=1, source_target_pairs={{0,14},{1,15},{2,12},{3,13},{4,10},{5,11},{6,8},{7,9},{8,6},{9,7},... | collective-permute-start | bytes 294920 | tf_op jit(solution)/shard_map/ppermute | solution.py:241
  37.7 11.2 %collective-permute-start.12 = (bf16[1,2,2,16,768]{4,3,2,1,0:T(8,128)(2,1)S(1)}, bf16[1,2,2,16,768]{4,3,2,1,0:T(8,128)(2,1)S(1)}, u32[]{:S(2)}, u32[]{:S(2)}) collective-permute-start(bf16[1,2,2,16,768]{4,3,2,1,0:T(8,128)(2,1)S(1)} %get-tuple-element.52), channel_id=1, source_target_pairs={{0,8},{1,9},{2,10},{3,11},{4,12},{5,13},{6,14},{7,15},{8,0},{9,1},... | collective-permute-start | bytes 294920 | tf_op jit(solution)/shard_map/ppermute | solution.py:241
  38.2 13.0 %collective-permute-start.13 = (bf16[1,2,2,16,768]{4,3,2,1,0:T(8,128)(2,1)S(1)}, bf16[1,2,2,16,768]{4,3,2,1,0:T(8,128)(2,1)S(1)}, u32[]{:S(2)}, u32[]{:S(2)}) collective-permute-start(bf16[1,2,2,16,768]{4,3,2,1,0:T(8,128)(2,1)S(1)} %get-tuple-element.53), channel_id=1, source_target_pairs={{0,10},{1,11},{2,8},{3,9},{4,14},{5,15},{6,12},{7,13},{8,2},{9,3},... | collective-permute-start | bytes 294920 | tf_op jit(solution)/shard_map/ppermute | solution.py:241
  41.5 9.7 %collective-permute-start.14 = (bf16[1,2,2,16,768]{4,3,2,1,0:T(8,128)(2,1)S(1)}, bf16[1,2,2,16,768]{4,3,2,1,0:T(8,128)(2,1)S(1)}, u32[]{:S(2)}, u32[]{:S(2)}) collective-permute-start(bf16[1,2,2,16,768]{4,3,2,1,0:T(8,128)(2,1)S(1)} %get-tuple-element.54), channel_id=1, source_target_pairs={{0,12},{1,13},{2,14},{3,15},{4,8},{5,9},{6,10},{7,11},{8,4},{9,5},... | collective-permute-start | bytes 294920 | tf_op jit(solution)/shard_map/ppermute | solution.py:241
  57.9 7.9 %collective-permute-start.16 = (bf16[8,1,2,16,768]{4,3,2,1,0:T(8,128)(2,1)S(1)}, bf16[8,1,2,16,768]{4,3,2,1,0:T(8,128)(2,1)S(1)}, u32[]{:S(2)}, u32[]{:S(2)}) collective-permute-start(bf16[8,1,2,16,768]{4,3,2,1,0:T(8,128)(2,1)S(1)} %get-tuple-element.46), channel_id=1, source_target_pairs={{0,1},{1,0},{2,3},{3,2},{4,5},{5,4},{6,7},{7,6},{8,9},{9,8},{10,11... | collective-permute-start | bytes 1179656 | tf_op jit(solution)/shard_map/ppermute | solution.py:241
  59.6 25.3 %collective-permute-start.31 = (bf16[1,2,2,16,768]{4,3,2,1,0:T(8,128)(2,1)S(1)}, bf16[1,2,2,16,768]{4,3,2,1,0:T(8,128)(2,1)S(1)}, u32[]{:S(2)}, u32[]{:S(2)}) collective-permute-start(bf16[1,2,2,16,768]{4,3,2,1,0:T(8,128)(2,1)S(1)} %get-tuple-element.27), channel_id=1, source_target_pairs={{0,14},{1,15},{2,12},{3,13},{4,10},{5,11},{6,8},{7,9},{8,6},{9,7},... | collective-permute-start | bytes 294920 | tf_op jit(solution)/shard_map/ppermute | solution.py:241
  63.6 9.9 %collective-permute-start.27 = (bf16[1,2,2,16,768]{4,3,2,1,0:T(8,128)(2,1)S(1)}, bf16[1,2,2,16,768]{4,3,2,1,0:T(8,128)(2,1)S(1)}, u32[]{:S(2)}, u32[]{:S(2)}) collective-permute-start(bf16[1,2,2,16,768]{4,3,2,1,0:T(8,128)(2,1)S(1)} %get-tuple-element.31), channel_id=1, source_target_pairs={{0,6},{1,7},{2,4},{3,5},{4,2},{5,3},{6,0},{7,1},{8,14},{9,15},{10,... | collective-permute-start | bytes 294920 | tf_op jit(solution)/shard_map/ppermute | solution.py:241
  65.8 11.9 %collective-permute-start.28 = (bf16[1,2,2,16,768]{4,3,2,1,0:T(8,128)(2,1)S(1)}, bf16[1,2,2,16,768]{4,3,2,1,0:T(8,128)(2,1)S(1)}, u32[]{:S(2)}, u32[]{:S(2)}) collective-permute-start(bf16[1,2,2,16,768]{4,3,2,1,0:T(8,128)(2,1)S(1)} %get-tuple-element.32), channel_id=1, source_target_pairs={{0,8},{1,9},{2,10},{3,11},{4,12},{5,13},{6,14},{7,15},{8,0},{9,1},... | collective-permute-start | bytes 294920 | tf_op jit(solution)/shard_map/ppermute | solution.py:241
  68.9 13.3 %collective-permute-start.29 = (bf16[1,2,2,16,768]{4,3,2,1,0:T(8,128)(2,1)S(1)}, bf16[1,2,2,16,768]{4,3,2,1,0:T(8,128)(2,1)S(1)}, u32[]{:S(2)}, u32[]{:S(2)}) collective-permute-start(bf16[1,2,2,16,768]{4,3,2,1,0:T(8,128)(2,1)S(1)} %get-tuple-element.33), channel_id=1, source_target_pairs={{0,10},{1,11},{2,8},{3,9},{4,14},{5,15},{6,12},{7,13},{8,2},{9,3},... | collective-permute-start | bytes 294920 | tf_op jit(solution)/shard_map/ppermute | solution.py:241
  70.4 11.8 %collective-permute-start.30 = (bf16[1,2,2,16,768]{4,3,2,1,0:T(8,128)(2,1)S(1)}, bf16[1,2,2,16,768]{4,3,2,1,0:T(8,128)(2,1)S(1)}, u32[]{:S(2)}, u32[]{:S(2)}) collective-permute-start(bf16[1,2,2,16,768]{4,3,2,1,0:T(8,128)(2,1)S(1)} %get-tuple-element.34), channel_id=1, source_target_pairs={{0,12},{1,13},{2,14},{3,15},{4,8},{5,9},{6,10},{7,11},{8,4},{9,5},... | collective-permute-start | bytes 294920 | tf_op jit(solution)/shard_map/ppermute | solution.py:241
  73.6 11.9 %collective-permute-start.23 = (bf16[1,2,2,16,768]{4,3,2,1,0:T(8,128)(2,1)S(1)}, bf16[1,2,2,16,768]{4,3,2,1,0:T(8,128)(2,1)S(1)}, u32[]{:S(2)}, u32[]{:S(2)}) collective-permute-start(bf16[1,2,2,16,768]{4,3,2,1,0:T(8,128)(2,1)S(1)} %get-tuple-element.37), channel_id=1, source_target_pairs={{0,14},{1,15},{2,12},{3,13},{4,10},{5,11},{6,8},{7,9},{8,6},{9,7},... | collective-permute-start | bytes 294920 | tf_op jit(solution)/shard_map/ppermute | solution.py:241
  77.7 10.9 %collective-permute-start.17 = (bf16[1,2,2,16,768]{4,3,2,1,0:T(8,128)(2,1)S(1)}, bf16[1,2,2,16,768]{4,3,2,1,0:T(8,128)(2,1)S(1)}, u32[]{:S(2)}, u32[]{:S(2)}) collective-permute-start(bf16[1,2,2,16,768]{4,3,2,1,0:T(8,128)(2,1)S(1)} %get-tuple-element.39), channel_id=1, source_target_pairs={{0,2},{1,3},{2,0},{3,1},{4,6},{5,7},{6,4},{7,5},{8,10},{9,11},{10,... | collective-permute-start | bytes 294920 | tf_op jit(solution)/shard_map/ppermute | solution.py:241
  82.2 16.8 %collective-permute-start.18 = (bf16[1,2,2,16,768]{4,3,2,1,0:T(8,128)(2,1)S(1)}, bf16[1,2,2,16,768]{4,3,2,1,0:T(8,128)(2,1)S(1)}, u32[]{:S(2)}, u32[]{:S(2)}) collective-permute-start(bf16[1,2,2,16,768]{4,3,2,1,0:T(8,128)(2,1)S(1)} %get-tuple-element.40), channel_id=1, source_target_pairs={{0,4},{1,5},{2,6},{3,7},{4,0},{5,1},{6,2},{7,3},{8,12},{9,13},{10,... | collective-permute-start | bytes 294920 | tf_op jit(solution)/shard_map/ppermute | solution.py:241
  82.2 16.8 %collective-permute-start.19 = (bf16[1,2,2,16,768]{4,3,2,1,0:T(8,128)(2,1)S(1)}, bf16[1,2,2,16,768]{4,3,2,1,0:T(8,128)(2,1)S(1)}, u32[]{:S(2)}, u32[]{:S(2)}) collective-permute-start(bf16[1,2,2,16,768]{4,3,2,1,0:T(8,128)(2,1)S(1)} %get-tuple-element.41), channel_id=1, source_target_pairs={{0,6},{1,7},{2,4},{3,5},{4,2},{5,3},{6,0},{7,1},{8,14},{9,15},{10,... | collective-permute-start | bytes 294920 | tf_op jit(solution)/shard_map/ppermute | solution.py:241
  84.9 14.1 %collective-permute-start.20 = (bf16[1,2,2,16,768]{4,3,2,1,0:T(8,128)(2,1)S(1)}, bf16[1,2,2,16,768]{4,3,2,1,0:T(8,128)(2,1)S(1)}, u32[]{:S(2)}, u32[]{:S(2)}) collective-permute-start(bf16[1,2,2,16,768]{4,3,2,1,0:T(8,128)(2,1)S(1)} %get-tuple-element.42), channel_id=1, source_target_pairs={{0,8},{1,9},{2,10},{3,11},{4,12},{5,13},{6,14},{7,15},{8,0},{9,1},... | collective-permute-start | bytes 294920 | tf_op jit(solution)/shard_map/ppermute | solution.py:241
  85.5 14.0 %collective-permute-start.21 = (bf16[1,2,2,16,768]{4,3,2,1,0:T(8,128)(2,1)S(1)}, bf16[1,2,2,16,768]{4,3,2,1,0:T(8,128)(2,1)S(1)}, u32[]{:S(2)}, u32[]{:S(2)}) collective-permute-start(bf16[1,2,2,16,768]{4,3,2,1,0:T(8,128)(2,1)S(1)} %get-tuple-element.43), channel_id=1, source_target_pairs={{0,10},{1,11},{2,8},{3,9},{4,14},{5,15},{6,12},{7,13},{8,2},{9,3},... | collective-permute-start | bytes 294920 | tf_op jit(solution)/shard_map/ppermute | solution.py:241
  88.6 11.0 %collective-permute-start.22 = (bf16[1,2,2,16,768]{4,3,2,1,0:T(8,128)(2,1)S(1)}, bf16[1,2,2,16,768]{4,3,2,1,0:T(8,128)(2,1)S(1)}, u32[]{:S(2)}, u32[]{:S(2)}) collective-permute-start(bf16[1,2,2,16,768]{4,3,2,1,0:T(8,128)(2,1)S(1)} %get-tuple-element.44), channel_id=1, source_target_pairs={{0,12},{1,13},{2,14},{3,15},{4,8},{5,9},{6,10},{7,11},{8,4},{9,5},... | collective-permute-start | bytes 294920 | tf_op jit(solution)/shard_map/ppermute | solution.py:241
  (21 other events, 308.6 us)
